TPU v7x, 256 devices: a whole 4x4x8 slice. The times are simulated.
256 devices in a mesh: blk: 32 (over z, y_hi, core), grp: 8 (over y_lo, x).
Axes of the slice: x: 4, y: 4 (y_hi: 2, y_lo: 2; y = y_hi * 2 + y_lo), z: 8, core: 2. Of those that a mesh axis runs over, the one named last changes fastest.
Arguments:
- coeffs: bfloat16 [4096, 360, 128], P('blk', 'grp'), may hold values from -6 to 6
- vectors: float32 [4096, 16], P(('blk', 'grp')), may hold values from -6 to 6
Outputs:
- next_vectors: float32 [4096, 16], P(('blk', 'grp'))
All inputs are finite; a program needn't handle non-finite values.
Results may differ from a plain program's by a relative error of at most 0.0015.
The roundings to bfloat16 on the way count: a program that leaves them out, or rounds other values in their place, can miss the bound.
Values may be sent and summed in bfloat16 or wider, within the bound.
No kernel may reach another device: no remote copies, remote signals or barrier semaphores. Data moves between devices by JAX's collectives and lax.ppermute only.
A program may use at most 64 MiB of HBM per device.

v0:
```python
import math

import jax
import jax.numpy as jnp
from jax import lax
from jax.sharding import PartitionSpec as P

sharpness = 2.5
epsilon = 1e-06


def passed_along(block, axis, distance):
    devices = range(lax.axis_size(axis))
    route = [((i - distance) % len(devices), i) for i in devices]
    return lax.ppermute(block, axis, route)


def trig_rows(freq_local, group_size):
    total = freq_local * group_size
    row_ids = jnp.arange(2 * total, dtype=jnp.int32)
    within = row_ids % (2 * freq_local)
    freq = row_ids // (2 * freq_local) * freq_local + within % freq_local
    angles = jnp.arange(total, dtype=jnp.int32)
    phase = (freq[:, None] * angles[None, :] % total).astype(jnp.float32) * (2.0 * math.pi / total)
    cos_part = jnp.cos(phase).astype(jnp.bfloat16)
    sin_part = (-jnp.sin(phase)).astype(jnp.bfloat16)
    return jnp.where((within >= freq_local)[:, None], sin_part, cos_part)


def per_device(coeffs, vectors):
    block, freq_local, channels = coeffs.shape
    half_width = channels // 2
    group_size = lax.axis_size("grp")
    group_index = lax.axis_index("grp")
    own_rows = vectors.shape[0]
    angles = freq_local * group_size
    squares = jnp.einsum("ikc,ikc->i", coeffs, coeffs, preferred_element_type=jnp.float32)
    total_sq = lax.psum(squares, "grp")
    inv_norm = lax.rsqrt(total_sq / (angles * channels) + epsilon)
    unit_coef = (coeffs.astype(jnp.float32) * inv_norm[:, None, None]).astype(jnp.bfloat16)
    before_blk = passed_along(unit_coef, "blk", 1)
    after_blk = passed_along(unit_coef, "blk", -1)
    columns = jnp.concatenate([unit_coef, before_blk, after_blk], axis=0)
    swapped = jnp.concatenate([-columns[..., half_width:], columns[..., :half_width]], axis=-1)
    real_part = jnp.einsum("ikc,jkc->kij", unit_coef, columns, preferred_element_type=jnp.float32)
    imag_part = jnp.einsum("ikc,jkc->kij", unit_coef, swapped, preferred_element_type=jnp.float32)
    pair_terms = jnp.concatenate([real_part, imag_part], axis=0).astype(jnp.bfloat16)
    trig_table = trig_rows(freq_local, group_size)
    factor = sharpness / math.sqrt(angles * channels)
    corr = jnp.einsum(
        "frj,fm->rjm",
        lax.all_to_all(pair_terms, "grp", split_axis=1, concat_axis=0, tiled=True),
        trig_table,
        preferred_element_type=jnp.float32,
    )
    weights = jnp.mean(jnp.exp(factor * corr), axis=-1)
    col_ids = jnp.arange(weights.shape[1], dtype=jnp.int32)
    own_ids = group_index * own_rows + jnp.arange(own_rows, dtype=jnp.int32)
    weights = jnp.where(col_ids[None, :] == own_ids[:, None], jnp.zeros_like(weights), weights)
    row_degree = jnp.sum(weights, axis=-1)
    local_degree = jnp.sum(row_degree)
    degree_sum = lax.psum(local_degree, ("blk", "grp"))
    inv_root = lax.rsqrt(row_degree)
    scaled = vectors * inv_root[:, None]
    block_vec = lax.all_gather(scaled, "grp", axis=0, tiled=True)
    prev_vec = passed_along(block_vec, "blk", 1)
    next_vec = passed_along(block_vec, "blk", -1)
    neigh = jnp.concatenate([block_vec, prev_vec, next_vec], axis=0)
    product = jnp.dot(weights, neigh, precision=lax.Precision.HIGHEST)
    image = product * inv_root[:, None] * (3.0 * block)
    root_degree = jnp.sqrt(row_degree)
    local_proj = jnp.dot(root_degree, image, precision=lax.Precision.HIGHEST)
    projection = lax.psum(local_proj, ("blk", "grp"))
    deflated = image - root_degree[:, None] * (projection / degree_sum)[None, :]
    column_sq = lax.psum(jnp.sum(deflated * deflated, axis=0), ("blk", "grp"))
    total_rows = own_rows * group_size * lax.axis_size("blk")
    return deflated * lax.rsqrt(column_sq / total_rows + epsilon)[None, :]


def solution(mesh):
    placed = (P("blk", "grp", None), P(("blk", "grp"), None))
    return jax.shard_map(
        per_device, mesh=mesh, in_specs=placed, out_specs=P(("blk", "grp"), None), check_vma=False
    )
```

profile of v0, /device:TPU:1, one launch (start us, length us, event | category | flops | bytes accessed | tf_op | source)
XLA Modules:
  0.0 412.6 jit_solution(10428899602804066392)
XLA Ops:
  0.0 1.8 fusion.8
  1.8 16.8 %psum.28 = f32[128]{0:T(128)S(1)} all-reduce(f32[128]{0:T(128)S(1)} %fusion.8), channel_id=1, replica_groups=mesh['blk'=32,'grp'=8] {'grp'}, use_global_device_ids=true, to_apply=%region_0.0 | all-reduce | flops 128 | bytes 1024 | tf_op jit(solution)/shard_map/psum | solution.py:38
  18.5 1.9 multiply_convert_fusion
  20.4 7.0 %collective-permute-start = (bf16[128,45,128]{2,0,1:T(8,128)(2,1)S(1)}, bf16[128,45,128]{2,0,1:T(8,128)(2,1)S(1)}, u32[]{:S(2)}, u32[]{:S(2)}) collective-permute-start(bf16[128,45,128]{2,0,1:T(8,128)(2,1)S(1)} %multiply_convert_fusion), channel_id=1, source_target_pairs={{248,0},{0,8},{8,16},{16,24},{24,32},{32,40},{40,48},{48,56},{56,6... | collective-permute-start | bytes 4423688 | tf_op jit(solution)/shard_map/ppermute | solution.py:15
  27.5 0.0 collective-permute-start.1
  27.5 32.1 %collective-permute-done = bf16[128,45,128]{2,0,1:T(8,128)(2,1)S(1)} collective-permute-done((bf16[128,45,128]{2,0,1:T(8,128)(2,1)S(1)}, bf16[128,45,128]{2,0,1:T(8,128)(2,1)S(1)}, u32[]{:S(2)}, u32[]{:S(2)}) %collective-permute-start) | collective-permute-done | bytes 1474592 | tf_op jit(solution)/shard_map/ppermute | solution.py:15
  59.6 2.9 collective-permute-done.1
  62.5 0.0 copy-start
  62.5 1.1 copy-done
  63.6 0.7 pad_maximum_fusion.1
  64.3 3.2 slice_negate_fusion
  67.5 0.0 copy-start.1
  67.5 7.4 %fusion.9 = bf16[45,128,384]{2,1,0:T(8,128)(2,1)} fusion(bf16[128,45,128]{2,0,1:T(8,128)(2,1)S(1)} %multiply_convert_fusion, bf16[384,45,64]{2,0,1:T(8,128)(2,1)} %get-tuple-element.10, bf16[384,45,64]{2,0,1:T(8,128)(2,1)S(1)} %get-tuple-element.9), kind=kOutput, calls=%fused_computation.13 | convolution fusion | flops 577290240 | bytes 10321920 | tf_op jit(solution)/shard_map/ikc,jkc->kij/dot_general | solution.py:46
  74.9 0.0 copy-done.1
  74.9 3.8 convolution_convert_fusion
  78.7 8.0 %pad_maximum_fusion = bf16[90,128,384]{2,1,0:T(8,128)(2,1)} fusion(bf16[45,128,384]{2,1,0:T(8,128)(2,1)} %fusion.9, bf16[45,128,384]{2,1,0:T(8,128)(2,1)} %convolution_convert_fusion), kind=kLoop, calls=%fused_computation | loop fusion | flops 4423680 | bytes 17694720 | tf_op jit(solution)/shard_map/concatenate | solution.py:47
  86.7 12.5 %copy.18 = bf16[90,128,384]{2,0,1:T(8,128)(2,1)} copy(bf16[90,128,384]{2,1,0:T(8,128)(2,1)} %pad_maximum_fusion) | data formatting | bytes 17694720 | tf_op jit(solution)/shard_map/concatenate | solution.py:47
  99.2 5.3 %all-to-all-start = ((bf16[90,128,384]{2,0,1:T(8,128)(2,1)}), bf16[90,128,384]{2,0,1:T(8,128)(2,1)}, u32[]{:S(2)}, u32[]{:S(2)}) async-start(bf16[90,128,384]{2,0,1:T(8,128)(2,1)} %copy.18), calls=%async_computation | async-start | bytes 18874368 | tf_op jit(solution)/shard_map/all_to_all | solution.py:52
  104.5 91.0 %all-to-all-done = bf16[90,128,384]{2,0,1:T(8,128)(2,1)} async-done(((bf16[90,128,384]{2,0,1:T(8,128)(2,1)}), bf16[90,128,384]{2,0,1:T(8,128)(2,1)}, u32[]{:S(2)}, u32[]{:S(2)}) %all-to-all-start) | async-done | bytes 8847392 | tf_op jit(solution)/shard_map/all_to_all | solution.py:52
  195.6 10.7 %copy.20 = bf16[8,90,16,384]{3,2,1,0:T(8,128)(2,1)} copy(bf16[8,90,16,384]{3,1,2,0:T(8,128)(2,1)} %bitcast.4) | data formatting | bytes 17694720 | tf_op jit(solution)/shard_map/all_to_all | solution.py:52
  206.2 0.0 copy-start.2
  206.2 12.9 %exponential_reduce_fusion = f32[16,384]{1,0:T(8,128)S(1)} fusion(bf16[720,16,384]{2,1,0:T(8,128)(2,1)} %bitcast.18, s32[720]{0:T(1024)S(1)} %fusion.39, pred[720]{0:T(1024)(128)(4,1)S(1)} %fusion.44), kind=kOutput, calls=%fused_computation.3 | convolution fusion | flops 3192836608 | bytes 8875536 | tf_op jit(solution)/shard_map/frj,fm->rjm/dot_general | solution.py:50
  219.1 0.7 fusion.32
  219.8 0.0 copy-done.2
  219.8 0.1 broadcast_multiply_fusion
  219.9 21.8 %all_gather.3 = f32[128,16]{1,0:T(8,128)S(1)} all-gather(f32[16,16]{1,0:T(8,128)S(1)} %broadcast_multiply_fusion), channel_id=1, replica_groups=mesh['blk'=32,'grp'=8] {'grp'}, dimensions={0}, use_global_device_ids=true | all-gather | bytes 9216 | tf_op jit(solution)/shard_map/all_gather | solution.py:65
  241.7 9.5 %collective-permute-start.2 = (f32[128,16]{1,0:T(8,128)S(1)}, f32[128,16]{1,0:T(8,128)S(1)}, u32[]{:S(2)}, u32[]{:S(2)}) collective-permute-start(f32[128,16]{1,0:T(8,128)S(1)} %all_gather.3), channel_id=1, source_target_pairs={{248,0},{0,8},{8,16},{16,24},{24,32},{32,40},{40,48},{48,56},{56,6... | collective-permute-start | bytes 24584 | tf_op jit(solution)/shard_map/ppermute | solution.py:15
  251.1 0.0 collective-permute-start.3
  251.2 1.3 collective-permute-done.2
  252.5 3.8 collective-permute-done.3
  256.4 0.2 fusion.12
  256.6 0.1 convolution_bitcast_fusion
  256.8 81.0 %all-reduce = (f32[16]{0:T(128)S(1)}, f32[]{:T(128)}) all-reduce(f32[16]{0:T(128)S(1)} %convolution_bitcast_fusion, f32[]{:T(128)} %get-tuple-element.5), channel_id=1, replica_groups=mesh['blk'=32,'grp'=8] {'blk','grp'}, use_global_device_ids=true, to_apply=%region_3.4 | all-reduce | flops 17 | bytes 136 | tf_op jit(solution)/shard_map/psum | solution.py:73
  337.8 0.6 broadcast_divide_fusion
  338.5 0.1 multiply_reduce_fusion
  338.6 73.4 %psum.31 = f32[16]{0:T(128)S(1)} all-reduce(f32[16]{0:T(128)S(1)} %multiply_reduce_fusion), channel_id=1, replica_groups=mesh['blk'=32,'grp'=8] {'blk','grp'}, use_global_device_ids=true, to_apply=%region_7.8 | all-reduce | flops 16 | bytes 128 | tf_op jit(solution)/shard_map/psum | solution.py:75
  412.0 0.7 fusion.37
  (9 shorter events, 0.2 us)
Async XLA Ops:
  20.4 39.1 %collective-permute-start = (bf16[128,45,128]{2,0,1:T(8,128)(2,1)S(1)}, bf16[128,45,128]{2,0,1:T(8,128)(2,1)S(1)}, u32[]{:S(2)}, u32[]{:S(2)}) collective-permute-start(bf16[128,45,128]{2,0,1:T(8,128)(2,1)S(1)} %multiply_convert_fusion), channel_id=1, source_target_pairs={{248,0},{0,8},{8,16},{16,24},{24,32},{32,40},{40,48},{48,56},{56,6... | collective-permute-start | bytes 4423688 | tf_op jit(solution)/shard_map/ppermute | solution.py:15
  27.5 35.0 %collective-permute-start.1 = (bf16[128,45,128]{2,0,1:T(8,128)(2,1)S(1)}, bf16[128,45,128]{2,0,1:T(8,128)(2,1)S(1)}, u32[]{:S(2)}, u32[]{:S(2)}) collective-permute-start(bf16[128,45,128]{2,0,1:T(8,128)(2,1)S(1)} %multiply_convert_fusion), channel_id=1, source_target_pairs={{8,0},{16,8},{24,16},{32,24},{40,32},{48,40},{56,48},{64,56},{72,6... | collective-permute-start | bytes 4423688 | tf_op jit(solution)/shard_map/ppermute | solution.py:15
  62.5 1.1 copy-start
  67.5 7.4 %copy-start.1 = (bf16[128,45,128]{2,0,1:T(8,128)(2,1)S(1)}, bf16[128,45,128]{2,0,1:T(8,128)(2,1)}, u32[]{:S(2)}) copy-start(bf16[128,45,128]{2,0,1:T(8,128)(2,1)} %copy-done) | copy-start | bytes 4423684
  99.2 96.4 %all-to-all-start = ((bf16[90,128,384]{2,0,1:T(8,128)(2,1)}), bf16[90,128,384]{2,0,1:T(8,128)(2,1)}, u32[]{:S(2)}, u32[]{:S(2)}) async-start(bf16[90,128,384]{2,0,1:T(8,128)(2,1)} %copy.18), calls=%async_computation | async-start | bytes 18874368 | tf_op jit(solution)/shard_map/all_to_all | solution.py:52
  206.2 13.6 %copy-start.2 = (f32[16,16]{1,0:T(8,128)S(1)}, f32[16,16]{1,0:T(8,128)}, u32[]{:S(2)}) copy-start(f32[16,16]{1,0:T(8,128)} %param.3) | copy-start | bytes 3076
  241.7 10.8 %collective-permute-start.2 = (f32[128,16]{1,0:T(8,128)S(1)}, f32[128,16]{1,0:T(8,128)S(1)}, u32[]{:S(2)}, u32[]{:S(2)}) collective-permute-start(f32[128,16]{1,0:T(8,128)S(1)} %all_gather.3), channel_id=1, source_target_pairs={{248,0},{0,8},{8,16},{16,24},{24,32},{32,40},{40,48},{48,56},{56,6... | collective-permute-start | bytes 24584 | tf_op jit(solution)/shard_map/ppermute | solution.py:15
  251.1 5.2 %collective-permute-start.3 = (f32[128,16]{1,0:T(8,128)S(1)}, f32[128,16]{1,0:T(8,128)S(1)}, u32[]{:S(2)}, u32[]{:S(2)}) collective-permute-start(f32[128,16]{1,0:T(8,128)S(1)} %all_gather.3), channel_id=1, source_target_pairs={{8,0},{16,8},{24,16},{32,24},{40,32},{48,40},{56,48},{64,56},{72,6... | collective-permute-start | bytes 24584 | tf_op jit(solution)/shard_map/ppermute | solution.py:15
where the time goes:
time: 413 us
  blocking collectives  193 us (47%)
  waiting for transfers between devices  131 us (32%)
  matrix products  24.5 us (6%)
  local copies, waits for them, and re-layouts  24.4 us (6%)
  starting transfers between devices  21.8 us (5%)
  other arithmetic  17.7 us (4%)
    all_to_all x1, waiting for transfers between devices, per_device(): lax.all_to_all(pair_terms, 'grp', split_axis=1, concat_axis=0, tiled=True)  91 us
    psum x1, blocking collectives, per_device(): projection = lax.psum(local_proj, ('blk', 'grp'))  81 us
    psum x1, blocking collectives, per_device(): column_sq = lax.psum(jnp.sum(deflated * deflated, axis=0), ('blk', 'grp'))  73.4 us
    ppermute x4, waiting for transfers between devices, passed_along(): return lax.ppermute(block, axis, route)  40.1 us
    all_gather x1, blocking collectives, per_device(): block_vec = lax.all_gather(scaled, 'grp', axis=0, tiled=True)  21.8 us
    psum x1, blocking collectives, per_device(): total_sq = lax.psum(squares, 'grp')  16.8 us
    ppermute x4, starting transfers between devices, passed_along(): return lax.ppermute(block, axis, route)  16.5 us
    dot_general x1, matrix products, per_device(): jnp.einsum('frj,fm->rjm', lax.all_to_all(pair_terms, 'grp', split_axis=1,...  12.9 us
  transfers between devices with their start and end apart: 5, of which 5 were waited for; matrix products, arithmetic and copies ran while one was open for 0% of the time, Pallas kernels for 0%

commit v1 on v0

v1 whole, which is shorter than its diff:
```python
import functools
import math

import jax
import jax.numpy as jnp
from jax import lax
from jax.experimental import pallas as pl
from jax.experimental.pallas import tpu as pltpu
from jax.sharding import PartitionSpec as P

sharpness = 2.5
epsilon = 1e-06
HIGHEST = lax.Precision.HIGHEST
VMEM_LIMIT = 48 * 1024 * 1024


def passed_along(block, axis, distance):
    devices = range(lax.axis_size(axis))
    route = [((i - distance) % len(devices), i) for i in devices]
    return lax.ppermute(block, axis, route)


def trig_columns(freq_local, group_size):
    total = freq_local * group_size
    row_ids = jnp.arange(2 * total, dtype=jnp.int32)
    freq = row_ids // 2
    angles = jnp.arange(total, dtype=jnp.int32)
    phase = (angles[:, None] * freq[None, :] % total).astype(jnp.float32) * (2.0 * math.pi / total)
    cos_part = jnp.cos(phase).astype(jnp.bfloat16)
    sin_part = (-jnp.sin(phase)).astype(jnp.bfloat16)
    return jnp.where((row_ids % 2 == 1)[None, :], sin_part, cos_part)


def iota(shape, dim):
    return lax.broadcasted_iota(jnp.int32, shape, dim)


def dot(a, b, dims):
    return lax.dot_general(a, b, (dims, ((), ())), precision=HIGHEST, preferred_element_type=jnp.float32)


def start_kernel(group_ref, coeffs_ref, vectors_ref, out_ref, sq_ref):
    step = pl.program_id(0)
    size = coeffs_ref.shape[0]
    values = coeffs_ref[...].astype(jnp.float32)
    sq_ref[pl.ds(pl.multiple_of(step * size, size), size), :] = jnp.sum(values * values, axis=1)

    @pl.when(step == pl.num_programs(0) - 1)
    def _():
        block = sq_ref.shape[0]
        rows = vectors_ref.shape[0]
        total = dot(jnp.ones((8, sq_ref.shape[1]), jnp.float32), sq_ref[...], ((1,), (1,)))
        place = iota((rows, block), 1) == iota((rows, block), 0) + rows * group_ref[0]
        placed = dot(vectors_ref[...], place.astype(jnp.float32), ((0,), (0,)))
        for d in range(out_ref.shape[0]):
            out_ref[d, 0:8, :] = total
            out_ref[d, 8 : 8 + placed.shape[0], :] = placed


def start(group_index, coeffs, vectors, group_size):
    block, freq_local, channels = coeffs.shape
    rows = 8 + vectors.shape[1]
    steps = 4
    return pl.pallas_call(
        start_kernel,
        grid_spec=pltpu.PrefetchScalarGridSpec(
            num_scalar_prefetch=1,
            grid=(steps,),
            in_specs=[
                pl.BlockSpec((block // steps, freq_local, channels), lambda s, g: (s, 0, 0)),
                pl.BlockSpec(vectors.shape, lambda s, g: (0, 0)),
            ],
            out_specs=pl.BlockSpec((group_size, rows, block), lambda s, g: (0, 0, 0)),
            scratch_shapes=[pltpu.VMEM((block, channels), jnp.float32)],
        ),
        out_shape=jax.ShapeDtypeStruct((group_size, rows, block), jnp.float32),
        compiler_params=pltpu.CompilerParams(vmem_limit_bytes=VMEM_LIMIT),
        name="start",
    )(group_index, coeffs, vectors)


def swapped(a):
    half = a.shape[1] // 2
    wide = a.astype(jnp.float32)
    turned = pltpu.roll(wide, half, 1)
    return jnp.where(iota(a.shape, 1) < half, turned, -turned).astype(a.dtype)


def upper_half(half, block):
    gap = (iota((half, block), 1) - iota((half, block), 0)) & (block - 1)
    return (gap >= 1) & (gap <= half), gap != 0


def cross_kernel(folded, a_ref, b_ref, out_ref):
    block = a_ref.shape[1]
    half = block // 2
    parts = out_ref.shape[0]
    for k in range(a_ref.shape[0]):
        a = a_ref[k]
        lhs = jnp.concatenate([a, swapped(a)], axis=0)
        pair = lax.dot_general(lhs, b_ref[k], (((1,), (1,)), ((), ())), preferred_element_type=jnp.float32)
        real, imag = pair[:block], pair[block:]
        if folded:
            top, _ = upper_half(half, block)
            real = jnp.where(top, real[:half], real[half:])
            imag = jnp.where(top, imag[:half], imag[half:])
        rows = real.shape[0] // parts
        for d in range(parts):
            both = jnp.concatenate([real[d * rows : (d + 1) * rows], imag[d * rows : (d + 1) * rows]], axis=0)
            out_ref[d, k * 2 * rows : (k + 1) * 2 * rows, :] = both.astype(jnp.bfloat16)


def cross(folded, own, other, parts, steps):
    freq, block, channels = own.shape
    rows = freq * (block if folded else 2 * block) // parts
    one = freq // steps
    spec = pl.BlockSpec((one, block, channels), lambda s: (s, 0, 0))
    return pl.pallas_call(
        functools.partial(cross_kernel, folded),
        grid=(steps,),
        in_specs=[spec, spec],
        out_specs=pl.BlockSpec((parts, rows // steps, block), lambda s: (0, s, 0)),
        out_shape=jax.ShapeDtypeStruct((parts, rows, block), jnp.bfloat16),
        compiler_params=pltpu.CompilerParams(vmem_limit_bytes=VMEM_LIMIT),
        name="cross_own" if folded else "cross_next",
    )(own, other)


def affinities(terms_ref, trig_ref, held_ref, rows, factor):
    depth = trig_ref.shape[1]
    angles = trig_ref.shape[0]
    width = terms_ref.shape[1]
    chunk = 16 * rows
    at = iota((chunk, chunk), 0)
    turn = (iota((chunk, chunk), 1) == (at & 15) * rows + (at >> 4)).astype(jnp.bfloat16)
    for c in range(depth // 16):
        piece = terms_ref[c * chunk : (c + 1) * chunk, :]
        turned = jnp.dot(turn, piece, preferred_element_type=jnp.float32).astype(jnp.bfloat16)
        for i in range(rows):
            held_ref[c * 16 : (c + 1) * 16, i * width : (i + 1) * width] = turned[i * 16 : (i + 1) * 16]
    out = []
    for pair in range(rows // 2):
        corr = jnp.dot(
            trig_ref[...], held_ref[:, pair * 2 * width : (pair + 1) * 2 * width], preferred_element_type=jnp.float32
        )
        mean = jnp.sum(jnp.exp(factor * corr), axis=0, keepdims=True) * (1.0 / angles)
        out += [mean[:, :width], mean[:, width:]]
    return out


def own_kernel(factor, group_ref, terms_ref, trig_ref, out_ref, held_ref):
    rows = 8
    block = terms_ref.shape[1]
    means = affinities(terms_ref, trig_ref, held_ref, rows, factor)
    for i in range(rows):
        out_ref[i : i + 1, :] = means[i]
    at = iota((rows, block), 0) + rows * group_ref[0]
    gap = (iota((rows, block), 1) - at) & (block - 1)
    out_ref[...] = jnp.where(gap == 0, 0.0, out_ref[...])


def own_part(group_index, terms, trig, factor):
    rows = 8
    block = terms.shape[1]
    return pl.pallas_call(
        functools.partial(own_kernel, factor),
        in_specs=[pl.BlockSpec(memory_space=pltpu.SMEM)] + [pl.BlockSpec(memory_space=pltpu.VMEM)] * 2,
        out_specs=pl.BlockSpec(memory_space=pltpu.VMEM),
        out_shape=jax.ShapeDtypeStruct((rows, block), jnp.float32),
        scratch_shapes=[pltpu.VMEM((trig.shape[1], rows * block), jnp.bfloat16)],
        compiler_params=pltpu.CompilerParams(vmem_limit_bytes=VMEM_LIMIT),
        name="own_part",
    )(group_index, terms, trig)


def next_kernel(factor, group_ref, terms_ref, trig_ref, own_ref, out_ref, held_ref, wide_ref):
    rows = 16
    block = terms_ref.shape[1]
    half = block // 2
    group = group_ref[0]
    means = affinities(terms_ref, trig_ref, held_ref, rows, factor)
    for i in range(rows):
        out_ref[i : i + 1, :] = means[i]
    own = own_ref[...]
    at = iota((8, block), 0) + 8 * group
    gap = (iota((8, block), 1) - at) & (block - 1)
    top = (gap >= 1) & (gap <= half)
    upper, lower = jnp.where(top, own, 0.0), jnp.where(top, 0.0, own)
    wide_ref[...] = jnp.zeros_like(wide_ref)
    wide_ref[pl.ds(pl.multiple_of(rows * group, rows), rows), :] = out_ref[0:rows, :]
    own_at = pl.multiple_of(8 * group, 8)
    wide_ref[pl.ds(block + own_at, 8), :] = upper
    wide_ref[pl.ds(block + half + own_at, 8), :] = lower
    ones = jnp.ones((8, block), jnp.float32)
    by_row = dot(ones, wide_ref[...], ((1,), (1,)))
    degree = by_row[0:1, :block] + by_row[0:1, block:] + jnp.sum(own, axis=0, keepdims=True)
    out_ref[rows : rows + 8, :] = jnp.zeros((8, block), jnp.float32)
    out_ref[rows : rows + 1, :] = degree
    out_ref[rows + 1 : rows + 2, :] = jnp.sum(out_ref[0:rows, :], axis=0, keepdims=True)


def next_part(group_index, terms, trig, own, factor):
    rows = 16
    block = terms.shape[1]
    return pl.pallas_call(
        functools.partial(next_kernel, factor),
        in_specs=[pl.BlockSpec(memory_space=pltpu.SMEM)] + [pl.BlockSpec(memory_space=pltpu.VMEM)] * 3,
        out_specs=pl.BlockSpec(memory_space=pltpu.VMEM),
        out_shape=jax.ShapeDtypeStruct((rows + 8, block), jnp.float32),
        scratch_shapes=[
            pltpu.VMEM((trig.shape[1], rows * block), jnp.bfloat16),
            pltpu.VMEM((2 * block, block), jnp.float32),
        ],
        compiler_params=pltpu.CompilerParams(vmem_limit_bytes=VMEM_LIMIT),
        name="next_part",
    )(group_index, terms, trig, own)


def image_kernel(group_ref, parts_ref, vec_ref, out_ref, own_ref, full_ref):
    groups, _, block = parts_ref.shape
    half = block // 2
    shares = parts_ref[0, 40:48, :]
    for s in range(groups):
        if s:
            shares = shares + parts_ref[s, 40:48, :]
        full_ref[0, 16 * s : 16 * s + 16, :] = parts_ref[s, 0:16, :]
        full_ref[1, 16 * s : 16 * s + 16, :] = parts_ref[s, 16:32, :]
        full_ref[2, 8 * s : 8 * s + 8, :] = parts_ref[s, 32:40, :]
    top, _ = upper_half(half, block)
    own = full_ref[2, 0:half, :]
    full_ref[2, 0:half, :] = jnp.where(top, own, 0.0)
    full_ref[2, half:block, :] = jnp.where(top, 0.0, own)
    inv_root = lax.rsqrt(shares)
    scaled_before = vec_ref[0] * inv_root[0:1, :]
    scaled_own = vec_ref[1] * inv_root[1:2, :]
    scaled_after = vec_ref[2] * inv_root[2:3, :]
    along, across = ((1,), (1,)), ((1,), (0,))
    product = dot(scaled_own, full_ref[2], along) + dot(scaled_own, full_ref[2], across)
    product = product + dot(scaled_after, full_ref[0], along) + dot(scaled_before, full_ref[1], across)
    image = product * inv_root[1:2, :] * (3.0 * block)
    degree = shares[1:2, :]
    root_degree = jnp.sqrt(degree)
    degree_sum = jnp.sum(degree, axis=1, keepdims=True)
    proj = jnp.sum(root_degree * image, axis=1, keepdims=True)
    rest = image - root_degree * (proj / degree_sum)
    rest_sq = jnp.sum(rest * rest, axis=1, keepdims=True)
    count = image.shape[0]
    at, lane = iota((count, block), 0), iota((count, block), 1)
    stats = jnp.where(lane == at, proj, 0.0) + jnp.where(lane == at + count, rest_sq, 0.0)
    stats = jnp.sum(stats, axis=0, keepdims=True)
    stats = jnp.where(iota((1, block), 1) == 2 * count, degree_sum, stats)
    out_ref[...] = jnp.broadcast_to(stats, out_ref.shape)
    place = (lane == at + count * group_ref[0]).astype(jnp.float32)
    own_ref[0] = dot(place, image, along)
    own_ref[1] = dot(place, jnp.broadcast_to(root_degree, image.shape), along)


def image_part(group_index, parts, vecs, n_blk):
    groups, _, block = parts.shape
    count = vecs.shape[1]
    return pl.pallas_call(
        image_kernel,
        in_specs=[pl.BlockSpec(memory_space=pltpu.SMEM)] + [pl.BlockSpec(memory_space=pltpu.VMEM)] * 2,
        out_specs=[pl.BlockSpec(memory_space=pltpu.VMEM)] * 2,
        out_shape=[
            jax.ShapeDtypeStruct((n_blk, block), jnp.float32),
            jax.ShapeDtypeStruct((2, count, count), jnp.float32),
        ],
        scratch_shapes=[pltpu.VMEM((3, block, block), jnp.float32)],
        compiler_params=pltpu.CompilerParams(vmem_limit_bytes=VMEM_LIMIT),
        name="image_part",
    )(group_index, parts, vecs)


def final_kernel(total_rows, stats_ref, own_ref, out_ref):
    count = out_ref.shape[1]
    stats = stats_ref[...]
    proj, rest_sq, degree = stats[:, :count], stats[:, count : 2 * count], stats[:, 2 * count : 2 * count + 1]
    ratio = jnp.sum(proj, axis=0, keepdims=True) / jnp.sum(degree, axis=0, keepdims=True)
    shift = proj / degree - ratio
    column_sq = jnp.sum(rest_sq + degree * (shift * shift), axis=0, keepdims=True)
    deflated = own_ref[0] - own_ref[1] * ratio
    out_ref[...] = deflated * lax.rsqrt(column_sq / total_rows + epsilon)


def final_part(stats, own, total_rows):
    count = own.shape[1]
    return pl.pallas_call(
        functools.partial(final_kernel, total_rows),
        in_specs=[pl.BlockSpec(memory_space=pltpu.VMEM)] * 2,
        out_specs=pl.BlockSpec(memory_space=pltpu.VMEM),
        out_shape=jax.ShapeDtypeStruct((count, count), jnp.float32),
        name="final_part",
    )(stats, own)


def per_device(coeffs, vectors):
    block, freq_local, channels = coeffs.shape
    group_size = lax.axis_size("grp")
    n_blk = lax.axis_size("blk")
    group_index = lax.axis_index("grp").astype(jnp.int32)[None]
    angles = freq_local * group_size
    factor = sharpness / math.sqrt(angles * channels)
    trig = trig_columns(freq_local, group_size)

    after_raw = passed_along(coeffs, "blk", -1)
    begun = start(group_index, coeffs, vectors, group_size)
    summed = jnp.sum(lax.all_to_all(begun, "grp", 0, 0, tiled=True), axis=0)
    summed_after = passed_along(summed, "blk", -1)
    summed_before = passed_along(summed, "blk", 1)

    def unit(raw, sums):
        inv_norm = lax.rsqrt(sums[0] / (angles * channels) + epsilon)
        return (raw.astype(jnp.float32) * inv_norm[:, None, None]).astype(jnp.bfloat16).transpose(1, 0, 2)

    own_unit = unit(coeffs, summed)
    own_terms = cross(True, own_unit, own_unit, group_size, 5)
    own_terms = lax.all_to_all(own_terms, "grp", 0, 0, tiled=True).reshape(-1, block)
    after_unit = unit(after_raw, summed_after)
    next_terms = cross(False, own_unit, after_unit, group_size, 5)
    next_terms = lax.all_to_all(next_terms, "grp", 0, 0, tiled=True).reshape(-1, block)
    own_aff = own_part(group_index, own_terms, trig, factor)
    found = next_part(group_index, next_terms, trig, own_aff, factor)

    found_before = passed_along(found, "blk", 1)
    edge_after = passed_along(found[16:], "blk", -1)
    edge_before = passed_along(found[16:], "blk", 2)
    zeros = jnp.zeros((5, block), jnp.float32)
    shares = jnp.concatenate(
        [
            found_before[16:17] + edge_before[1:2],
            found[16:17] + found_before[17:18],
            edge_after[0:1] + found[17:18],
            zeros,
        ],
        axis=0,
    )
    sent = jnp.concatenate([found[:16], found_before[:16], own_aff, shares], axis=0)
    sent = jnp.broadcast_to(sent[None], (group_size,) + sent.shape)
    parts = lax.all_to_all(sent, "grp", 0, 0, tiled=True)
    vecs = jnp.stack([summed_before[8:], summed[8:], summed_after[8:]])
    stats, own = image_part(group_index, parts, vecs, n_blk)
    stats = lax.all_to_all(stats, "blk", 0, 0, tiled=True)
    return final_part(stats, own, block * n_blk)


def solution(mesh):
    placed = (P("blk", "grp", None), P(("blk", "grp"), None))
    return jax.shard_map(
        per_device, mesh=mesh, in_specs=placed, out_specs=P(("blk", "grp"), None), check_vma=False
    )
```

time: 413 us -> 143 us (0.35)
  blocking collectives: 193 us -> 21.2 us
  waiting for transfers between devices: 131 us -> 60.4 us
  matrix products: 24.5 us -> 0 us
  local copies, waits for them, and re-layouts: 24.4 us -> 8.85 us
  Pallas kernels: 0 us -> 12 us
  starting transfers between devices: 21.8 us -> 31 us
  other arithmetic: 17.7 us -> 8.64 us
    psum x3 -> x0, blocking collectives: 171 us -> none  [the longest x1 81 us: per_device(): projection = lax.psum(local_proj, ('blk', 'grp'))]
    all_to_all x1 -> x4, waiting for transfers between devices: 91 us -> 35.5 us  [the longest x1 25.1 us: per_device(): lax.all_to_all(next_terms, 'grp', 0, 0, tiled=True).reshape(-1, block)]
    dot_general x5 -> x0, matrix products: 24.5 us -> none  [the longest x1 12.9 us: per_device(): jnp.einsum('frj,fm->rjm', lax.all_to_all(pair_terms, 'grp', split_axis=1,...]
    all_gather x1 -> x0, blocking collectives: 21.8 us -> none  [per_device(): block_vec = lax.all_gather(scaled, 'grp', axis=0, tiled=True)]
    all_to_all x0 -> x1, blocking collectives: none -> 21.2 us  [per_device(): stats = lax.all_to_all(stats, 'blk', 0, 0, tiled=True)]
    all_to_all x1 -> x4, starting transfers between devices: 5.25 us -> 21.2 us  [the longest x1 7.33 us: per_device(): parts = lax.all_to_all(sent, 'grp', 0, 0, tiled=True)]
    ppermute x4 -> x6, waiting for transfers between devices: 40.1 us -> 24.9 us  [passed_along(): return lax.ppermute(block, axis, route)]
    concatenate x1, local copies, waits for them, and re-layouts: 12.5 us -> 0.03 us  [per_device(): jnp.concatenate([found[:16], found_before[:16], own_aff, shares], axis=0)]
  transfers between devices with their start and end apart: 5 -> 10, of which waited for: 5 -> 5; matrix products, arithmetic and copies ran while one was open for 0% -> 7% of each run, Pallas kernels for 0% -> 6%
where the time goes in v1:
time: 143 us; the launch traced here: 142 us
  waiting for transfers between devices  60.4 us (42%)
  starting transfers between devices  31 us (22%)
  blocking collectives  21.2 us (15%)
  Pallas kernels  12 us (8%)
  local copies, waits for them, and re-layouts  8.85 us (6%)
  other arithmetic  8.64 us (6%)
    all_to_all x1, waiting for transfers between devices, per_device(): lax.all_to_all(next_terms, 'grp', 0, 0, tiled=True).reshape(-1, block)  25.1 us
    ppermute x6, waiting for transfers between devices, passed_along(): return lax.ppermute(block, axis, route)  24.9 us
    all_to_all x1, blocking collectives, per_device(): stats = lax.all_to_all(stats, 'blk', 0, 0, tiled=True)  21.2 us
    ppermute x6, starting transfers between devices, passed_along(): return lax.ppermute(block, axis, route)  9.77 us
    unnamed x13, local copies, waits for them, and re-layouts  8.12 us
    all_to_all x1, starting transfers between devices, per_device(): parts = lax.all_to_all(sent, 'grp', 0, 0, tiled=True)  7.33 us
    all_to_all x1, waiting for transfers between devices, per_device(): parts = lax.all_to_all(sent, 'grp', 0, 0, tiled=True)  6.05 us
    all_to_all x1, starting transfers between devices, per_device(): summed = jnp.sum(lax.all_to_all(begun, 'grp', 0, 0, tiled=True), axis=0)  5.86 us
  transfers between devices with their start and end apart: 10, of which 5 were waited for; matrix products, arithmetic and copies ran while one was open for 7% of the time, Pallas kernels for 6%

profile of v1, /device:TPU:1, one launch (start us, length us, event | category | flops | bytes accessed | tf_op | source)
XLA Modules:
  0.0 142.2 jit_solution(1061740722444009626)
XLA Ops:
  0.0 0.0 copy-start.5
  0.0 2.4 %copy.4.coeffs_ref = bf16[128,45,128]{2,1,0:T(8,128)(2,1)S(1)} copy(bf16[128,45,128]{2,0,1:T(8,128)(2,1)} %param.2) | data formatting | bytes 2949120 | tf_op args[0]
  2.4 0.0 copy-done.5
  2.4 1.4 start.1
  3.7 5.9 %all-to-all-start = ((f32[8,24,128]{2,1,0:T(8,128)}), f32[8,24,128]{2,1,0:T(8,128)S(1)}, u32[]{:S(2)}, u32[]{:S(2)}) async-start(f32[8,24,128]{2,1,0:T(8,128)} %start.1), calls=%async_computation | async-start | bytes 196608 | tf_op jit(solution)/shard_map/all_to_all | solution.py:308
  9.6 1.0 collective-permute-start
  10.6 4.4 %all-to-all-done = f32[8,24,128]{2,1,0:T(8,128)S(1)} async-done(((f32[8,24,128]{2,1,0:T(8,128)}), f32[8,24,128]{2,1,0:T(8,128)S(1)}, u32[]{:S(2)}, u32[]{:S(2)}) %all-to-all-start) | async-done | bytes 98336 | tf_op jit(solution)/shard_map/all_to_all | solution.py:308
  15.0 1.8 %fusion.a_ref.b_ref = bf16[45,128,128]{2,1,0:T(8,128)(2,1)S(1)} fusion(bf16[128,45,128]{2,0,1:T(8,128)(2,1)} %param.2, f32[128]{0:T(128)S(1)} %fusion.19), kind=kLoop, calls=%fused_computation.3 | loop fusion | flops 2211840 | bytes 2949632 | tf_op jit(solution)/shard_map/transpose | solution.py:314
  16.8 2.0 %cross_own.1 = bf16[8,720,128]{2,1,0:T(8,128)(2,1)S(1)} custom-call(bf16[45,128,128]{2,1,0:T(8,128)(2,1)S(1)} %fusion.a_ref.b_ref, bf16[45,128,128]{2,1,0:T(8,128)(2,1)S(1)} %fusion.a_ref.b_ref), custom_call_target="tpu_custom_call" | custom-call | tf_op jit(solution)/shard_map/cross_own/pallas_call | solution.py:118
  18.8 0.0 copy-start.3
  18.8 1.1 copy-done.3
  19.9 3.6 %all-to-all-start.2 = ((bf16[8,720,128]{2,1,0:T(8,128)(2,1)}), bf16[8,720,128]{2,1,0:T(8,128)(2,1)S(1)}, u32[]{:S(2)}, u32[]{:S(2)}) async-start(bf16[8,720,128]{2,1,0:T(8,128)(2,1)} %copy-done.3), calls=%async_computation.2 | async-start | bytes 2949120 | tf_op jit(solution)/shard_map/all_to_all | solution.py:318
  23.5 4.2 %collective-permute-start.1 = (f32[24,128]{1,0:T(8,128)S(1)}, f32[24,128]{1,0:T(8,128)S(1)}, u32[]{:S(2)}, u32[]{:S(2)}) collective-permute-start(f32[24,128]{1,0:T(8,128)S(1)} %reduce_sum.9), channel_id=1, source_target_pairs={{8,0},{16,8},{24,16},{32,24},{40,32},{48,40},{56,48},{64,56},{72,6... | collective-permute-start | bytes 36872 | tf_op jit(solution)/shard_map/ppermute | solution.py:20
  27.7 19.5 %collective-permute-done.1 = f32[24,128]{1,0:T(8,128)S(1)} collective-permute-done((f32[24,128]{1,0:T(8,128)S(1)}, f32[24,128]{1,0:T(8,128)S(1)}, u32[]{:S(2)}, u32[]{:S(2)}) %collective-permute-start.1) | collective-permute-done | bytes 12320 | tf_op jit(solution)/shard_map/ppermute | solution.py:20
  47.2 0.0 collective-permute-done
  47.2 1.9 %fusion.1.b_ref = bf16[45,128,128]{2,1,0:T(8,128)(2,1)S(1)} fusion(bf16[128,45,128]{2,0,1:T(8,128)(2,1)} %collective-permute-done, f32[128]{0:T(128)S(1)} %fusion.16), kind=kLoop, calls=%fused_computation.4 | loop fusion | flops 2211840 | bytes 2949632 | tf_op jit(solution)/shard_map/transpose | solution.py:314
  49.1 2.0 %cross_next.1 = bf16[8,1440,128]{2,1,0:T(8,128)(2,1)S(1)} custom-call(bf16[45,128,128]{2,1,0:T(8,128)(2,1)S(1)} %fusion.a_ref.b_ref, bf16[45,128,128]{2,1,0:T(8,128)(2,1)S(1)} %fusion.1.b_ref), custom_call_target="tpu_custom_call" | custom-call | tf_op jit(solution)/shard_map/cross_next/pallas_call | solution.py:118
  51.1 0.0 copy-start
  51.1 1.6 %copy-done = bf16[8,1440,128]{2,1,0:T(8,128)(2,1)} copy-done((bf16[8,1440,128]{2,1,0:T(8,128)(2,1)}, bf16[8,1440,128]{2,1,0:T(8,128)(2,1)S(1)}, u32[]{:S(2)}) %copy-start) | copy-done | bytes 2949144
  52.7 0.0 all-to-all-done.2
  52.7 0.0 copy-start.1
  52.7 1.1 copy-done.1
  53.8 4.4 %all-to-all-start.1 = ((bf16[8,1440,128]{2,1,0:T(8,128)(2,1)}), bf16[8,1440,128]{2,1,0:T(8,128)(2,1)S(1)}, u32[]{:S(2)}, u32[]{:S(2)}) async-start(bf16[8,1440,128]{2,1,0:T(8,128)(2,1)} %copy-done), calls=%async_computation.1 | async-start | bytes 5898240 | tf_op jit(solution)/shard_map/all_to_all | solution.py:321
  58.3 4.9 %fusion.7.trig_ref = bf16[360,720]{1,0:T(8,128)(2,1)S(1)} fusion(s32[720]{0:T(1024)S(1)} %add_select_fusion.1, pred[720]{0:T(1024)(128)(4,1)S(1)} %fusion.8), kind=kLoop, calls=%fused_computation.13 | loop fusion | flops 3369600 | bytes 522000 | tf_op jit(solution)/shard_map/jit(_where)/select_n | solution.py:31
  63.1 0.8 collective-permute-start.5
  63.9 0.0 copy-start.2
  63.9 1.4 copy-done.2
  65.3 1.2 own_part.1.own_ref
  66.5 25.1 %all-to-all-done.1 = bf16[8,1440,128]{2,1,0:T(8,128)(2,1)S(1)} async-done(((bf16[8,1440,128]{2,1,0:T(8,128)(2,1)}), bf16[8,1440,128]{2,1,0:T(8,128)(2,1)S(1)}, u32[]{:S(2)}, u32[]{:S(2)}) %all-to-all-start.1) | async-done | bytes 2949152 | tf_op jit(solution)/shard_map/all_to_all | solution.py:321
  91.6 3.3 %next_part.1 = f32[24,128]{1,0:T(8,128)S(1)} custom-call(s32[1]{0:T(128)} %bitcast.group_ref, bf16[11520,128]{1,0:T(8,128)(2,1)S(1)} %bitcast.21, bf16[360,720]{1,0:T(8,128)(2,1)S(1)} %fusion.7.trig_ref, f32[8,128]{1,0:T(8,128)S(1)} %own_part.1.own_ref), custom_call_target="tpu_custom_call" | custom-call | tf_op jit(solution)/shard_map/next_part/pallas_call | solution.py:205
  94.8 2.8 %collective-permute-start.2 = (f32[24,128]{1,0:T(8,128)S(1)}, f32[24,128]{1,0:T(8,128)S(1)}, u32[]{:S(2)}, u32[]{:S(2)}) collective-permute-start(f32[24,128]{1,0:T(8,128)S(1)} %next_part.1), channel_id=1, source_target_pairs={{248,0},{0,8},{8,16},{16,24},{24,32},{32,40},{40,48},{48,56},{56,6... | collective-permute-start | bytes 36872 | tf_op jit(solution)/shard_map/ppermute | solution.py:20
  97.6 1.0 collective-permute-start.3
  98.6 0.0 collective-permute-start.4
  98.6 5.4 %collective-permute-done.3 = f32[8,128]{1,0:T(8,128)S(1)} collective-permute-done((f32[8,128]{1,0:T(8,128)S(1)}, f32[8,128]{1,0:T(8,128)S(1)}, u32[]{:S(2)}, u32[]{:S(2)}) %collective-permute-start.3) | collective-permute-done | bytes 4128 | tf_op jit(solution)/shard_map/ppermute | solution.py:20
  104.0 0.0 collective-permute-done.4
  104.0 0.0 collective-permute-done.2
  104.1 0.7 broadcast_in_dim.30
  104.8 7.3 %all-to-all-start.3 = ((f32[8,48,128]{2,1,0:T(8,128)}), f32[8,48,128]{2,1,0:T(8,128)S(1)}, u32[]{:S(2)}, u32[]{:S(2)}) async-start(f32[8,48,128]{2,1,0:T(8,128)} %broadcast_in_dim.30), calls=%async_computation.3 | async-start | bytes 393216 | tf_op jit(solution)/shard_map/all_to_all | solution.py:340
  112.1 0.0 collective-permute-done.5
  112.1 6.1 %all-to-all-done.3.parts_ref = f32[8,48,128]{2,1,0:T(8,128)S(1)} async-done(((f32[8,48,128]{2,1,0:T(8,128)}), f32[8,48,128]{2,1,0:T(8,128)S(1)}, u32[]{:S(2)}, u32[]{:S(2)}) %all-to-all-start.3) | async-done | bytes 196640 | tf_op jit(solution)/shard_map/all_to_all | solution.py:340
  118.2 0.6 image_part.1
  118.8 0.0 copy-start.4
  118.8 0.6 copy-done.4
  119.4 21.2 %all_to_all.31 = f32[32,1,128]{2,1,0:T(1,128)} all-to-all(f32[32,1,128]{2,1,0:T(1,128)S(1)} %bitcast.23), channel_id=1, replica_groups=mesh['blk'=32,'grp'=8] {'blk'}, dimensions={0} | all-to-all | bytes 32768 | tf_op jit(solution)/shard_map/all_to_all | solution.py:343
  140.7 1.6 %final_part.1 = f32[16,16]{1,0:T(8,128)} custom-call(f32[32,128]{1,0:T(8,128)} %bitcast.24, f32[2,16,16]{2,1,0:T(8,128)} %copy-done.4), custom_call_target="tpu_custom_call" | custom-call | tf_op jit(solution)/shard_map/final_part/pallas_call | solution.py:288
  (15 shorter events, 0.1 us)
Async XLA Ops:
  0.0 2.4 %copy-start.5 = (f32[16,16]{1,0:T(8,128)S(1)}, f32[16,16]{1,0:T(8,128)}, u32[]{:S(2)}) copy-start(f32[16,16]{1,0:T(8,128)} %vectors_ref.1) | copy-start | bytes 3076
  3.7 11.2 %all-to-all-start = ((f32[8,24,128]{2,1,0:T(8,128)}), f32[8,24,128]{2,1,0:T(8,128)S(1)}, u32[]{:S(2)}, u32[]{:S(2)}) async-start(f32[8,24,128]{2,1,0:T(8,128)} %start.1), calls=%async_computation | async-start | bytes 196608 | tf_op jit(solution)/shard_map/all_to_all | solution.py:308
  9.6 37.6 %collective-permute-start = (bf16[128,45,128]{2,0,1:T(8,128)(2,1)}, bf16[128,45,128]{2,0,1:T(8,128)(2,1)}, u32[]{:S(2)}, u32[]{:S(2)}) collective-permute-start(bf16[128,45,128]{2,0,1:T(8,128)(2,1)} %param.2), channel_id=1, source_target_pairs={{8,0},{16,8},{24,16},{32,24},{40,32},{48,40},{56,48},{64,56},{72,6... | collective-permute-start | bytes 4423688 | tf_op jit(solution)/shard_map/ppermute | solution.py:20
  18.8 1.1 copy-start.3
  19.9 32.8 %all-to-all-start.2 = ((bf16[8,720,128]{2,1,0:T(8,128)(2,1)}), bf16[8,720,128]{2,1,0:T(8,128)(2,1)S(1)}, u32[]{:S(2)}, u32[]{:S(2)}) async-start(bf16[8,720,128]{2,1,0:T(8,128)(2,1)} %copy-done.3), calls=%async_computation.2 | async-start | bytes 2949120 | tf_op jit(solution)/shard_map/all_to_all | solution.py:318
  23.5 23.7 %collective-permute-start.1 = (f32[24,128]{1,0:T(8,128)S(1)}, f32[24,128]{1,0:T(8,128)S(1)}, u32[]{:S(2)}, u32[]{:S(2)}) collective-permute-start(f32[24,128]{1,0:T(8,128)S(1)} %reduce_sum.9), channel_id=1, source_target_pairs={{8,0},{16,8},{24,16},{32,24},{40,32},{48,40},{56,48},{64,56},{72,6... | collective-permute-start | bytes 36872 | tf_op jit(solution)/shard_map/ppermute | solution.py:20
  51.1 1.6 %copy-start = (bf16[8,1440,128]{2,1,0:T(8,128)(2,1)}, bf16[8,1440,128]{2,1,0:T(8,128)(2,1)S(1)}, u32[]{:S(2)}) copy-start(bf16[8,1440,128]{2,1,0:T(8,128)(2,1)S(1)} %cross_next.1) | copy-start | bytes 8847364
  52.7 1.1 copy-start.1
  53.8 37.8 %all-to-all-start.1 = ((bf16[8,1440,128]{2,1,0:T(8,128)(2,1)}), bf16[8,1440,128]{2,1,0:T(8,128)(2,1)S(1)}, u32[]{:S(2)}, u32[]{:S(2)}) async-start(bf16[8,1440,128]{2,1,0:T(8,128)(2,1)} %copy-done), calls=%async_computation.1 | async-start | bytes 5898240 | tf_op jit(solution)/shard_map/all_to_all | solution.py:321
  63.1 49.0 %collective-permute-start.5 = (f32[24,128]{1,0:T(8,128)S(1)}, f32[24,128]{1,0:T(8,128)S(1)}, u32[]{:S(2)}, u32[]{:S(2)}) collective-permute-start(f32[24,128]{1,0:T(8,128)S(1)} %reduce_sum.9), channel_id=1, source_target_pairs={{248,0},{0,8},{8,16},{16,24},{24,32},{32,40},{40,48},{48,56},{56,6... | collective-permute-start | bytes 36872 | tf_op jit(solution)/shard_map/ppermute | solution.py:20
  63.9 1.4 copy-start.2
  94.8 9.2 %collective-permute-start.2 = (f32[24,128]{1,0:T(8,128)S(1)}, f32[24,128]{1,0:T(8,128)S(1)}, u32[]{:S(2)}, u32[]{:S(2)}) collective-permute-start(f32[24,128]{1,0:T(8,128)S(1)} %next_part.1), channel_id=1, source_target_pairs={{248,0},{0,8},{8,16},{16,24},{24,32},{32,40},{40,48},{48,56},{56,6... | collective-permute-start | bytes 36872 | tf_op jit(solution)/shard_map/ppermute | solution.py:20
  97.6 6.4 %collective-permute-start.3 = (f32[8,128]{1,0:T(8,128)S(1)}, f32[8,128]{1,0:T(8,128)S(1)}, u32[]{:S(2)}, u32[]{:S(2)}) collective-permute-start(f32[8,128]{1,0:T(8,128)S(1)} %slice.62), channel_id=1, source_target_pairs={{240,0},{248,8},{0,16},{8,24},{16,32},{24,40},{32,48},{40,56},{48,... | collective-permute-start | bytes 12296 | tf_op jit(solution)/shard_map/ppermute | solution.py:20
  98.6 5.4 %collective-permute-start.4 = (f32[8,128]{1,0:T(8,128)S(1)}, f32[8,128]{1,0:T(8,128)S(1)}, u32[]{:S(2)}, u32[]{:S(2)}) collective-permute-start(f32[8,128]{1,0:T(8,128)S(1)} %slice.62), channel_id=1, source_target_pairs={{8,0},{16,8},{24,16},{32,24},{40,32},{48,40},{56,48},{64,56},{72,6... | collective-permute-start | bytes 12296 | tf_op jit(solution)/shard_map/ppermute | solution.py:20
  104.8 13.4 %all-to-all-start.3 = ((f32[8,48,128]{2,1,0:T(8,128)}), f32[8,48,128]{2,1,0:T(8,128)S(1)}, u32[]{:S(2)}, u32[]{:S(2)}) async-start(f32[8,48,128]{2,1,0:T(8,128)} %broadcast_in_dim.30), calls=%async_computation.3 | async-start | bytes 393216 | tf_op jit(solution)/shard_map/all_to_all | solution.py:340
  118.8 0.6 copy-start.4

commit v2 on v1

--- a/solution.py
+++ b/solution.py
@@ -41,9 +41,16 @@
 
 def start_kernel(group_ref, coeffs_ref, vectors_ref, out_ref, sq_ref):
     step = pl.program_id(0)
-    size = coeffs_ref.shape[0]
-    values = coeffs_ref[...].astype(jnp.float32)
-    sq_ref[pl.ds(pl.multiple_of(step * size, size), size), :] = jnp.sum(values * values, axis=1)
+
+    @pl.when(step == 0)
+    def _():
+        sq_ref[...] = jnp.zeros_like(sq_ref)
+
+    total = sq_ref[...]
+    for k in range(coeffs_ref.shape[0]):
+        values = coeffs_ref[k].astype(jnp.float32)
+        total = total + values * values
+    sq_ref[...] = total
 
     @pl.when(step == pl.num_programs(0) - 1)
     def _():
@@ -58,22 +65,22 @@
 
 
 def start(group_index, coeffs, vectors, group_size):
-    block, freq_local, channels = coeffs.shape
+    freq_local, block, channels = coeffs.shape
     rows = 8 + vectors.shape[1]
-    steps = 4
+    steps = 5
     return pl.pallas_call(
         start_kernel,
         grid_spec=pltpu.PrefetchScalarGridSpec(
             num_scalar_prefetch=1,
             grid=(steps,),
             in_specs=[
-                pl.BlockSpec((block // steps, freq_local, channels), lambda s, g: (s, 0, 0)),
+                pl.BlockSpec((freq_local // steps, block, channels), lambda s, g: (s, 0, 0)),
                 pl.BlockSpec(vectors.shape, lambda s, g: (0, 0)),
             ],
             out_specs=pl.BlockSpec((group_size, rows, block), lambda s, g: (0, 0, 0)),
             scratch_shapes=[pltpu.VMEM((block, channels), jnp.float32)],
         ),
-        out_shape=jax.ShapeDtypeStruct((group_size, rows, block), jnp.float32),
+        out_shape=pltpu.HBM((group_size, rows, block), jnp.float32),
         compiler_params=pltpu.CompilerParams(vmem_limit_bytes=VMEM_LIMIT),
         name="start",
     )(group_index, coeffs, vectors)
@@ -88,42 +95,102 @@
 
 def upper_half(half, block):
     gap = (iota((half, block), 1) - iota((half, block), 0)) & (block - 1)
-    return (gap >= 1) & (gap <= half), gap != 0
-
-
-def cross_kernel(folded, a_ref, b_ref, out_ref):
-    block = a_ref.shape[1]
+    return (gap >= 1) & (gap <= half)
+
+
+def inverse_norm(total, count):
+    block = total.shape[1]
+    eye = iota((block, block), 0) == iota((block, block), 1)
+    column = jnp.sum(jnp.where(eye, total, 0.0), axis=1, keepdims=True)
+    return lax.rsqrt(column / count + epsilon)
+
+
+def normalized(raw, inv_norm):
+    return (raw.astype(jnp.float32) * inv_norm).astype(jnp.bfloat16)
+
+
+def pair_terms(own, other):
+    lhs = jnp.concatenate([own, swapped(own)], axis=0)
+    pair = lax.dot_general(lhs, other, (((1,), (1,)), ((), ())), preferred_element_type=jnp.float32)
+    return pair[: own.shape[0]], pair[own.shape[0] :]
+
+
+def store_terms(out_ref, k, real, imag):
+    parts = out_ref.shape[0]
+    rows = real.shape[0] // parts
+    for d in range(parts):
+        both = jnp.concatenate([real[d * rows : (d + 1) * rows], imag[d * rows : (d + 1) * rows]], axis=0)
+        out_ref[d, k * 2 * rows : (k + 1) * 2 * rows, :] = both.astype(jnp.bfloat16)
+
+
+def cross_own_kernel(count, raw_ref, begun_ref, out_ref, unit_ref, summed_ref, inv_ref):
+    block = raw_ref.shape[1]
     half = block // 2
-    parts = out_ref.shape[0]
-    for k in range(a_ref.shape[0]):
-        a = a_ref[k]
-        lhs = jnp.concatenate([a, swapped(a)], axis=0)
-        pair = lax.dot_general(lhs, b_ref[k], (((1,), (1,)), ((), ())), preferred_element_type=jnp.float32)
-        real, imag = pair[:block], pair[block:]
-        if folded:
-            top, _ = upper_half(half, block)
-            real = jnp.where(top, real[:half], real[half:])
-            imag = jnp.where(top, imag[:half], imag[half:])
-        rows = real.shape[0] // parts
-        for d in range(parts):
-            both = jnp.concatenate([real[d * rows : (d + 1) * rows], imag[d * rows : (d + 1) * rows]], axis=0)
-            out_ref[d, k * 2 * rows : (k + 1) * 2 * rows, :] = both.astype(jnp.bfloat16)
-
-
-def cross(folded, own, other, parts, steps):
-    freq, block, channels = own.shape
-    rows = freq * (block if folded else 2 * block) // parts
-    one = freq // steps
-    spec = pl.BlockSpec((one, block, channels), lambda s: (s, 0, 0))
-    return pl.pallas_call(
-        functools.partial(cross_kernel, folded),
+
+    @pl.when(pl.program_id(0) == 0)
+    def _():
+        summed_ref[...] = jnp.sum(begun_ref[...], axis=0)
+        inv_ref[...] = jnp.broadcast_to(inverse_norm(summed_ref[0:1, :], count), inv_ref.shape)
+
+    inv_norm = inv_ref[...]
+    top = upper_half(half, block)
+    for k in range(raw_ref.shape[0]):
+        unit = normalized(raw_ref[k], inv_norm)
+        unit_ref[k] = unit
+        real, imag = pair_terms(unit, unit)
+        store_terms(out_ref, k, jnp.where(top, real[:half], real[half:]), jnp.where(top, imag[:half], imag[half:]))
+
+
+def cross_own(raw, begun, steps):
+    freq, block, channels = raw.shape
+    parts, sums, _ = begun.shape
+    rows = freq * block // parts
+    spec = pl.BlockSpec((freq // steps, block, channels), lambda s: (s, 0, 0))
+    return pl.pallas_call(
+        functools.partial(cross_own_kernel, freq * parts * channels),
         grid=(steps,),
-        in_specs=[spec, spec],
+        in_specs=[spec, pl.BlockSpec(begun.shape, lambda s: (0, 0, 0))],
+        out_specs=[
+            pl.BlockSpec((parts, rows // steps, block), lambda s: (0, s, 0)),
+            spec,
+            pl.BlockSpec((sums, block), lambda s: (0, 0)),
+        ],
+        out_shape=[
+            pltpu.HBM((parts, rows, block), jnp.bfloat16),
+            pltpu.HBM(raw.shape, jnp.bfloat16),
+            jax.ShapeDtypeStruct((sums, block), jnp.float32),
+        ],
+        scratch_shapes=[pltpu.VMEM((block, channels), jnp.float32)],
+        compiler_params=pltpu.CompilerParams(vmem_limit_bytes=VMEM_LIMIT),
+        name="cross_own",
+    )(raw, begun)
+
+
+def cross_next_kernel(count, unit_ref, raw_ref, summed_ref, out_ref, inv_ref):
+    @pl.when(pl.program_id(0) == 0)
+    def _():
+        inv_ref[...] = jnp.broadcast_to(inverse_norm(summed_ref[0:1, :], count), inv_ref.shape)
+
+    inv_norm = inv_ref[...]
+    for k in range(raw_ref.shape[0]):
+        real, imag = pair_terms(unit_ref[k], normalized(raw_ref[k], inv_norm))
+        store_terms(out_ref, k, real, imag)
+
+
+def cross_next(unit, raw, summed, parts, steps):
+    freq, block, channels = raw.shape
+    rows = freq * 2 * block // parts
+    spec = pl.BlockSpec((freq // steps, block, channels), lambda s: (s, 0, 0))
+    return pl.pallas_call(
+        functools.partial(cross_next_kernel, freq * parts * channels),
+        grid=(steps,),
+        in_specs=[spec, spec, pl.BlockSpec(summed.shape, lambda s: (0, 0))],
         out_specs=pl.BlockSpec((parts, rows // steps, block), lambda s: (0, s, 0)),
-        out_shape=jax.ShapeDtypeStruct((parts, rows, block), jnp.bfloat16),
-        compiler_params=pltpu.CompilerParams(vmem_limit_bytes=VMEM_LIMIT),
-        name="cross_own" if folded else "cross_next",
-    )(own, other)
+        out_shape=pltpu.HBM((parts, rows, block), jnp.bfloat16),
+        scratch_shapes=[pltpu.VMEM((block, channels), jnp.float32)],
+        compiler_params=pltpu.CompilerParams(vmem_limit_bytes=VMEM_LIMIT),
+        name="cross_next",
+    )(unit, raw, summed)
 
 
 def affinities(terms_ref, trig_ref, held_ref, rows, factor):
@@ -148,9 +215,12 @@
     return out
 
 
-def own_kernel(factor, group_ref, terms_ref, trig_ref, out_ref, held_ref):
+def own_kernel(factor, group_ref, far_ref, trig_ref, out_ref, held_ref, terms_ref, sem):
     rows = 8
     block = terms_ref.shape[1]
+    fetch = pltpu.make_async_copy(far_ref, terms_ref, sem)
+    fetch.start()
+    fetch.wait()
     means = affinities(terms_ref, trig_ref, held_ref, rows, factor)
     for i in range(rows):
         out_ref[i : i + 1, :] = means[i]
@@ -164,10 +234,18 @@
     block = terms.shape[1]
     return pl.pallas_call(
         functools.partial(own_kernel, factor),
-        in_specs=[pl.BlockSpec(memory_space=pltpu.SMEM)] + [pl.BlockSpec(memory_space=pltpu.VMEM)] * 2,
+        in_specs=[
+            pl.BlockSpec(memory_space=pltpu.SMEM),
+            pl.BlockSpec(memory_space=pltpu.HBM),
+            pl.BlockSpec(memory_space=pltpu.VMEM),
+        ],
         out_specs=pl.BlockSpec(memory_space=pltpu.VMEM),
         out_shape=jax.ShapeDtypeStruct((rows, block), jnp.float32),
-        scratch_shapes=[pltpu.VMEM((trig.shape[1], rows * block), jnp.bfloat16)],
+        scratch_shapes=[
+            pltpu.VMEM((trig.shape[1], rows * block), jnp.bfloat16),
+            pltpu.VMEM(terms.shape, terms.dtype),
+            pltpu.SemaphoreType.DMA,
+        ],
         compiler_params=pltpu.CompilerParams(vmem_limit_bytes=VMEM_LIMIT),
         name="own_part",
     )(group_index, terms, trig)
@@ -216,7 +294,7 @@
     )(group_index, terms, trig, own)
 
 
-def image_kernel(group_ref, parts_ref, vec_ref, out_ref, own_ref, full_ref):
+def image_kernel(group_ref, parts_ref, before_ref, here_ref, after_ref, out_ref, own_ref, full_ref):
     groups, _, block = parts_ref.shape
     half = block // 2
     shares = parts_ref[0, 40:48, :]
@@ -226,14 +304,14 @@
         full_ref[0, 16 * s : 16 * s + 16, :] = parts_ref[s, 0:16, :]
         full_ref[1, 16 * s : 16 * s + 16, :] = parts_ref[s, 16:32, :]
         full_ref[2, 8 * s : 8 * s + 8, :] = parts_ref[s, 32:40, :]
-    top, _ = upper_half(half, block)
+    top = upper_half(half, block)
     own = full_ref[2, 0:half, :]
     full_ref[2, 0:half, :] = jnp.where(top, own, 0.0)
     full_ref[2, half:block, :] = jnp.where(top, 0.0, own)
     inv_root = lax.rsqrt(shares)
-    scaled_before = vec_ref[0] * inv_root[0:1, :]
-    scaled_own = vec_ref[1] * inv_root[1:2, :]
-    scaled_after = vec_ref[2] * inv_root[2:3, :]
+    scaled_before = before_ref[8:, :] * inv_root[0:1, :]
+    scaled_own = here_ref[8:, :] * inv_root[1:2, :]
+    scaled_after = after_ref[8:, :] * inv_root[2:3, :]
     along, across = ((1,), (1,)), ((1,), (0,))
     product = dot(scaled_own, full_ref[2], along) + dot(scaled_own, full_ref[2], across)
     product = product + dot(scaled_after, full_ref[0], along) + dot(scaled_before, full_ref[1], across)
@@ -255,12 +333,12 @@
     own_ref[1] = dot(place, jnp.broadcast_to(root_degree, image.shape), along)
 
 
-def image_part(group_index, parts, vecs, n_blk):
+def image_part(group_index, parts, before, here, after, n_blk):
     groups, _, block = parts.shape
-    count = vecs.shape[1]
+    count = here.shape[0] - 8
     return pl.pallas_call(
         image_kernel,
-        in_specs=[pl.BlockSpec(memory_space=pltpu.SMEM)] + [pl.BlockSpec(memory_space=pltpu.VMEM)] * 2,
+        in_specs=[pl.BlockSpec(memory_space=pltpu.SMEM)] + [pl.BlockSpec(memory_space=pltpu.VMEM)] * 4,
         out_specs=[pl.BlockSpec(memory_space=pltpu.VMEM)] * 2,
         out_shape=[
             jax.ShapeDtypeStruct((n_blk, block), jnp.float32),
@@ -269,7 +347,7 @@
         scratch_shapes=[pltpu.VMEM((3, block, block), jnp.float32)],
         compiler_params=pltpu.CompilerParams(vmem_limit_bytes=VMEM_LIMIT),
         name="image_part",
-    )(group_index, parts, vecs)
+    )(group_index, parts, before, here, after)
 
 
 def final_kernel(total_rows, stats_ref, own_ref, out_ref):
@@ -303,21 +381,14 @@
     factor = sharpness / math.sqrt(angles * channels)
     trig = trig_columns(freq_local, group_size)
 
-    after_raw = passed_along(coeffs, "blk", -1)
-    begun = start(group_index, coeffs, vectors, group_size)
-    summed = jnp.sum(lax.all_to_all(begun, "grp", 0, 0, tiled=True), axis=0)
+    by_freq = coeffs.transpose(1, 0, 2)
+    after_raw = passed_along(by_freq, "blk", -1)
+    begun = lax.all_to_all(start(group_index, by_freq, vectors, group_size), "grp", 0, 0, tiled=True)
+    own_terms, own_unit, summed = cross_own(by_freq, begun, 5)
+    own_terms = lax.all_to_all(own_terms, "grp", 0, 0, tiled=True).reshape(-1, block)
     summed_after = passed_along(summed, "blk", -1)
     summed_before = passed_along(summed, "blk", 1)
-
-    def unit(raw, sums):
-        inv_norm = lax.rsqrt(sums[0] / (angles * channels) + epsilon)
-        return (raw.astype(jnp.float32) * inv_norm[:, None, None]).astype(jnp.bfloat16).transpose(1, 0, 2)
-
-    own_unit = unit(coeffs, summed)
-    own_terms = cross(True, own_unit, own_unit, group_size, 5)
-    own_terms = lax.all_to_all(own_terms, "grp", 0, 0, tiled=True).reshape(-1, block)
-    after_unit = unit(after_raw, summed_after)
-    next_terms = cross(False, own_unit, after_unit, group_size, 5)
+    next_terms = cross_next(own_unit, after_raw, summed_after, group_size, 5)
     next_terms = lax.all_to_all(next_terms, "grp", 0, 0, tiled=True).reshape(-1, block)
     own_aff = own_part(group_index, own_terms, trig, factor)
     found = next_part(group_index, next_terms, trig, own_aff, factor)
@@ -338,8 +409,7 @@
     sent = jnp.concatenate([found[:16], found_before[:16], own_aff, shares], axis=0)
     sent = jnp.broadcast_to(sent[None], (group_size,) + sent.shape)
     parts = lax.all_to_all(sent, "grp", 0, 0, tiled=True)
-    vecs = jnp.stack([summed_before[8:], summed[8:], summed_after[8:]])
-    stats, own = image_part(group_index, parts, vecs, n_blk)
+    stats, own = image_part(group_index, parts, summed_before, summed, summed_after, n_blk)
     stats = lax.all_to_all(stats, "blk", 0, 0, tiled=True)
     return final_part(stats, own, block * n_blk)
 

time: 143 us -> 151 us (1.056)
  blocking collectives: 21.2 us -> 41.2 us
  waiting for transfers between devices: 60.4 us -> 47.6 us
  other arithmetic: 8.64 us -> 4.89 us
  Pallas kernels: 12 us -> 15.7 us
  starting transfers between devices: 31 us -> 33.3 us
  local copies, waits for them, and re-layouts: 8.85 us -> 7.24 us
    all_to_all x0 -> x1, blocking collectives: none -> 17.2 us  [per_device(): lax.all_to_all(start(group_index, by_freq, vectors, group_size), 'grp', 0...]
    ppermute x6, waiting for transfers between devices: 24.9 us -> 13.9 us  [passed_along(): return lax.ppermute(block, axis, route)]
    all_to_all x1, waiting for transfers between devices: 6.05 us -> 0.01 us  [per_device(): parts = lax.all_to_all(sent, 'grp', 0, 0, tiled=True)]
    all_to_all x1 -> x0, starting transfers between devices: 5.86 us -> none  [per_device(): summed = jnp.sum(lax.all_to_all(begun, 'grp', 0, 0, tiled=True), axis=0)]
    all_to_all x1, waiting for transfers between devices: 0.01 us -> 5.34 us  [per_device(): lax.all_to_all(own_terms, 'grp', 0, 0, tiled=True).reshape(-1, block)]
    all_to_all x1 -> x0, waiting for transfers between devices: 4.37 us -> none  [per_device(): summed = jnp.sum(lax.all_to_all(begun, 'grp', 0, 0, tiled=True), axis=0)]
    ppermute x6, starting transfers between devices: 9.77 us -> 13.7 us  [passed_along(): return lax.ppermute(block, axis, route)]
    all_to_all x1, starting transfers between devices: 7.33 us -> 11.1 us  [per_device(): parts = lax.all_to_all(sent, 'grp', 0, 0, tiled=True)]
  transfers between devices with their start and end apart: 10 -> 9, of which waited for: 5 -> 5; matrix products, arithmetic and copies ran while one was open for 7% -> 3% of each run, Pallas kernels for 6% -> 7%
where the time goes in v2:
time: 151 us; the launch traced here: 150 us
  waiting for transfers between devices  47.6 us (32%)
  blocking collectives  41.2 us (27%)
  starting transfers between devices  33.3 us (22%)
  Pallas kernels  15.7 us (10%)
  local copies, waits for them, and re-layouts  7.24 us (5%)
  other arithmetic  4.89 us (3%)
    all_to_all x1, waiting for transfers between devices, per_device(): lax.all_to_all(next_terms, 'grp', 0, 0, tiled=True).reshape(-1, block)  28.4 us
    all_to_all x1, blocking collectives, per_device(): stats = lax.all_to_all(stats, 'blk', 0, 0, tiled=True)  24 us
    all_to_all x1, blocking collectives, per_device(): lax.all_to_all(start(group_index, by_freq, vectors, group_size), 'grp', 0...  17.2 us
    ppermute x6, waiting for transfers between devices, passed_along(): return lax.ppermute(block, axis, route)  13.9 us
    ppermute x6, starting transfers between devices, passed_along(): return lax.ppermute(block, axis, route)  13.7 us
    all_to_all x1, starting transfers between devices, per_device(): parts = lax.all_to_all(sent, 'grp', 0, 0, tiled=True)  11.1 us
    unnamed x14, local copies, waits for them, and re-layouts  6.53 us
    all_to_all x1, waiting for transfers between devices, per_device(): lax.all_to_all(own_terms, 'grp', 0, 0, tiled=True).reshape(-1, block)  5.34 us
  transfers between devices with their start and end apart: 9, of which 5 were waited for; matrix products, arithmetic and copies ran while one was open for 3% of the time, Pallas kernels for 7%

profile of v2, /device:TPU:1, one launch (start us, length us, event | category | flops | bytes accessed | tf_op | source)
XLA Modules:
  0.0 150.0 jit_solution(752861453587514972)
XLA Ops:
  0.0 3.2 %collective-permute-start = (bf16[45,128,128]{2,1,0:T(8,128)(2,1)}, bf16[45,128,128]{2,1,0:T(8,128)(2,1)S(1)}, u32[]{:S(2)}, u32[]{:S(2)}) collective-permute-start(bf16[45,128,128]{2,1,0:T(8,128)(2,1)} %bitcast.9), channel_id=1, source_target_pairs={{8,0},{16,8},{24,16},{32,24},{40,32},{48,40},{56,48},{64,56},{72,6... | collective-permute-start | bytes 4423688 | tf_op jit(solution)/shard_map/ppermute | solution.py:20
  3.2 0.0 copy-start
  3.2 1.4 copy-done
  4.6 0.0 copy-start.6
  4.6 0.7 copy-done.6
  5.3 0.0 copy-start.1
  5.3 1.3 start.1
  6.6 17.2 %all_to_all.31.begun_ref = f32[8,24,128]{2,1,0:T(8,128)S(1)} all-to-all(f32[8,24,128]{2,1,0:T(8,128)} %start.1), channel_id=1, replica_groups=mesh['blk'=32,'grp'=8] {'grp'}, dimensions={0} | all-to-all | bytes 196608 | tf_op jit(solution)/shard_map/all_to_all | solution.py:386
  23.8 0.0 copy-done.1
  23.8 3.8 %cross_own.1 = (bf16[8,720,128]{2,1,0:T(8,128)(2,1)}, bf16[45,128,128]{2,1,0:T(8,128)(2,1)}, f32[24,128]{1,0:T(8,128)S(1)}) custom-call(bf16[45,128,128]{2,1,0:T(8,128)(2,1)S(1)} %bitcast.11, f32[8,24,128]{2,1,0:T(8,128)S(1)} %all_to_all.31.begun_ref), custom_call_target="tpu_custom_call" | custom-call | tf_op jit(solution)/shard_map/cross_own/pallas_call | solution.py:149
  27.6 4.8 %all-to-all-start.2 = ((bf16[8,720,128]{2,1,0:T(8,128)(2,1)}), bf16[8,720,128]{2,1,0:T(8,128)(2,1)S(1)}, u32[]{:S(2)}, u32[]{:S(2)}) async-start(bf16[8,720,128]{2,1,0:T(8,128)(2,1)} %get-tuple-element.12), calls=%async_computation.2 | async-start | bytes 2949120 | tf_op jit(solution)/shard_map/all_to_all | solution.py:388
  32.4 0.8 collective-permute-start.1
  33.2 9.2 %collective-permute-done.1.summed_ref.after_ref = f32[24,128]{1,0:T(8,128)S(1)} collective-permute-done((f32[24,128]{1,0:T(8,128)S(1)}, f32[24,128]{1,0:T(8,128)S(1)}, u32[]{:S(2)}, u32[]{:S(2)}) %collective-permute-start.1) | collective-permute-done | bytes 12320 | tf_op jit(solution)/shard_map/ppermute | solution.py:20
  42.4 0.0 collective-permute-done.raw_ref
  42.4 0.0 copy-start.4
  42.4 1.4 copy-done.4
  43.8 3.7 %cross_next.1 = bf16[8,1440,128]{2,1,0:T(8,128)(2,1)} custom-call(bf16[45,128,128]{2,1,0:T(8,128)(2,1)S(1)} %copy-done.4, bf16[45,128,128]{2,1,0:T(8,128)(2,1)S(1)} %collective-permute-done.raw_ref, f32[24,128]{1,0:T(8,128)S(1)} %collective-permute-done.1.summed_ref.after_ref), custom_call_target="tpu_custom_call" | custom-call | tf_op jit(solution)/shard_map/cross_next/pallas_call | solution.py:184
  47.5 5.3 %all-to-all-done.2 = bf16[8,720,128]{2,1,0:T(8,128)(2,1)S(1)} async-done(((bf16[8,720,128]{2,1,0:T(8,128)(2,1)}), bf16[8,720,128]{2,1,0:T(8,128)(2,1)S(1)}, u32[]{:S(2)}, u32[]{:S(2)}) %all-to-all-start.2) | async-done | bytes 1474592 | tf_op jit(solution)/shard_map/all_to_all | solution.py:388
  52.8 0.0 copy-start.2
  52.8 1.1 copy-done.2
  53.9 3.6 %all-to-all-start.1 = ((bf16[8,1440,128]{2,1,0:T(8,128)(2,1)}), bf16[8,1440,128]{2,1,0:T(8,128)(2,1)S(1)}, u32[]{:S(2)}, u32[]{:S(2)}) async-start(bf16[8,1440,128]{2,1,0:T(8,128)(2,1)} %cross_next.1), calls=%async_computation.1 | async-start | bytes 5898240 | tf_op jit(solution)/shard_map/all_to_all | solution.py:392
  57.6 4.9 %fusion.5.trig_ref = bf16[360,720]{1,0:T(8,128)(2,1)S(1)} fusion(s32[720]{0:T(1024)S(1)} %add_select_fusion.1, pred[720]{0:T(1024)(128)(4,1)S(1)} %fusion.6), kind=kLoop, calls=%fused_computation.9 | loop fusion | flops 3369600 | bytes 522000 | tf_op jit(solution)/shard_map/jit(_where)/select_n | solution.py:31
  62.5 0.0 copy-start.3
  62.5 1.4 copy-done.3
  63.8 1.5 own_part.1.own_ref
  65.3 28.4 %all-to-all-done.1 = bf16[8,1440,128]{2,1,0:T(8,128)(2,1)S(1)} async-done(((bf16[8,1440,128]{2,1,0:T(8,128)(2,1)}), bf16[8,1440,128]{2,1,0:T(8,128)(2,1)S(1)}, u32[]{:S(2)}, u32[]{:S(2)}) %all-to-all-start.1) | async-done | bytes 2949152 | tf_op jit(solution)/shard_map/all_to_all | solution.py:392
  93.7 3.3 %next_part.1 = f32[24,128]{1,0:T(8,128)S(1)} custom-call(s32[1]{0:T(128)} %bitcast.group_ref, bf16[11520,128]{1,0:T(8,128)(2,1)S(1)} %bitcast.8, bf16[360,720]{1,0:T(8,128)(2,1)S(1)} %fusion.5.trig_ref, f32[8,128]{1,0:T(8,128)S(1)} %own_part.1.own_ref), custom_call_target="tpu_custom_call" | custom-call | tf_op jit(solution)/shard_map/next_part/pallas_call | solution.py:283
  97.0 0.0 collective-permute-start.2
  97.0 0.9 collective-permute-start.4
  97.9 4.2 %collective-permute-start.3 = (f32[8,128]{1,0:T(8,128)S(1)}, f32[8,128]{1,0:T(8,128)S(1)}, u32[]{:S(2)}, u32[]{:S(2)}) collective-permute-start(f32[8,128]{1,0:T(8,128)S(1)} %slice.40), channel_id=1, source_target_pairs={{240,0},{248,8},{0,16},{8,24},{16,32},{24,40},{32,48},{40,56},{48,... | collective-permute-start | bytes 12296 | tf_op jit(solution)/shard_map/ppermute | solution.py:20
  102.1 0.0 collective-permute-done.2
  102.1 0.0 collective-permute-done.4
  102.1 2.1 %collective-permute-done.3 = f32[8,128]{1,0:T(8,128)S(1)} collective-permute-done((f32[8,128]{1,0:T(8,128)S(1)}, f32[8,128]{1,0:T(8,128)S(1)}, u32[]{:S(2)}, u32[]{:S(2)}) %collective-permute-start.3) | collective-permute-done | bytes 4128 | tf_op jit(solution)/shard_map/ppermute | solution.py:20
  104.3 0.7 broadcast_in_dim.28
  104.9 11.1 %all-to-all-start.3 = ((f32[8,48,128]{2,1,0:T(8,128)}), f32[8,48,128]{2,1,0:T(8,128)S(1)}, u32[]{:S(2)}, u32[]{:S(2)}) async-start(f32[8,48,128]{2,1,0:T(8,128)} %broadcast_in_dim.28), calls=%async_computation.3 | async-start | bytes 393216 | tf_op jit(solution)/shard_map/all_to_all | solution.py:411
  116.1 4.6 %collective-permute-start.5 = (f32[24,128]{1,0:T(8,128)S(1)}, f32[24,128]{1,0:T(8,128)S(1)}, u32[]{:S(2)}, u32[]{:S(2)}) collective-permute-start(f32[24,128]{1,0:T(8,128)S(1)} %get-tuple-element.11.here_ref), channel_id=1, source_target_pairs={{248,0},{0,8},{8,16},{16,24},{24,32},{32,40},{40,48},{48,56},{56,6... | collective-permute-start | bytes 36872 | tf_op jit(solution)/shard_map/ppermute | solution.py:20
  120.7 2.6 %collective-permute-done.5.before_ref = f32[24,128]{1,0:T(8,128)S(1)} collective-permute-done((f32[24,128]{1,0:T(8,128)S(1)}, f32[24,128]{1,0:T(8,128)S(1)}, u32[]{:S(2)}, u32[]{:S(2)}) %collective-permute-start.5) | collective-permute-done | bytes 12320 | tf_op jit(solution)/shard_map/ppermute | solution.py:20
  123.3 0.0 all-to-all-done.3.parts_ref
  123.3 0.6 image_part.1
  123.9 0.0 copy-start.5
  123.9 0.6 copy-done.5
  124.5 24.0 %all_to_all.32 = f32[32,1,128]{2,1,0:T(1,128)} all-to-all(f32[32,1,128]{2,1,0:T(1,128)S(1)} %bitcast.13), channel_id=1, replica_groups=mesh['blk'=32,'grp'=8] {'blk'}, dimensions={0} | all-to-all | bytes 32768 | tf_op jit(solution)/shard_map/all_to_all | solution.py:413
  148.5 1.6 %final_part.1 = f32[16,16]{1,0:T(8,128)} custom-call(f32[32,128]{1,0:T(8,128)} %bitcast.14, f32[2,16,16]{2,1,0:T(8,128)} %copy-done.5), custom_call_target="tpu_custom_call" | custom-call | tf_op jit(solution)/shard_map/final_part/pallas_call | solution.py:366
  (8 shorter events, 0.0 us)
Async XLA Ops:
  0.0 42.4 %collective-permute-start = (bf16[45,128,128]{2,1,0:T(8,128)(2,1)}, bf16[45,128,128]{2,1,0:T(8,128)(2,1)S(1)}, u32[]{:S(2)}, u32[]{:S(2)}) collective-permute-start(bf16[45,128,128]{2,1,0:T(8,128)(2,1)} %bitcast.9), channel_id=1, source_target_pairs={{8,0},{16,8},{24,16},{32,24},{40,32},{48,40},{56,48},{64,56},{72,6... | collective-permute-start | bytes 4423688 | tf_op jit(solution)/shard_map/ppermute | solution.py:20
  3.2 1.4 copy-start
  4.6 0.7 copy-start.6
  5.3 18.5 %copy-start.1 = (bf16[128,45,128]{2,0,1:T(8,128)(2,1)S(1)}, bf16[128,45,128]{2,0,1:T(8,128)(2,1)}, u32[]{:S(2)}) copy-start(bf16[128,45,128]{2,0,1:T(8,128)(2,1)} %param.2) | copy-start | bytes 4423684
  27.6 25.2 %all-to-all-start.2 = ((bf16[8,720,128]{2,1,0:T(8,128)(2,1)}), bf16[8,720,128]{2,1,0:T(8,128)(2,1)S(1)}, u32[]{:S(2)}, u32[]{:S(2)}) async-start(bf16[8,720,128]{2,1,0:T(8,128)(2,1)} %get-tuple-element.12), calls=%async_computation.2 | async-start | bytes 2949120 | tf_op jit(solution)/shard_map/all_to_all | solution.py:388
  32.4 10.0 %collective-permute-start.1 = (f32[24,128]{1,0:T(8,128)S(1)}, f32[24,128]{1,0:T(8,128)S(1)}, u32[]{:S(2)}, u32[]{:S(2)}) collective-permute-start(f32[24,128]{1,0:T(8,128)S(1)} %get-tuple-element.11.here_ref), channel_id=1, source_target_pairs={{8,0},{16,8},{24,16},{32,24},{40,32},{48,40},{56,48},{64,56},{72,6... | collective-permute-start | bytes 36872 | tf_op jit(solution)/shard_map/ppermute | solution.py:20
  42.4 1.4 copy-start.4
  52.8 1.1 copy-start.2
  53.9 39.8 %all-to-all-start.1 = ((bf16[8,1440,128]{2,1,0:T(8,128)(2,1)}), bf16[8,1440,128]{2,1,0:T(8,128)(2,1)S(1)}, u32[]{:S(2)}, u32[]{:S(2)}) async-start(bf16[8,1440,128]{2,1,0:T(8,128)(2,1)} %cross_next.1), calls=%async_computation.1 | async-start | bytes 5898240 | tf_op jit(solution)/shard_map/all_to_all | solution.py:392
  62.5 1.4 copy-start.3
  97.0 5.1 %collective-permute-start.2 = (f32[24,128]{1,0:T(8,128)S(1)}, f32[24,128]{1,0:T(8,128)S(1)}, u32[]{:S(2)}, u32[]{:S(2)}) collective-permute-start(f32[24,128]{1,0:T(8,128)S(1)} %next_part.1), channel_id=1, source_target_pairs={{248,0},{0,8},{8,16},{16,24},{24,32},{32,40},{40,48},{48,56},{56,6... | collective-permute-start | bytes 36872 | tf_op jit(solution)/shard_map/ppermute | solution.py:20
  97.0 5.1 %collective-permute-start.4 = (f32[8,128]{1,0:T(8,128)S(1)}, f32[8,128]{1,0:T(8,128)S(1)}, u32[]{:S(2)}, u32[]{:S(2)}) collective-permute-start(f32[8,128]{1,0:T(8,128)S(1)} %slice.40), channel_id=1, source_target_pairs={{8,0},{16,8},{24,16},{32,24},{40,32},{48,40},{56,48},{64,56},{72,6... | collective-permute-start | bytes 12296 | tf_op jit(solution)/shard_map/ppermute | solution.py:20
  97.9 6.3 %collective-permute-start.3 = (f32[8,128]{1,0:T(8,128)S(1)}, f32[8,128]{1,0:T(8,128)S(1)}, u32[]{:S(2)}, u32[]{:S(2)}) collective-permute-start(f32[8,128]{1,0:T(8,128)S(1)} %slice.40), channel_id=1, source_target_pairs={{240,0},{248,8},{0,16},{8,24},{16,32},{24,40},{32,48},{40,56},{48,... | collective-permute-start | bytes 12296 | tf_op jit(solution)/shard_map/ppermute | solution.py:20
  104.9 18.3 %all-to-all-start.3 = ((f32[8,48,128]{2,1,0:T(8,128)}), f32[8,48,128]{2,1,0:T(8,128)S(1)}, u32[]{:S(2)}, u32[]{:S(2)}) async-start(f32[8,48,128]{2,1,0:T(8,128)} %broadcast_in_dim.28), calls=%async_computation.3 | async-start | bytes 393216 | tf_op jit(solution)/shard_map/all_to_all | solution.py:411
  116.1 7.2 %collective-permute-start.5 = (f32[24,128]{1,0:T(8,128)S(1)}, f32[24,128]{1,0:T(8,128)S(1)}, u32[]{:S(2)}, u32[]{:S(2)}) collective-permute-start(f32[24,128]{1,0:T(8,128)S(1)} %get-tuple-element.11.here_ref), channel_id=1, source_target_pairs={{248,0},{0,8},{8,16},{16,24},{24,32},{32,40},{40,48},{48,56},{56,6... | collective-permute-start | bytes 36872 | tf_op jit(solution)/shard_map/ppermute | solution.py:20
  123.9 0.6 copy-start.5

commit v3 on v2

--- a/solution.py
+++ b/solution.py
@@ -20,15 +20,17 @@
     return lax.ppermute(block, axis, route)
 
 
-def trig_columns(freq_local, group_size):
+def trig_columns(freq_local, group_size, group_index):
     total = freq_local * group_size
     row_ids = jnp.arange(2 * total, dtype=jnp.int32)
-    freq = row_ids // 2
+    within = row_ids % (2 * freq_local)
+    source = (group_index + group_size - row_ids // (2 * freq_local)) % group_size
+    freq = source * freq_local + within // 2
     angles = jnp.arange(total, dtype=jnp.int32)
     phase = (angles[:, None] * freq[None, :] % total).astype(jnp.float32) * (2.0 * math.pi / total)
     cos_part = jnp.cos(phase).astype(jnp.bfloat16)
     sin_part = (-jnp.sin(phase)).astype(jnp.bfloat16)
-    return jnp.where((row_ids % 2 == 1)[None, :], sin_part, cos_part)
+    return jnp.where((within % 2 == 1)[None, :], sin_part, cos_part)
 
 
 def iota(shape, dim):
@@ -39,7 +41,7 @@
     return lax.dot_general(a, b, (dims, ((), ())), precision=HIGHEST, preferred_element_type=jnp.float32)
 
 
-def start_kernel(group_ref, coeffs_ref, vectors_ref, out_ref, sq_ref):
+def start_kernel(group_ref, coeffs_ref, vectors_ref, out_ref, same_ref, sq_ref):
     step = pl.program_id(0)
 
     @pl.when(step == 0)
@@ -51,6 +53,7 @@
         values = coeffs_ref[k].astype(jnp.float32)
         total = total + values * values
     sq_ref[...] = total
+    same_ref[...] = coeffs_ref[...]
 
     @pl.when(step == pl.num_programs(0) - 1)
     def _():
@@ -77,10 +80,13 @@
                 pl.BlockSpec((freq_local // steps, block, channels), lambda s, g: (s, 0, 0)),
                 pl.BlockSpec(vectors.shape, lambda s, g: (0, 0)),
             ],
-            out_specs=pl.BlockSpec((group_size, rows, block), lambda s, g: (0, 0, 0)),
+            out_specs=[
+                pl.BlockSpec((group_size, rows, block), lambda s, g: (0, 0, 0)),
+                pl.BlockSpec((freq_local // steps, block, channels), lambda s, g: (s, 0, 0)),
+            ],
             scratch_shapes=[pltpu.VMEM((block, channels), jnp.float32)],
         ),
-        out_shape=pltpu.HBM((group_size, rows, block), jnp.float32),
+        out_shape=[pltpu.HBM((group_size, rows, block), jnp.float32), pltpu.HBM(coeffs.shape, coeffs.dtype)],
         compiler_params=pltpu.CompilerParams(vmem_limit_bytes=VMEM_LIMIT),
         name="start",
     )(group_index, coeffs, vectors)
@@ -123,13 +129,12 @@
         out_ref[d, k * 2 * rows : (k + 1) * 2 * rows, :] = both.astype(jnp.bfloat16)
 
 
-def cross_own_kernel(count, raw_ref, begun_ref, out_ref, unit_ref, summed_ref, inv_ref):
+def cross_own_kernel(count, raw_ref, summed_ref, out_ref, unit_ref, inv_ref):
     block = raw_ref.shape[1]
     half = block // 2
 
     @pl.when(pl.program_id(0) == 0)
     def _():
-        summed_ref[...] = jnp.sum(begun_ref[...], axis=0)
         inv_ref[...] = jnp.broadcast_to(inverse_norm(summed_ref[0:1, :], count), inv_ref.shape)
 
     inv_norm = inv_ref[...]
@@ -141,67 +146,80 @@
         store_terms(out_ref, k, jnp.where(top, real[:half], real[half:]), jnp.where(top, imag[:half], imag[half:]))
 
 
-def cross_own(raw, begun, steps):
+def cross_own(raw, summed, parts, steps):
     freq, block, channels = raw.shape
-    parts, sums, _ = begun.shape
     rows = freq * block // parts
     spec = pl.BlockSpec((freq // steps, block, channels), lambda s: (s, 0, 0))
     return pl.pallas_call(
         functools.partial(cross_own_kernel, freq * parts * channels),
         grid=(steps,),
-        in_specs=[spec, pl.BlockSpec(begun.shape, lambda s: (0, 0, 0))],
-        out_specs=[
-            pl.BlockSpec((parts, rows // steps, block), lambda s: (0, s, 0)),
-            spec,
-            pl.BlockSpec((sums, block), lambda s: (0, 0)),
-        ],
-        out_shape=[
-            pltpu.HBM((parts, rows, block), jnp.bfloat16),
-            pltpu.HBM(raw.shape, jnp.bfloat16),
-            jax.ShapeDtypeStruct((sums, block), jnp.float32),
-        ],
+        in_specs=[spec, pl.BlockSpec(summed.shape, lambda s: (0, 0))],
+        out_specs=[pl.BlockSpec((parts, rows // steps, block), lambda s: (0, s, 0)), spec],
+        out_shape=[pltpu.HBM((parts, rows, block), jnp.bfloat16), pltpu.HBM(raw.shape, jnp.bfloat16)],
         scratch_shapes=[pltpu.VMEM((block, channels), jnp.float32)],
         compiler_params=pltpu.CompilerParams(vmem_limit_bytes=VMEM_LIMIT),
         name="cross_own",
-    )(raw, begun)
-
-
-def cross_next_kernel(count, unit_ref, raw_ref, summed_ref, out_ref, inv_ref):
+    )(raw, summed)
+
+
+def cross_next_kernel(count, group_ref, unit_ref, raw_ref, summed_ref, *refs):
+    *out_refs, inv_ref, terms_ref = refs
+    parts = len(out_refs)
+    rows = raw_ref.shape[1] // parts
+
     @pl.when(pl.program_id(0) == 0)
     def _():
         inv_ref[...] = jnp.broadcast_to(inverse_norm(summed_ref[0:1, :], count), inv_ref.shape)
 
     inv_norm = inv_ref[...]
+    at = [pl.multiple_of(rows * lax.rem(group_ref[0] + r, parts), rows) for r in range(parts)]
     for k in range(raw_ref.shape[0]):
         real, imag = pair_terms(unit_ref[k], normalized(raw_ref[k], inv_norm))
-        store_terms(out_ref, k, real, imag)
-
-
-def cross_next(unit, raw, summed, parts, steps):
+        terms_ref[k, 0] = real
+        terms_ref[k, 1] = imag
+    for k in range(raw_ref.shape[0]):
+        for r in range(parts):
+            for c in range(2):
+                place = slice((2 * k + c) * rows, (2 * k + c + 1) * rows)
+                out_refs[r][place, :] = terms_ref[k, c, pl.ds(at[r], rows), :].astype(jnp.bfloat16)
+
+
+def cross_next(group_index, unit, raw, summed, parts, steps):
     freq, block, channels = raw.shape
     rows = freq * 2 * block // parts
-    spec = pl.BlockSpec((freq // steps, block, channels), lambda s: (s, 0, 0))
+    one = freq // steps
+    spec = pl.BlockSpec((one, block, channels), lambda s, g: (s, 0, 0))
     return pl.pallas_call(
         functools.partial(cross_next_kernel, freq * parts * channels),
-        grid=(steps,),
-        in_specs=[spec, spec, pl.BlockSpec(summed.shape, lambda s: (0, 0))],
-        out_specs=pl.BlockSpec((parts, rows // steps, block), lambda s: (0, s, 0)),
-        out_shape=pltpu.HBM((parts, rows, block), jnp.bfloat16),
-        scratch_shapes=[pltpu.VMEM((block, channels), jnp.float32)],
+        grid_spec=pltpu.PrefetchScalarGridSpec(
+            num_scalar_prefetch=1,
+            grid=(steps,),
+            in_specs=[spec, spec, pl.BlockSpec(summed.shape, lambda s, g: (0, 0))],
+            out_specs=[pl.BlockSpec((rows // steps, block), lambda s, g: (s, 0))] * parts,
+            scratch_shapes=[
+                pltpu.VMEM((block, channels), jnp.float32),
+                pltpu.VMEM((one, 2, block, block), jnp.float32),
+            ],
+        ),
+        out_shape=[pltpu.HBM((rows, block), jnp.bfloat16)] * parts,
         compiler_params=pltpu.CompilerParams(vmem_limit_bytes=VMEM_LIMIT),
         name="cross_next",
-    )(unit, raw, summed)
-
-
-def affinities(terms_ref, trig_ref, held_ref, rows, factor):
+    )(group_index, unit, raw, summed)
+
+
+def affinities(load, pieces, piece_rows, trig_ref, held_ref, rows, width, factor):
     depth = trig_ref.shape[1]
     angles = trig_ref.shape[0]
-    width = terms_ref.shape[1]
     chunk = 16 * rows
     at = iota((chunk, chunk), 0)
     turn = (iota((chunk, chunk), 1) == (at & 15) * rows + (at >> 4)).astype(jnp.bfloat16)
     for c in range(depth // 16):
-        piece = terms_ref[c * chunk : (c + 1) * chunk, :]
+        begin, end = c * chunk, (c + 1) * chunk
+        found = []
+        for p in range(begin // piece_rows, (end - 1) // piece_rows + 1):
+            low, high = max(begin, p * piece_rows), min(end, (p + 1) * piece_rows)
+            found.append(load(p, low - p * piece_rows, high - low))
+        piece = found[0] if len(found) == 1 else jnp.concatenate(found, axis=0)
         turned = jnp.dot(turn, piece, preferred_element_type=jnp.float32).astype(jnp.bfloat16)
         for i in range(rows):
             held_ref[c * 16 : (c + 1) * 16, i * width : (i + 1) * width] = turned[i * 16 : (i + 1) * 16]
@@ -215,13 +233,15 @@
     return out
 
 
-def own_kernel(factor, group_ref, far_ref, trig_ref, out_ref, held_ref, terms_ref, sem):
-    rows = 8
-    block = terms_ref.shape[1]
-    fetch = pltpu.make_async_copy(far_ref, terms_ref, sem)
-    fetch.start()
-    fetch.wait()
-    means = affinities(terms_ref, trig_ref, held_ref, rows, factor)
+def own_kernel(factor, group_ref, terms_ref, trig_ref, out_ref, held_ref):
+    parts, size, block = terms_ref.shape
+    rows = out_ref.shape[0]
+    sources = [lax.rem(group_ref[0] + (parts - p), parts) for p in range(parts)]
+
+    def load(p, begin, count):
+        return terms_ref[sources[p], begin : begin + count, :]
+
+    means = affinities(load, parts, size, trig_ref, held_ref, rows, block, factor)
     for i in range(rows):
         out_ref[i : i + 1, :] = means[i]
     at = iota((rows, block), 0) + rows * group_ref[0]
@@ -230,33 +250,30 @@
 
 
 def own_part(group_index, terms, trig, factor):
-    rows = 8
-    block = terms.shape[1]
+    parts, _, block = terms.shape
+    rows = block // 2 // parts
     return pl.pallas_call(
         functools.partial(own_kernel, factor),
-        in_specs=[
-            pl.BlockSpec(memory_space=pltpu.SMEM),
-            pl.BlockSpec(memory_space=pltpu.HBM),
-            pl.BlockSpec(memory_space=pltpu.VMEM),
-        ],
+        in_specs=[pl.BlockSpec(memory_space=pltpu.SMEM)] + [pl.BlockSpec(memory_space=pltpu.VMEM)] * 2,
         out_specs=pl.BlockSpec(memory_space=pltpu.VMEM),
         out_shape=jax.ShapeDtypeStruct((rows, block), jnp.float32),
-        scratch_shapes=[
-            pltpu.VMEM((trig.shape[1], rows * block), jnp.bfloat16),
-            pltpu.VMEM(terms.shape, terms.dtype),
-            pltpu.SemaphoreType.DMA,
-        ],
+        scratch_shapes=[pltpu.VMEM((trig.shape[1], rows * block), jnp.bfloat16)],
         compiler_params=pltpu.CompilerParams(vmem_limit_bytes=VMEM_LIMIT),
         name="own_part",
     )(group_index, terms, trig)
 
 
-def next_kernel(factor, group_ref, terms_ref, trig_ref, own_ref, out_ref, held_ref, wide_ref):
+def next_kernel(factor, group_ref, trig_ref, own_ref, summed_ref, *refs):
+    *piece_refs, out_ref, held_ref, wide_ref = refs
     rows = 16
-    block = terms_ref.shape[1]
+    size, block = piece_refs[0].shape
     half = block // 2
     group = group_ref[0]
-    means = affinities(terms_ref, trig_ref, held_ref, rows, factor)
+
+    def load(p, begin, count):
+        return piece_refs[p][begin : begin + count, :]
+
+    means = affinities(load, len(piece_refs), size, trig_ref, held_ref, rows, block, factor)
     for i in range(rows):
         out_ref[i : i + 1, :] = means[i]
     own = own_ref[...]
@@ -275,23 +292,25 @@
     out_ref[rows : rows + 8, :] = jnp.zeros((8, block), jnp.float32)
     out_ref[rows : rows + 1, :] = degree
     out_ref[rows + 1 : rows + 2, :] = jnp.sum(out_ref[0:rows, :], axis=0, keepdims=True)
-
-
-def next_part(group_index, terms, trig, own, factor):
+    out_ref[rows + 8 :, :] = summed_ref[8:, :]
+
+
+def next_part(group_index, pieces, trig, own, summed, factor):
     rows = 16
-    block = terms.shape[1]
+    block = pieces[0].shape[1]
     return pl.pallas_call(
         functools.partial(next_kernel, factor),
-        in_specs=[pl.BlockSpec(memory_space=pltpu.SMEM)] + [pl.BlockSpec(memory_space=pltpu.VMEM)] * 3,
+        in_specs=[pl.BlockSpec(memory_space=pltpu.SMEM)]
+        + [pl.BlockSpec(memory_space=pltpu.VMEM)] * (3 + len(pieces)),
         out_specs=pl.BlockSpec(memory_space=pltpu.VMEM),
-        out_shape=jax.ShapeDtypeStruct((rows + 8, block), jnp.float32),
+        out_shape=jax.ShapeDtypeStruct((rows + summed.shape[0], block), jnp.float32),
         scratch_shapes=[
             pltpu.VMEM((trig.shape[1], rows * block), jnp.bfloat16),
             pltpu.VMEM((2 * block, block), jnp.float32),
         ],
         compiler_params=pltpu.CompilerParams(vmem_limit_bytes=VMEM_LIMIT),
         name="next_part",
-    )(group_index, terms, trig, own)
+    )(group_index, trig, own, summed, *pieces)
 
 
 def image_kernel(group_ref, parts_ref, before_ref, here_ref, after_ref, out_ref, own_ref, full_ref):
@@ -309,7 +328,7 @@
     full_ref[2, 0:half, :] = jnp.where(top, own, 0.0)
     full_ref[2, half:block, :] = jnp.where(top, 0.0, own)
     inv_root = lax.rsqrt(shares)
-    scaled_before = before_ref[8:, :] * inv_root[0:1, :]
+    scaled_before = before_ref[24:, :] * inv_root[0:1, :]
     scaled_own = here_ref[8:, :] * inv_root[1:2, :]
     scaled_after = after_ref[8:, :] * inv_root[2:3, :]
     along, across = ((1,), (1,)), ((1,), (0,))
@@ -379,23 +398,22 @@
     group_index = lax.axis_index("grp").astype(jnp.int32)[None]
     angles = freq_local * group_size
     factor = sharpness / math.sqrt(angles * channels)
-    trig = trig_columns(freq_local, group_size)
-
-    by_freq = coeffs.transpose(1, 0, 2)
+    trig = trig_columns(freq_local, group_size, group_index[0])
+
+    begun, by_freq = start(group_index, coeffs.transpose(1, 0, 2), vectors, group_size)
+    summed = jnp.sum(lax.all_to_all(begun, "grp", 0, 0, tiled=True), axis=0)
     after_raw = passed_along(by_freq, "blk", -1)
-    begun = lax.all_to_all(start(group_index, by_freq, vectors, group_size), "grp", 0, 0, tiled=True)
-    own_terms, own_unit, summed = cross_own(by_freq, begun, 5)
-    own_terms = lax.all_to_all(own_terms, "grp", 0, 0, tiled=True).reshape(-1, block)
     summed_after = passed_along(summed, "blk", -1)
-    summed_before = passed_along(summed, "blk", 1)
-    next_terms = cross_next(own_unit, after_raw, summed_after, group_size, 5)
-    next_terms = lax.all_to_all(next_terms, "grp", 0, 0, tiled=True).reshape(-1, block)
+    own_terms, own_unit = cross_own(by_freq, summed, group_size, 5)
+    own_terms = lax.all_to_all(own_terms, "grp", 0, 0, tiled=True)
+    next_terms = cross_next(group_index, own_unit, after_raw, summed_after, group_size, 5)
+    next_terms = [next_terms[0]] + [passed_along(next_terms[r], "grp", r) for r in range(1, group_size)]
     own_aff = own_part(group_index, own_terms, trig, factor)
-    found = next_part(group_index, next_terms, trig, own_aff, factor)
+    found = next_part(group_index, next_terms, trig, own_aff, summed, factor)
 
     found_before = passed_along(found, "blk", 1)
-    edge_after = passed_along(found[16:], "blk", -1)
-    edge_before = passed_along(found[16:], "blk", 2)
+    edge_after = passed_along(found[16:24], "blk", -1)
+    edge_before = passed_along(found[16:24], "blk", 2)
     zeros = jnp.zeros((5, block), jnp.float32)
     shares = jnp.concatenate(
         [
@@ -409,7 +427,7 @@
     sent = jnp.concatenate([found[:16], found_before[:16], own_aff, shares], axis=0)
     sent = jnp.broadcast_to(sent[None], (group_size,) + sent.shape)
     parts = lax.all_to_all(sent, "grp", 0, 0, tiled=True)
-    stats, own = image_part(group_index, parts, summed_before, summed, summed_after, n_blk)
+    stats, own = image_part(group_index, parts, found_before, summed, summed_after, n_blk)
     stats = lax.all_to_all(stats, "blk", 0, 0, tiled=True)
     return final_part(stats, own, block * n_blk)
 

time: 151 us -> 150 us (level)
  blocking collectives: 41.2 us -> 54.9 us
  waiting for transfers between devices: 47.6 us -> 37.8 us
  starting transfers between devices: 33.3 us -> 27.8 us
  Pallas kernels: 15.7 us -> 18.2 us
  local copies, waits for them, and re-layouts: 7.24 us -> 5.46 us
    all_to_all x3 -> x1, waiting for transfers between devices: 33.7 us -> 0.01 us  [per_device(): own_terms = lax.all_to_all(own_terms, 'grp', 0, 0, tiled=True)]
    ppermute x6 -> x12, waiting for transfers between devices: 13.9 us -> 37.8 us  [passed_along(): return lax.ppermute(block, axis, route)]
    all_to_all x3 -> x1, starting transfers between devices: 19.6 us -> 4.82 us  [per_device(): own_terms = lax.all_to_all(own_terms, 'grp', 0, 0, tiled=True)]
    all_to_all x1 -> x2, blocking collectives: 17.2 us -> 29.5 us  [the longest x1 20.6 us: per_device(): summed = jnp.sum(lax.all_to_all(begun, 'grp', 0, 0, tiled=True), axis=0)]
    ppermute x6 -> x12, starting transfers between devices: 13.7 us -> 23 us  [passed_along(): return lax.ppermute(block, axis, route)]
    unnamed x14 -> x12, local copies, waits for them, and re-layouts: 6.53 us -> 5.41 us
    select_n x2 -> x1, other arithmetic: 4.88 us -> 4.87 us  [trig_columns(): return jnp.where((within % 2 == 1)[None, :], sin_part, cos_part)]
  transfers between devices with their start and end apart: 9 -> 13, of which waited for: 5 -> 7; matrix products, arithmetic and copies ran while one was open for 3% -> 3% of each run, Pallas kernels for 7% -> 6%
where the time goes in v3:
time: 150 us; the launch traced here: 149 us
  blocking collectives  54.9 us (37%)
  waiting for transfers between devices  37.8 us (25%)
  starting transfers between devices  27.8 us (19%)
  Pallas kernels  18.2 us (12%)
  local copies, waits for them, and re-layouts  5.46 us (4%)
  other arithmetic  4.93 us (3%)
    ppermute x12, waiting for transfers between devices, passed_along(): return lax.ppermute(block, axis, route)  37.8 us
    all_to_all x1, blocking collectives, per_device(): stats = lax.all_to_all(stats, 'blk', 0, 0, tiled=True)  25.4 us
    ppermute x12, starting transfers between devices, passed_along(): return lax.ppermute(block, axis, route)  23 us
    all_to_all x1, blocking collectives, per_device(): summed = jnp.sum(lax.all_to_all(begun, 'grp', 0, 0, tiled=True), axis=0)  20.6 us
    all_to_all x1, blocking collectives, per_device(): parts = lax.all_to_all(sent, 'grp', 0, 0, tiled=True)  8.9 us
    unnamed x12, local copies, waits for them, and re-layouts  5.41 us
    select_n x1, other arithmetic, trig_columns(): return jnp.where((within % 2 == 1)[None, :], sin_part, cos_part)  4.87 us
    all_to_all x1, starting transfers between devices, per_device(): own_terms = lax.all_to_all(own_terms, 'grp', 0, 0, tiled=True)  4.82 us
  transfers between devices with their start and end apart: 13, of which 7 were waited for; matrix products, arithmetic and copies ran while one was open for 3% of the time, Pallas kernels for 6%

profile of v3, /device:TPU:1, one launch (start us, length us, event | category | flops | bytes accessed | tf_op | source)
XLA Modules:
  0.0 149.3 jit_solution(7023436116125264413)
XLA Ops:
  0.0 0.0 copy-start.1
  0.0 1.4 copy-done.1
  1.4 0.0 copy-start.5
  1.4 0.7 copy-done.5
  2.1 2.6 %start.1 = (f32[8,24,128]{2,1,0:T(8,128)}, bf16[45,128,128]{2,1,0:T(8,128)(2,1)}) custom-call(s32[1]{0:T(128)} %bitcast.group_ref, bf16[45,128,128]{2,1,0:T(8,128)(2,1)S(1)} %bitcast.6, f32[16,16]{1,0:T(8,128)S(1)} %copy-done.5), custom_call_target="tpu_custom_call" | custom-call | tf_op jit(solution)/shard_map/start/pallas_call | solution.py:74
  4.7 3.2 %collective-permute-start = (bf16[45,128,128]{2,1,0:T(8,128)(2,1)}, bf16[45,128,128]{2,1,0:T(8,128)(2,1)S(1)}, u32[]{:S(2)}, u32[]{:S(2)}) collective-permute-start(bf16[45,128,128]{2,1,0:T(8,128)(2,1)} %get-tuple-element.19.raw_ref), channel_id=1, source_target_pairs={{8,0},{16,8},{24,16},{32,24},{40,32},{48,40},{56,48},{64,56},{72,6... | collective-permute-start | bytes 4423688 | tf_op jit(solution)/shard_map/ppermute | solution.py:20
  7.9 20.6 %all_to_all.26 = f32[8,24,128]{2,1,0:T(8,128)S(1)} all-to-all(f32[8,24,128]{2,1,0:T(8,128)} %get-tuple-element.20), channel_id=1, replica_groups=mesh['blk'=32,'grp'=8] {'grp'}, dimensions={0} | all-to-all | bytes 196608 | tf_op jit(solution)/shard_map/all_to_all | solution.py:404
  28.5 0.0 copy-start.2
  28.5 1.4 copy-done.2
  29.9 3.8 %cross_own.1 = (bf16[8,720,128]{2,1,0:T(8,128)(2,1)}, bf16[45,128,128]{2,1,0:T(8,128)(2,1)}) custom-call(bf16[45,128,128]{2,1,0:T(8,128)(2,1)S(1)} %copy-done.2, f32[24,128]{1,0:T(8,128)S(1)} %reduce_sum.9.summed_ref.here_ref), custom_call_target="tpu_custom_call" | custom-call | tf_op jit(solution)/shard_map/cross_own/pallas_call | solution.py:153
  33.7 4.8 %all-to-all-start.1 = ((bf16[8,720,128]{2,1,0:T(8,128)(2,1)}), bf16[8,720,128]{2,1,0:T(8,128)(2,1)S(1)}, u32[]{:S(2)}, u32[]{:S(2)}) async-start(bf16[8,720,128]{2,1,0:T(8,128)(2,1)} %get-tuple-element.21), calls=%async_computation.1 | async-start | bytes 2949120 | tf_op jit(solution)/shard_map/all_to_all | solution.py:408
  38.5 0.8 collective-permute-start.1
  39.3 3.9 %collective-permute-done.1.summed_ref.after_ref = f32[24,128]{1,0:T(8,128)S(1)} collective-permute-done((f32[24,128]{1,0:T(8,128)S(1)}, f32[24,128]{1,0:T(8,128)S(1)}, u32[]{:S(2)}, u32[]{:S(2)}) %collective-permute-start.1) | collective-permute-done | bytes 12320 | tf_op jit(solution)/shard_map/ppermute | solution.py:20
  43.1 0.0 collective-permute-done.raw_ref
  43.1 1.4 copy-done
  44.5 3.8 %cross_next.1 = (bf16[1440,128]{1,0:T(8,128)(2,1)}, bf16[1440,128]{1,0:T(8,128)(2,1)}, bf16[1440,128]{1,0:T(8,128)(2,1)}, bf16[1440,128]{1,0:T(8,128)(2,1)}, bf1...) custom-call(s32[1]{0:T(128)} %bitcast.group_ref, ...), custom_call_target="tpu_custom_call" | custom-call | tf_op jit(solution)/shard_map/cross_next/pallas_call | solution.py:192
  48.3 1.5 collective-permute-start.2
  49.8 6.7 %collective-permute-start.3 = (bf16[1440,128]{1,0:T(8,128)(2,1)}, bf16[1440,128]{1,0:T(8,128)(2,1)S(1)}, u32[]{:S(2)}, u32[]{:S(2)}) collective-permute-start(bf16[1440,128]{1,0:T(8,128)(2,1)} %get-tuple-element.25), channel_id=1, source_target_pairs={{6,0},{7,1},{0,2},{1,3},{2,4},{3,5},{4,6},{5,7},{14,8},{15,9},{8,1... | collective-permute-start | bytes 1105928 | tf_op jit(solution)/shard_map/ppermute | solution.py:20
  56.5 3.1 %collective-permute-start.4 = (bf16[1440,128]{1,0:T(8,128)(2,1)}, bf16[1440,128]{1,0:T(8,128)(2,1)S(1)}, u32[]{:S(2)}, u32[]{:S(2)}) collective-permute-start(bf16[1440,128]{1,0:T(8,128)(2,1)} %get-tuple-element.26), channel_id=1, source_target_pairs={{5,0},{6,1},{7,2},{0,3},{1,4},{2,5},{3,6},{4,7},{13,8},{14,9},{15,... | collective-permute-start | bytes 1105928 | tf_op jit(solution)/shard_map/ppermute | solution.py:20
  59.6 0.0 collective-permute-start.5
  59.6 0.6 collective-permute-start.6
  60.3 6.9 %collective-permute-done.2.refs_1_ = bf16[1440,128]{1,0:T(8,128)(2,1)S(1)} collective-permute-done((bf16[1440,128]{1,0:T(8,128)(2,1)}, bf16[1440,128]{1,0:T(8,128)(2,1)S(1)}, u32[]{:S(2)}, u32[]{:S(2)}) %collective-permute-start.2) | collective-permute-done | bytes 368672 | tf_op jit(solution)/shard_map/ppermute | solution.py:20
  67.2 2.4 %collective-permute-start.7 = (bf16[1440,128]{1,0:T(8,128)(2,1)}, bf16[1440,128]{1,0:T(8,128)(2,1)}, u32[]{:S(2)}, u32[]{:S(2)}) collective-permute-start(bf16[1440,128]{1,0:T(8,128)(2,1)} %get-tuple-element.29), channel_id=1, source_target_pairs={{2,0},{3,1},{4,2},{5,3},{6,4},{7,5},{0,6},{1,7},{10,8},{11,9},{12,... | collective-permute-start | bytes 1105928 | tf_op jit(solution)/shard_map/ppermute | solution.py:20
  69.6 9.4 %collective-permute-done.3.refs_2_ = bf16[1440,128]{1,0:T(8,128)(2,1)S(1)} collective-permute-done((bf16[1440,128]{1,0:T(8,128)(2,1)}, bf16[1440,128]{1,0:T(8,128)(2,1)S(1)}, u32[]{:S(2)}, u32[]{:S(2)}) %collective-permute-start.3) | collective-permute-done | bytes 368672 | tf_op jit(solution)/shard_map/ppermute | solution.py:20
  79.0 0.0 collective-permute-start.8
  79.1 4.9 %fusion.5.trig_ref = bf16[360,720]{1,0:T(8,128)(2,1)S(1)} fusion(s32[720]{0:T(1024)S(1)} %fusion.11, pred[720]{0:T(1024)(128)(4,1)S(1)} %fusion.7), kind=kLoop, calls=%fused_computation.9 | loop fusion | flops 3369600 | bytes 522000 | tf_op jit(solution)/shard_map/jit(_where)/select_n | solution.py:33
  83.9 0.0 copy-start.3
  83.9 0.0 all-to-all-done.1.terms_ref
  84.0 1.2 own_part.1.own_ref
  85.2 0.0 collective-permute-done.4.refs_3_
  85.2 5.9 %collective-permute-done.5.refs_4_ = bf16[1440,128]{1,0:T(8,128)(2,1)} collective-permute-done((bf16[1440,128]{1,0:T(8,128)(2,1)}, bf16[1440,128]{1,0:T(8,128)(2,1)}, u32[]{:S(2)}, u32[]{:S(2)}) %collective-permute-start.5) | collective-permute-done | bytes 368672 | tf_op jit(solution)/shard_map/ppermute | solution.py:20
  91.0 0.0 collective-permute-done.6.refs_5_
  91.0 2.4 %collective-permute-done.7.refs_6_ = bf16[1440,128]{1,0:T(8,128)(2,1)} collective-permute-done((bf16[1440,128]{1,0:T(8,128)(2,1)}, bf16[1440,128]{1,0:T(8,128)(2,1)}, u32[]{:S(2)}, u32[]{:S(2)}) %collective-permute-start.7) | collective-permute-done | bytes 368672 | tf_op jit(solution)/shard_map/ppermute | solution.py:20
  93.4 7.2 %collective-permute-done.8.refs_7_ = bf16[1440,128]{1,0:T(8,128)(2,1)} collective-permute-done((bf16[1440,128]{1,0:T(8,128)(2,1)}, bf16[1440,128]{1,0:T(8,128)(2,1)}, u32[]{:S(2)}, u32[]{:S(2)}) %collective-permute-start.8) | collective-permute-done | bytes 368672 | tf_op jit(solution)/shard_map/ppermute | solution.py:20
  100.6 0.0 copy-done.3
  100.6 4.6 %next_part.1 = f32[40,128]{1,0:T(8,128)S(1)} custom-call(s32[1]{0:T(128)} %bitcast.group_ref, bf16[360,720]{1,0:T(8,128)(2,1)S(1)} %fusion.5.trig_ref, f32[8,128]{1,0:T(8,128)S(1)} %own_part.1.own_ref, f32[24,128]{1,0:T(8,128)S(1)} %reduce_sum.9.summed_ref.here_ref, bf16[1440,128]{1,0:T(8,128)(2,1)S(1)} %copy-done.3, ...), custom_call_target="tpu_custom_call" | custom-call | tf_op jit(solution)/shard_map/next_part/pallas_call | solution.py:301
  105.2 0.0 collective-permute-start.9
  105.2 0.5 collective-permute-start.11
  105.8 4.1 %collective-permute-start.10 = (f32[8,128]{1,0:T(8,128)S(1)}, f32[8,128]{1,0:T(8,128)S(1)}, u32[]{:S(2)}, u32[]{:S(2)}) collective-permute-start(f32[8,128]{1,0:T(8,128)S(1)} %slice.40), channel_id=1, source_target_pairs={{240,0},{248,8},{0,16},{8,24},{16,32},{24,40},{32,48},{40,56},{48,... | collective-permute-start | bytes 12296 | tf_op jit(solution)/shard_map/ppermute | solution.py:20
  109.8 0.0 collective-permute-done.9.before_ref
  109.9 0.0 collective-permute-done.11
  109.9 2.2 %collective-permute-done.10 = f32[8,128]{1,0:T(8,128)S(1)} collective-permute-done((f32[8,128]{1,0:T(8,128)S(1)}, f32[8,128]{1,0:T(8,128)S(1)}, u32[]{:S(2)}, u32[]{:S(2)}) %collective-permute-start.10) | collective-permute-done | bytes 4128 | tf_op jit(solution)/shard_map/ppermute | solution.py:20
  112.1 8.9 %all_to_all.27.parts_ref = f32[8,48,128]{2,1,0:T(8,128)S(1)} all-to-all(f32[8,48,128]{2,1,0:T(8,128)S(1)} %broadcast_in_dim.26), channel_id=1, replica_groups=mesh['blk'=32,'grp'=8] {'grp'}, dimensions={0} | all-to-all | bytes 393216 | tf_op jit(solution)/shard_map/all_to_all | solution.py:429
  121.0 0.6 image_part.1
  121.6 0.0 copy-start.4
  121.7 0.6 copy-done.4
  122.3 25.4 %all_to_all.28 = f32[32,1,128]{2,1,0:T(1,128)} all-to-all(f32[32,1,128]{2,1,0:T(1,128)S(1)} %bitcast.7), channel_id=1, replica_groups=mesh['blk'=32,'grp'=8] {'blk'}, dimensions={0} | all-to-all | bytes 32768 | tf_op jit(solution)/shard_map/all_to_all | solution.py:431
  147.7 1.6 %final_part.1 = f32[16,16]{1,0:T(8,128)} custom-call(f32[32,128]{1,0:T(8,128)} %bitcast.8, f32[2,16,16]{2,1,0:T(8,128)} %copy-done.4), custom_call_target="tpu_custom_call" | custom-call | tf_op jit(solution)/shard_map/final_part/pallas_call | solution.py:385
  (11 shorter events, 0.1 us)
Async XLA Ops:
  0.0 1.4 copy-start.1
  1.4 0.7 copy-start.5
  4.7 38.4 %collective-permute-start = (bf16[45,128,128]{2,1,0:T(8,128)(2,1)}, bf16[45,128,128]{2,1,0:T(8,128)(2,1)S(1)}, u32[]{:S(2)}, u32[]{:S(2)}) collective-permute-start(bf16[45,128,128]{2,1,0:T(8,128)(2,1)} %get-tuple-element.19.raw_ref), channel_id=1, source_target_pairs={{8,0},{16,8},{24,16},{32,24},{40,32},{48,40},{56,48},{64,56},{72,6... | collective-permute-start | bytes 4423688 | tf_op jit(solution)/shard_map/ppermute | solution.py:20
  28.5 1.4 copy-start.2
  33.7 50.3 %all-to-all-start.1 = ((bf16[8,720,128]{2,1,0:T(8,128)(2,1)}), bf16[8,720,128]{2,1,0:T(8,128)(2,1)S(1)}, u32[]{:S(2)}, u32[]{:S(2)}) async-start(bf16[8,720,128]{2,1,0:T(8,128)(2,1)} %get-tuple-element.21), calls=%async_computation.1 | async-start | bytes 2949120 | tf_op jit(solution)/shard_map/all_to_all | solution.py:408
  38.5 4.6 %collective-permute-start.1 = (f32[24,128]{1,0:T(8,128)S(1)}, f32[24,128]{1,0:T(8,128)S(1)}, u32[]{:S(2)}, u32[]{:S(2)}) collective-permute-start(f32[24,128]{1,0:T(8,128)S(1)} %reduce_sum.9.summed_ref.here_ref), channel_id=1, source_target_pairs={{8,0},{16,8},{24,16},{32,24},{40,32},{48,40},{56,48},{64,56},{72,6... | collective-permute-start | bytes 36872 | tf_op jit(solution)/shard_map/ppermute | solution.py:20
  43.1 1.4 copy-start
  48.3 18.9 %collective-permute-start.2 = (bf16[1440,128]{1,0:T(8,128)(2,1)}, bf16[1440,128]{1,0:T(8,128)(2,1)S(1)}, u32[]{:S(2)}, u32[]{:S(2)}) collective-permute-start(bf16[1440,128]{1,0:T(8,128)(2,1)} %get-tuple-element.24), channel_id=1, source_target_pairs={{7,0},{0,1},{1,2},{2,3},{3,4},{4,5},{5,6},{6,7},{15,8},{8,9},{9,10... | collective-permute-start | bytes 1105928 | tf_op jit(solution)/shard_map/ppermute | solution.py:20
  49.8 29.2 %collective-permute-start.3 = (bf16[1440,128]{1,0:T(8,128)(2,1)}, bf16[1440,128]{1,0:T(8,128)(2,1)S(1)}, u32[]{:S(2)}, u32[]{:S(2)}) collective-permute-start(bf16[1440,128]{1,0:T(8,128)(2,1)} %get-tuple-element.25), channel_id=1, source_target_pairs={{6,0},{7,1},{0,2},{1,3},{2,4},{3,5},{4,6},{5,7},{14,8},{15,9},{8,1... | collective-permute-start | bytes 1105928 | tf_op jit(solution)/shard_map/ppermute | solution.py:20
  56.5 28.7 %collective-permute-start.4 = (bf16[1440,128]{1,0:T(8,128)(2,1)}, bf16[1440,128]{1,0:T(8,128)(2,1)S(1)}, u32[]{:S(2)}, u32[]{:S(2)}) collective-permute-start(bf16[1440,128]{1,0:T(8,128)(2,1)} %get-tuple-element.26), channel_id=1, source_target_pairs={{5,0},{6,1},{7,2},{0,3},{1,4},{2,5},{3,6},{4,7},{13,8},{14,9},{15,... | collective-permute-start | bytes 1105928 | tf_op jit(solution)/shard_map/ppermute | solution.py:20
  59.6 31.4 %collective-permute-start.5 = (bf16[1440,128]{1,0:T(8,128)(2,1)}, bf16[1440,128]{1,0:T(8,128)(2,1)}, u32[]{:S(2)}, u32[]{:S(2)}) collective-permute-start(bf16[1440,128]{1,0:T(8,128)(2,1)} %get-tuple-element.27), channel_id=1, source_target_pairs={{4,0},{5,1},{6,2},{7,3},{0,4},{1,5},{2,6},{3,7},{12,8},{13,9},{14,... | collective-permute-start | bytes 1105928 | tf_op jit(solution)/shard_map/ppermute | solution.py:20
  59.6 31.4 %collective-permute-start.6 = (bf16[1440,128]{1,0:T(8,128)(2,1)}, bf16[1440,128]{1,0:T(8,128)(2,1)}, u32[]{:S(2)}, u32[]{:S(2)}) collective-permute-start(bf16[1440,128]{1,0:T(8,128)(2,1)} %get-tuple-element.28), channel_id=1, source_target_pairs={{3,0},{4,1},{5,2},{6,3},{7,4},{0,5},{1,6},{2,7},{11,8},{12,9},{13,... | collective-permute-start | bytes 1105928 | tf_op jit(solution)/shard_map/ppermute | solution.py:20
  67.2 26.2 %collective-permute-start.7 = (bf16[1440,128]{1,0:T(8,128)(2,1)}, bf16[1440,128]{1,0:T(8,128)(2,1)}, u32[]{:S(2)}, u32[]{:S(2)}) collective-permute-start(bf16[1440,128]{1,0:T(8,128)(2,1)} %get-tuple-element.29), channel_id=1, source_target_pairs={{2,0},{3,1},{4,2},{5,3},{6,4},{7,5},{0,6},{1,7},{10,8},{11,9},{12,... | collective-permute-start | bytes 1105928 | tf_op jit(solution)/shard_map/ppermute | solution.py:20
  79.0 21.6 %collective-permute-start.8 = (bf16[1440,128]{1,0:T(8,128)(2,1)}, bf16[1440,128]{1,0:T(8,128)(2,1)}, u32[]{:S(2)}, u32[]{:S(2)}) collective-permute-start(bf16[1440,128]{1,0:T(8,128)(2,1)} %get-tuple-element.30), channel_id=1, source_target_pairs={{1,0},{2,1},{3,2},{4,3},{5,4},{6,5},{7,6},{0,7},{9,8},{10,9},{11,1... | collective-permute-start | bytes 1105928 | tf_op jit(solution)/shard_map/ppermute | solution.py:20
  83.9 16.6 %copy-start.3 = (bf16[1440,128]{1,0:T(8,128)(2,1)S(1)}, bf16[1440,128]{1,0:T(8,128)(2,1)}, u32[]{:S(2)}) copy-start(bf16[1440,128]{1,0:T(8,128)(2,1)} %get-tuple-element.23.refs_0_) | copy-start | bytes 1105924
  105.2 4.6 %collective-permute-start.9 = (f32[40,128]{1,0:T(8,128)S(1)}, f32[40,128]{1,0:T(8,128)S(1)}, u32[]{:S(2)}, u32[]{:S(2)}) collective-permute-start(f32[40,128]{1,0:T(8,128)S(1)} %next_part.1), channel_id=1, source_target_pairs={{248,0},{0,8},{8,16},{16,24},{24,32},{32,40},{40,48},{48,56},{56,6... | collective-permute-start | bytes 61448 | tf_op jit(solution)/shard_map/ppermute | solution.py:20
  105.2 4.6 %collective-permute-start.11 = (f32[8,128]{1,0:T(8,128)S(1)}, f32[8,128]{1,0:T(8,128)S(1)}, u32[]{:S(2)}, u32[]{:S(2)}) collective-permute-start(f32[8,128]{1,0:T(8,128)S(1)} %slice.40), channel_id=1, source_target_pairs={{8,0},{16,8},{24,16},{32,24},{40,32},{48,40},{56,48},{64,56},{72,6... | collective-permute-start | bytes 12296 | tf_op jit(solution)/shard_map/ppermute | solution.py:20
  105.8 6.3 %collective-permute-start.10 = (f32[8,128]{1,0:T(8,128)S(1)}, f32[8,128]{1,0:T(8,128)S(1)}, u32[]{:S(2)}, u32[]{:S(2)}) collective-permute-start(f32[8,128]{1,0:T(8,128)S(1)} %slice.40), channel_id=1, source_target_pairs={{240,0},{248,8},{0,16},{8,24},{16,32},{24,40},{32,48},{40,56},{48,... | collective-permute-start | bytes 12296 | tf_op jit(solution)/shard_map/ppermute | solution.py:20
  121.6 0.6 copy-start.4

commit v4 on v1

v4 whole, which is shorter than its diff:
```python
import functools
import math

import jax
import jax.numpy as jnp
from jax import lax
from jax.experimental import pallas as pl
from jax.experimental.pallas import tpu as pltpu
from jax.sharding import PartitionSpec as P

sharpness = 2.5
epsilon = 1e-06
HIGHEST = lax.Precision.HIGHEST
VMEM_LIMIT = 24 * 1024 * 1024


def passed_along(block, axis, distance):
    devices = range(lax.axis_size(axis))
    route = [((i - distance) % len(devices), i) for i in devices]
    return lax.ppermute(block, axis, route)


def trig_columns(total):
    row_ids = jnp.arange(2 * total, dtype=jnp.int32)
    angles = jnp.arange(total, dtype=jnp.int32)
    phase = (angles[:, None] * (row_ids // 2)[None, :] % total).astype(jnp.float32) * (2.0 * math.pi / total)
    cos_part = jnp.cos(phase).astype(jnp.bfloat16)
    sin_part = (-jnp.sin(phase)).astype(jnp.bfloat16)
    return jnp.where((row_ids % 2 == 1)[None, :], sin_part, cos_part)


def iota(shape, dim):
    return lax.broadcasted_iota(jnp.int32, shape, dim)


def dot(a, b, dims):
    return lax.dot_general(a, b, (dims, ((), ())), precision=HIGHEST, preferred_element_type=jnp.float32)


def start_kernel(group_ref, squares_ref, vectors_ref, out_ref):
    block = squares_ref.shape[1]
    rows = vectors_ref.shape[0]
    total = jnp.broadcast_to(squares_ref[...], (8, block))
    place = iota((rows, block), 1) == iota((rows, block), 0) + rows * group_ref[0]
    placed = dot(vectors_ref[...], place.astype(jnp.float32), ((0,), (0,)))
    for d in range(out_ref.shape[0]):
        out_ref[d, 0:8, :] = total
        out_ref[d, 8 : 8 + placed.shape[0], :] = placed


def start(group_index, squares, vectors, group_size):
    shape = (group_size, 8 + vectors.shape[1], squares.shape[1])
    return pl.pallas_call(
        start_kernel,
        in_specs=[pl.BlockSpec(memory_space=pltpu.SMEM)] + [pl.BlockSpec(memory_space=pltpu.VMEM)] * 2,
        out_specs=pl.BlockSpec(memory_space=pltpu.VMEM),
        out_shape=jax.ShapeDtypeStruct(shape, jnp.float32),
        name="start",
    )(group_index, squares, vectors)


def swapped(a):
    half = a.shape[1] // 2
    wide = a.astype(jnp.float32)
    turned = pltpu.roll(wide, half, 1)
    return jnp.where(iota(a.shape, 1) < half, turned, -turned).astype(a.dtype)


def upper_half(half, block):
    gap = (iota((half, block), 1) - iota((half, block), 0)) & (block - 1)
    return (gap >= 1) & (gap <= half)


def pair_terms(own, other):
    lhs = jnp.concatenate([own, swapped(own)], axis=0)
    pair = lax.dot_general(lhs, other, (((1,), (1,)), ((), ())), preferred_element_type=jnp.float32)
    return pair[: own.shape[0]], pair[own.shape[0] :]


def store_terms(out_ref, k, real, imag):
    parts = out_ref.shape[0]
    rows = real.shape[0] // parts
    for d in range(parts):
        both = jnp.concatenate([real[d * rows : (d + 1) * rows], imag[d * rows : (d + 1) * rows]], axis=0)
        out_ref[d, k * 2 * rows : (k + 1) * 2 * rows, :] = both.astype(jnp.bfloat16)


def cross_kernel(folded, own_ref, other_ref, out_ref):
    block = own_ref.shape[1]
    half = block // 2
    for k in range(own_ref.shape[0]):
        real, imag = pair_terms(own_ref[k], other_ref[k])
        if folded:
            top = upper_half(half, block)
            real = jnp.where(top, real[:half], real[half:])
            imag = jnp.where(top, imag[:half], imag[half:])
        store_terms(out_ref, k, real, imag)


def cross(folded, own, other, parts, steps):
    freq, block, channels = own.shape
    rows = freq * (block if folded else 2 * block) // parts
    spec = pl.BlockSpec((freq // steps, block, channels), lambda s: (s, 0, 0))
    return pl.pallas_call(
        functools.partial(cross_kernel, folded),
        grid=(steps,),
        in_specs=[spec, spec],
        out_specs=pl.BlockSpec((parts, rows // steps, block), lambda s: (0, s, 0)),
        out_shape=pltpu.HBM((parts, rows, block), jnp.bfloat16),
        compiler_params=pltpu.CompilerParams(vmem_limit_bytes=VMEM_LIMIT),
        name="cross_own" if folded else "cross_next",
    )(own, other)


def affinities(load, pieces, piece_rows, trig_ref, held_ref, rows, width, factor):
    depth = trig_ref.shape[1]
    angles = trig_ref.shape[0]
    chunk = 16 * rows
    at = iota((chunk, chunk), 0)
    turn = (iota((chunk, chunk), 1) == (at & 15) * rows + (at >> 4)).astype(jnp.bfloat16)
    for c in range(depth // 16):
        begin, end = c * chunk, (c + 1) * chunk
        found = []
        for p in range(begin // piece_rows, (end - 1) // piece_rows + 1):
            low, high = max(begin, p * piece_rows), min(end, (p + 1) * piece_rows)
            found.append(load(p, low - p * piece_rows, high - low))
        piece = found[0] if len(found) == 1 else jnp.concatenate(found, axis=0)
        turned = jnp.dot(turn, piece, preferred_element_type=jnp.float32).astype(jnp.bfloat16)
        for i in range(rows):
            held_ref[c * 16 : (c + 1) * 16, i * width : (i + 1) * width] = turned[i * 16 : (i + 1) * 16]
    out = []
    for pair in range(rows // 2):
        corr = jnp.dot(
            trig_ref[...], held_ref[:, pair * 2 * width : (pair + 1) * 2 * width], preferred_element_type=jnp.float32
        )
        mean = jnp.sum(jnp.exp(factor * corr), axis=0, keepdims=True) * (1.0 / angles)
        out += [mean[:, :width], mean[:, width:]]
    return out


def own_kernel(factor, group_ref, terms_ref, trig_ref, out_ref, held_ref):
    parts, size, block = terms_ref.shape
    rows = out_ref.shape[0]

    def load(p, begin, count):
        return terms_ref[p, begin : begin + count, :]

    means = affinities(load, parts, size, trig_ref, held_ref, rows, block, factor)
    for i in range(rows):
        out_ref[i : i + 1, :] = means[i]
    at = iota((rows, block), 0) + rows * group_ref[0]
    gap = (iota((rows, block), 1) - at) & (block - 1)
    out_ref[...] = jnp.where(gap == 0, 0.0, out_ref[...])


def own_part(group_index, terms, trig, factor):
    parts, _, block = terms.shape
    rows = block // 2 // parts
    return pl.pallas_call(
        functools.partial(own_kernel, factor),
        in_specs=[pl.BlockSpec(memory_space=pltpu.SMEM)] + [pl.BlockSpec(memory_space=pltpu.VMEM)] * 2,
        out_specs=pl.BlockSpec(memory_space=pltpu.VMEM),
        out_shape=jax.ShapeDtypeStruct((rows, block), jnp.float32),
        scratch_shapes=[pltpu.VMEM((trig.shape[1], rows * block), jnp.bfloat16)],
        compiler_params=pltpu.CompilerParams(vmem_limit_bytes=VMEM_LIMIT),
        name="own_part",
    )(group_index, terms, trig)


def next_kernel(factor, group_ref, terms_ref, trig_ref, own_ref, summed_ref, out_ref, held_ref, wide_ref):
    rows = 16
    parts, size, block = terms_ref.shape
    half = block // 2
    group = group_ref[0]

    def load(p, begin, count):
        return terms_ref[p, begin : begin + count, :]

    means = affinities(load, parts, size, trig_ref, held_ref, rows, block, factor)
    for i in range(rows):
        out_ref[i : i + 1, :] = means[i]
    own = own_ref[...]
    at = iota((8, block), 0) + 8 * group
    gap = (iota((8, block), 1) - at) & (block - 1)
    top = (gap >= 1) & (gap <= half)
    upper, lower = jnp.where(top, own, 0.0), jnp.where(top, 0.0, own)
    wide_ref[...] = jnp.zeros_like(wide_ref)
    wide_ref[pl.ds(pl.multiple_of(rows * group, rows), rows), :] = out_ref[0:rows, :]
    own_at = pl.multiple_of(8 * group, 8)
    wide_ref[pl.ds(block + own_at, 8), :] = upper
    wide_ref[pl.ds(block + half + own_at, 8), :] = lower
    ones = jnp.ones((8, block), jnp.float32)
    by_row = dot(ones, wide_ref[...], ((1,), (1,)))
    degree = by_row[0:1, :block] + by_row[0:1, block:] + jnp.sum(own, axis=0, keepdims=True)
    out_ref[rows : rows + 8, :] = jnp.zeros((8, block), jnp.float32)
    out_ref[rows : rows + 1, :] = degree
    out_ref[rows + 1 : rows + 2, :] = jnp.sum(out_ref[0:rows, :], axis=0, keepdims=True)
    out_ref[rows + 8 :, :] = summed_ref[8:, :]


def next_part(group_index, terms, trig, own, summed, factor):
    rows = 16
    block = terms.shape[2]
    return pl.pallas_call(
        functools.partial(next_kernel, factor),
        in_specs=[pl.BlockSpec(memory_space=pltpu.SMEM)] + [pl.BlockSpec(memory_space=pltpu.VMEM)] * 4,
        out_specs=pl.BlockSpec(memory_space=pltpu.VMEM),
        out_shape=jax.ShapeDtypeStruct((rows + summed.shape[0], block), jnp.float32),
        scratch_shapes=[
            pltpu.VMEM((trig.shape[1], rows * block), jnp.bfloat16),
            pltpu.VMEM((2 * block, block), jnp.float32),
        ],
        compiler_params=pltpu.CompilerParams(vmem_limit_bytes=VMEM_LIMIT),
        name="next_part",
    )(group_index, terms, trig, own, summed)


def image_kernel(group_ref, parts_ref, before_ref, here_ref, after_ref, out_ref, own_ref, full_ref):
    groups, _, block = parts_ref.shape
    half = block // 2
    shares = parts_ref[0, 40:48, :]
    for s in range(groups):
        if s:
            shares = shares + parts_ref[s, 40:48, :]
        full_ref[0, 16 * s : 16 * s + 16, :] = parts_ref[s, 0:16, :]
        full_ref[1, 16 * s : 16 * s + 16, :] = parts_ref[s, 16:32, :]
        full_ref[2, 8 * s : 8 * s + 8, :] = parts_ref[s, 32:40, :]
    top = upper_half(half, block)
    own = full_ref[2, 0:half, :]
    full_ref[2, 0:half, :] = jnp.where(top, own, 0.0)
    full_ref[2, half:block, :] = jnp.where(top, 0.0, own)
    inv_root = lax.rsqrt(shares)
    scaled_before = before_ref[24:, :] * inv_root[0:1, :]
    scaled_own = here_ref[8:, :] * inv_root[1:2, :]
    scaled_after = after_ref[8:, :] * inv_root[2:3, :]
    along, across = ((1,), (1,)), ((1,), (0,))
    product = dot(scaled_own, full_ref[2], along) + dot(scaled_own, full_ref[2], across)
    product = product + dot(scaled_after, full_ref[0], along) + dot(scaled_before, full_ref[1], across)
    image = product * inv_root[1:2, :] * (3.0 * block)
    degree = shares[1:2, :]
    root_degree = jnp.sqrt(degree)
    degree_sum = jnp.sum(degree, axis=1, keepdims=True)
    proj = jnp.sum(root_degree * image, axis=1, keepdims=True)
    rest = image - root_degree * (proj / degree_sum)
    rest_sq = jnp.sum(rest * rest, axis=1, keepdims=True)
    count = image.shape[0]
    at, lane = iota((count, block), 0), iota((count, block), 1)
    stats = jnp.where(lane == at, proj, 0.0) + jnp.where(lane == at + count, rest_sq, 0.0)
    stats = jnp.sum(stats, axis=0, keepdims=True)
    stats = jnp.where(iota((1, block), 1) == 2 * count, degree_sum, stats)
    out_ref[...] = jnp.broadcast_to(stats, out_ref.shape)
    place = (lane == at + count * group_ref[0]).astype(jnp.float32)
    own_ref[0] = dot(place, image, along)
    own_ref[1] = dot(place, jnp.broadcast_to(root_degree, image.shape), along)


def image_part(group_index, parts, before, here, after, n_blk):
    groups, _, block = parts.shape
    count = here.shape[0] - 8
    return pl.pallas_call(
        image_kernel,
        in_specs=[pl.BlockSpec(memory_space=pltpu.SMEM)] + [pl.BlockSpec(memory_space=pltpu.VMEM)] * 4,
        out_specs=[pl.BlockSpec(memory_space=pltpu.VMEM)] * 2,
        out_shape=[
            jax.ShapeDtypeStruct((n_blk, block), jnp.float32),
            jax.ShapeDtypeStruct((2, count, count), jnp.float32),
        ],
        scratch_shapes=[pltpu.VMEM((3, block, block), jnp.float32)],
        compiler_params=pltpu.CompilerParams(vmem_limit_bytes=VMEM_LIMIT),
        name="image_part",
    )(group_index, parts, before, here, after)


def final_kernel(total_rows, stats_ref, own_ref, out_ref):
    count = out_ref.shape[1]
    stats = stats_ref[...]
    proj, rest_sq, degree = stats[:, :count], stats[:, count : 2 * count], stats[:, 2 * count : 2 * count + 1]
    ratio = jnp.sum(proj, axis=0, keepdims=True) / jnp.sum(degree, axis=0, keepdims=True)
    shift = proj / degree - ratio
    column_sq = jnp.sum(rest_sq + degree * (shift * shift), axis=0, keepdims=True)
    deflated = own_ref[0] - own_ref[1] * ratio
    out_ref[...] = deflated * lax.rsqrt(column_sq / total_rows + epsilon)


def final_part(stats, own, total_rows):
    count = own.shape[1]
    return pl.pallas_call(
        functools.partial(final_kernel, total_rows),
        in_specs=[pl.BlockSpec(memory_space=pltpu.VMEM)] * 2,
        out_specs=pl.BlockSpec(memory_space=pltpu.VMEM),
        out_shape=jax.ShapeDtypeStruct((count, count), jnp.float32),
        name="final_part",
    )(stats, own)


def per_device(coeffs, vectors):
    block, freq_local, channels = coeffs.shape
    group_size = lax.axis_size("grp")
    n_blk = lax.axis_size("blk")
    group_index = lax.axis_index("grp").astype(jnp.int32)[None]
    angles = freq_local * group_size
    factor = sharpness / math.sqrt(angles * channels)
    trig = trig_columns(angles)

    squares = jnp.einsum("ikc,ikc->i", coeffs, coeffs, preferred_element_type=jnp.float32)
    begun = start(group_index, squares[None], vectors, group_size)
    summed = jnp.sum(lax.all_to_all(begun, "grp", 0, 0, tiled=True), axis=0)
    inv_norm = lax.rsqrt(summed[0] / (angles * channels) + epsilon)
    own_unit = (coeffs.astype(jnp.float32) * inv_norm[:, None, None]).astype(jnp.bfloat16).transpose(1, 0, 2)
    after_unit = passed_along(own_unit, "blk", -1)
    own_terms = cross(True, own_unit, own_unit, group_size, 5)
    own_terms = lax.all_to_all(own_terms, "grp", 0, 0, tiled=True)
    next_terms = cross(False, own_unit, after_unit, group_size, 5)
    next_terms = lax.all_to_all(next_terms, "grp", 0, 0, tiled=True)
    own_aff = own_part(group_index, own_terms, trig, factor)
    found = next_part(group_index, next_terms, trig, own_aff, summed, factor)

    found_before = passed_along(found, "blk", 1)
    edge_after = passed_along(found[16:], "blk", -1)
    edge_before = passed_along(found[16:24], "blk", 2)
    zeros = jnp.zeros((5, block), jnp.float32)
    shares = jnp.concatenate(
        [
            found_before[16:17] + edge_before[1:2],
            found[16:17] + found_before[17:18],
            edge_after[0:1] + found[17:18],
            zeros,
        ],
        axis=0,
    )
    sent = jnp.concatenate([found[:16], found_before[:16], own_aff, shares], axis=0)
    sent = jnp.broadcast_to(sent[None], (group_size,) + sent.shape)
    parts = lax.all_to_all(sent, "grp", 0, 0, tiled=True)
    stats, own = image_part(group_index, parts, found_before, summed, edge_after, n_blk)
    stats = lax.all_to_all(stats, "blk", 0, 0, tiled=True)
    return final_part(stats, own, block * n_blk)


def solution(mesh):
    placed = (P("blk", "grp", None), P(("blk", "grp"), None))
    return jax.shard_map(
        per_device, mesh=mesh, in_specs=placed, out_specs=P(("blk", "grp"), None), check_vma=False
    )
```

time: 143 us -> 151 us (1.056)
  blocking collectives: 21.2 us -> 50.6 us
  starting transfers between devices: 31 us -> 10.7 us
  local copies, waits for them, and re-layouts: 8.85 us -> 3.14 us
  Pallas kernels: 12 us -> 16.9 us
    all_to_all x0 -> x2, blocking collectives: none -> 29.3 us  [the longest x1 18.1 us: per_device(): parts = lax.all_to_all(sent, 'grp', 0, 0, tiled=True)]
    all_to_all x4 -> x2, starting transfers between devices: 21.2 us -> 7.22 us  [the longest x1 3.64 us: per_device(): next_terms = lax.all_to_all(next_terms, 'grp', 0, 0, tiled=True)]
    ppermute x6 -> x4, waiting for transfers between devices: 24.9 us -> 32.4 us  [passed_along(): return lax.ppermute(block, axis, route)]
    all_to_all x4 -> x2, waiting for transfers between devices: 35.5 us -> 29 us  [the longest x1 29 us: per_device(): next_terms = lax.all_to_all(next_terms, 'grp', 0, 0, tiled=True)]
    ppermute x6 -> x4, starting transfers between devices: 9.77 us -> 3.52 us  [passed_along(): return lax.ppermute(block, axis, route)]
    unnamed x13 -> x8, local copies, waits for them, and re-layouts: 8.12 us -> 3.09 us
    pallas_call x2, Pallas kernels: 3.99 us -> 8.61 us  [cross(): pl.pallas_call(functools.partial(cross_kernel, folded), grid=(steps,), in...]
    transpose x2 -> x1, other arithmetic: 3.72 us -> 0.5 us  [per_device(): (coeffs.astype(jnp.float32) * inv_norm[:, None, None]).astype(jnp.bfloat16)]
  transfers between devices with their start and end apart: 10 -> 6, of which waited for: 5 -> 4; matrix products, arithmetic and copies ran while one was open for 7% -> 3% of each run, Pallas kernels for 6% -> 7%
where the time goes in v4:
time: 151 us
  waiting for transfers between devices  61.4 us (41%)
  blocking collectives  50.6 us (34%)
  Pallas kernels  16.9 us (11%)
  starting transfers between devices  10.7 us (7%)
  other arithmetic  7.82 us (5%)
  local copies, waits for them, and re-layouts  3.14 us (2%)
    ppermute x4, waiting for transfers between devices, passed_along(): return lax.ppermute(block, axis, route)  32.4 us
    all_to_all x1, waiting for transfers between devices, per_device(): next_terms = lax.all_to_all(next_terms, 'grp', 0, 0, tiled=True)  29 us
    all_to_all x1, blocking collectives, per_device(): stats = lax.all_to_all(stats, 'blk', 0, 0, tiled=True)  21.3 us
    all_to_all x1, blocking collectives, per_device(): parts = lax.all_to_all(sent, 'grp', 0, 0, tiled=True)  18.1 us
    all_to_all x1, blocking collectives, per_device(): summed = jnp.sum(lax.all_to_all(begun, 'grp', 0, 0, tiled=True), axis=0)  11.2 us
    pallas_call x2, Pallas kernels, cross(): pl.pallas_call(functools.partial(cross_kernel, folded), grid=(steps,), in...  8.61 us
    select_n x1, other arithmetic, trig_columns(): return jnp.where((row_ids % 2 == 1)[None, :], sin_part, cos_part)  4.87 us
    all_to_all x1, starting transfers between devices, per_device(): next_terms = lax.all_to_all(next_terms, 'grp', 0, 0, tiled=True)  3.64 us
  transfers between devices with their start and end apart: 6, of which 4 were waited for; matrix products, arithmetic and copies ran while one was open for 3% of the time, Pallas kernels for 7%

profile of v4, /device:TPU:1, one launch (start us, length us, event | category | flops | bytes accessed | tf_op | source)
XLA Modules:
  0.0 150.7 jit_solution(10679562819839918623)
XLA Ops:
  0.0 0.0 copy-start.3
  0.0 2.4 %fusion = f32[128]{0:T(128)} fusion(bf16[128,45,128]{2,0,1:T(8,128)(2,1)} %param.2), kind=kLoop, calls=%fused_computation.1 | loop fusion | flops 2211712 | bytes 1475072 | tf_op jit(solution)/shard_map/ikc,ikc->i/dot_general | solution.py:305
  2.4 1.5 %start.1 = f32[8,24,128]{2,1,0:T(8,128)} custom-call(s32[1]{0:T(128)} %bitcast.2.group_ref, f32[1,128]{1,0:T(1,128)} %bitcast.15, f32[16,16]{1,0:T(8,128)} %vectors_ref.1), custom_call_target="tpu_custom_call" | custom-call | tf_op jit(solution)/shard_map/start/pallas_call | solution.py:53
  4.0 11.2 %all_to_all.31 = f32[8,24,128]{2,1,0:T(8,128)S(1)} all-to-all(f32[8,24,128]{2,1,0:T(8,128)} %start.1), channel_id=1, replica_groups=mesh['blk'=32,'grp'=8] {'grp'}, dimensions={0} | all-to-all | bytes 196608 | tf_op jit(solution)/shard_map/all_to_all | solution.py:307
  15.2 0.0 copy-done.3
  15.2 0.5 fusion.1.own_ref.other_ref
  15.7 2.1 %collective-permute-start = (bf16[45,128,128]{2,1,0:T(8,128)(2,1)S(1)}, bf16[45,128,128]{2,1,0:T(8,128)(2,1)}, u32[]{:S(2)}, u32[]{:S(2)}) collective-permute-start(bf16[45,128,128]{2,1,0:T(8,128)(2,1)S(1)} %fusion.1.own_ref.other_ref), channel_id=1, source_target_pairs={{8,0},{16,8},{24,16},{32,24},{40,32},{48,40},{56,48},{64,56},{72,6... | collective-permute-start | bytes 4423688 | tf_op jit(solution)/shard_map/ppermute | solution.py:20
  17.8 3.3 %cross_own.1 = bf16[8,720,128]{2,1,0:T(8,128)(2,1)} custom-call(bf16[45,128,128]{2,1,0:T(8,128)(2,1)S(1)} %fusion.1.own_ref.other_ref, bf16[45,128,128]{2,1,0:T(8,128)(2,1)S(1)} %fusion.1.own_ref.other_ref), custom_call_target="tpu_custom_call" | custom-call | tf_op jit(solution)/shard_map/cross_own/pallas_call | solution.py:104
  21.1 3.6 %all-to-all-start.2 = ((bf16[8,720,128]{2,1,0:T(8,128)(2,1)}), bf16[8,720,128]{2,1,0:T(8,128)(2,1)S(1)}, u32[]{:S(2)}, u32[]{:S(2)}) async-start(bf16[8,720,128]{2,1,0:T(8,128)(2,1)} %cross_own.1), calls=%async_computation.2 | async-start | bytes 2949120 | tf_op jit(solution)/shard_map/all_to_all | solution.py:312
  24.7 26.6 %collective-permute-done.other_ref = bf16[45,128,128]{2,1,0:T(8,128)(2,1)} collective-permute-done((bf16[45,128,128]{2,1,0:T(8,128)(2,1)S(1)}, bf16[45,128,128]{2,1,0:T(8,128)(2,1)}, u32[]{:S(2)}, u32[]{:S(2)}) %collective-permute-start) | collective-permute-done | bytes 1474592 | tf_op jit(solution)/shard_map/ppermute | solution.py:20
  51.3 5.3 %cross_next.1 = bf16[8,1440,128]{2,1,0:T(8,128)(2,1)} custom-call(bf16[45,128,128]{2,1,0:T(8,128)(2,1)S(1)} %fusion.1.own_ref.other_ref, bf16[45,128,128]{2,1,0:T(8,128)(2,1)} %collective-permute-done.other_ref), custom_call_target="tpu_custom_call" | custom-call | tf_op jit(solution)/shard_map/cross_next/pallas_call | solution.py:104
  56.6 0.0 all-to-all-done.2.terms_ref
  56.6 0.0 copy-start
  56.6 1.1 copy-done
  57.7 3.6 %all-to-all-start.1 = ((bf16[8,1440,128]{2,1,0:T(8,128)(2,1)}), bf16[8,1440,128]{2,1,0:T(8,128)(2,1)S(1)}, u32[]{:S(2)}, u32[]{:S(2)}) async-start(bf16[8,1440,128]{2,1,0:T(8,128)(2,1)} %cross_next.1), calls=%async_computation.1 | async-start | bytes 5898240 | tf_op jit(solution)/shard_map/all_to_all | solution.py:314
  61.4 4.9 %fusion.7.trig_ref = bf16[360,720]{1,0:T(8,128)(2,1)S(1)} fusion(s32[720]{0:T(1024)S(1)} %add_select_fusion.1, pred[720]{0:T(1024)(128)(4,1)S(1)} %fusion.8), kind=kLoop, calls=%fused_computation.13 | loop fusion | flops 3369600 | bytes 522000 | tf_op jit(solution)/shard_map/jit(_where)/select_n | solution.py:29
  66.3 0.0 copy-start.1
  66.3 1.4 copy-done.1
  67.7 1.2 own_part.1.own_ref
  68.9 29.0 %all-to-all-done.1.terms_ref = bf16[8,1440,128]{2,1,0:T(8,128)(2,1)S(1)} async-done(((bf16[8,1440,128]{2,1,0:T(8,128)(2,1)}), bf16[8,1440,128]{2,1,0:T(8,128)(2,1)S(1)}, u32[]{:S(2)}, u32[]{:S(2)}) %all-to-all-start.1) | async-done | bytes 2949152 | tf_op jit(solution)/shard_map/all_to_all | solution.py:314
  97.9 3.3 %next_part.1 = f32[40,128]{1,0:T(8,128)S(1)} custom-call(s32[1]{0:T(128)} %bitcast.2.group_ref, bf16[8,1440,128]{2,1,0:T(8,128)(2,1)S(1)} %all-to-all-done.1.terms_ref, bf16[360,720]{1,0:T(8,128)(2,1)S(1)} %fusion.7.trig_ref, f32[8,128]{1,0:T(8,128)S(1)} %own_part.1.own_ref, f32[24,128]{1,0:T(8,128)S(1)} %reduce_sum.9.summed_ref.here_ref), custom_call_target="tpu_custom_call" | custom-call | tf_op jit(solution)/shard_map/next_part/pallas_call | solution.py:204
  101.2 0.7 collective-permute-start.1
  101.9 0.0 collective-permute-start.3
  101.9 0.7 collective-permute-start.2
  102.6 0.2 collective-permute-done.1.before_ref
  102.8 5.6 %collective-permute-done.2 = f32[8,128]{1,0:T(8,128)S(1)} collective-permute-done((f32[8,128]{1,0:T(8,128)S(1)}, f32[8,128]{1,0:T(8,128)S(1)}, u32[]{:S(2)}, u32[]{:S(2)}) %collective-permute-start.2) | collective-permute-done | bytes 4128 | tf_op jit(solution)/shard_map/ppermute | solution.py:20
  108.4 0.0 collective-permute-done.3.after_ref
  108.5 18.1 %all_to_all.32.parts_ref = f32[8,48,128]{2,1,0:T(8,128)S(1)} all-to-all(f32[8,48,128]{2,1,0:T(8,128)S(1)} %broadcast_in_dim.33), channel_id=1, replica_groups=mesh['blk'=32,'grp'=8] {'grp'}, dimensions={0} | all-to-all | bytes 393216 | tf_op jit(solution)/shard_map/all_to_all | solution.py:333
  126.6 0.6 image_part.1
  127.2 0.0 copy-start.2
  127.2 0.6 copy-done.2
  127.8 21.3 %all_to_all.33 = f32[32,1,128]{2,1,0:T(1,128)} all-to-all(f32[32,1,128]{2,1,0:T(1,128)S(1)} %bitcast.13), channel_id=1, replica_groups=mesh['blk'=32,'grp'=8] {'blk'}, dimensions={0} | all-to-all | bytes 32768 | tf_op jit(solution)/shard_map/all_to_all | solution.py:335
  149.1 1.6 %final_part.1 = f32[16,16]{1,0:T(8,128)} custom-call(f32[32,128]{1,0:T(8,128)} %bitcast.14, f32[2,16,16]{2,1,0:T(8,128)} %copy-done.2), custom_call_target="tpu_custom_call" | custom-call | tf_op jit(solution)/shard_map/final_part/pallas_call | solution.py:287
  (12 shorter events, 0.1 us)
Async XLA Ops:
  0.0 15.2 %copy-start.3 = (bf16[128,45,128]{2,0,1:T(8,128)(2,1)S(1)}, bf16[128,45,128]{2,0,1:T(8,128)(2,1)}, u32[]{:S(2)}) copy-start(bf16[128,45,128]{2,0,1:T(8,128)(2,1)} %param.2) | copy-start | bytes 4423684
  15.7 35.6 %collective-permute-start = (bf16[45,128,128]{2,1,0:T(8,128)(2,1)S(1)}, bf16[45,128,128]{2,1,0:T(8,128)(2,1)}, u32[]{:S(2)}, u32[]{:S(2)}) collective-permute-start(bf16[45,128,128]{2,1,0:T(8,128)(2,1)S(1)} %fusion.1.own_ref.other_ref), channel_id=1, source_target_pairs={{8,0},{16,8},{24,16},{32,24},{40,32},{48,40},{56,48},{64,56},{72,6... | collective-permute-start | bytes 4423688 | tf_op jit(solution)/shard_map/ppermute | solution.py:20
  21.1 35.5 %all-to-all-start.2 = ((bf16[8,720,128]{2,1,0:T(8,128)(2,1)}), bf16[8,720,128]{2,1,0:T(8,128)(2,1)S(1)}, u32[]{:S(2)}, u32[]{:S(2)}) async-start(bf16[8,720,128]{2,1,0:T(8,128)(2,1)} %cross_own.1), calls=%async_computation.2 | async-start | bytes 2949120 | tf_op jit(solution)/shard_map/all_to_all | solution.py:312
  56.6 1.1 copy-start
  57.7 40.1 %all-to-all-start.1 = ((bf16[8,1440,128]{2,1,0:T(8,128)(2,1)}), bf16[8,1440,128]{2,1,0:T(8,128)(2,1)S(1)}, u32[]{:S(2)}, u32[]{:S(2)}) async-start(bf16[8,1440,128]{2,1,0:T(8,128)(2,1)} %cross_next.1), calls=%async_computation.1 | async-start | bytes 5898240 | tf_op jit(solution)/shard_map/all_to_all | solution.py:314
  66.3 1.4 copy-start.1
  101.2 1.6 %collective-permute-start.1 = (f32[40,128]{1,0:T(8,128)S(1)}, f32[40,128]{1,0:T(8,128)S(1)}, u32[]{:S(2)}, u32[]{:S(2)}) collective-permute-start(f32[40,128]{1,0:T(8,128)S(1)} %next_part.1), channel_id=1, source_target_pairs={{248,0},{0,8},{8,16},{16,24},{24,32},{32,40},{40,48},{48,56},{56,6... | collective-permute-start | bytes 61448 | tf_op jit(solution)/shard_map/ppermute | solution.py:20
  101.9 6.5 %collective-permute-start.3 = (f32[24,128]{1,0:T(8,128)S(1)}, f32[24,128]{1,0:T(8,128)S(1)}, u32[]{:S(2)}, u32[]{:S(2)}) collective-permute-start(f32[24,128]{1,0:T(8,128)S(1)} %slice.51), channel_id=1, source_target_pairs={{8,0},{16,8},{24,16},{32,24},{40,32},{48,40},{56,48},{64,56},{72,6... | collective-permute-start | bytes 36872 | tf_op jit(solution)/shard_map/ppermute | solution.py:20
  101.9 6.5 %collective-permute-start.2 = (f32[8,128]{1,0:T(8,128)S(1)}, f32[8,128]{1,0:T(8,128)S(1)}, u32[]{:S(2)}, u32[]{:S(2)}) collective-permute-start(f32[8,128]{1,0:T(8,128)S(1)} %slice.48), channel_id=1, source_target_pairs={{240,0},{248,8},{0,16},{8,24},{16,32},{24,40},{32,48},{40,56},{48,... | collective-permute-start | bytes 12296 | tf_op jit(solution)/shard_map/ppermute | solution.py:20
  127.2 0.6 copy-start.2

commit v5 on v3

--- a/solution.py
+++ b/solution.py
@@ -11,7 +11,8 @@
 sharpness = 2.5
 epsilon = 1e-06
 HIGHEST = lax.Precision.HIGHEST
-VMEM_LIMIT = 48 * 1024 * 1024
+COST = pl.CostEstimate(flops=20000000000, transcendentals=0, bytes_accessed=6_000_000)
+VMEM_LIMIT = 24 * 1024 * 1024
 
 
 def passed_along(block, axis, distance):
@@ -22,15 +23,18 @@
 
 def trig_columns(freq_local, group_size, group_index):
     total = freq_local * group_size
-    row_ids = jnp.arange(2 * total, dtype=jnp.int32)
-    within = row_ids % (2 * freq_local)
-    source = (group_index + group_size - row_ids // (2 * freq_local)) % group_size
+    half_width = (total + 127) // 128 * 128
+    column = jnp.arange(2 * half_width, dtype=jnp.int32)
+    place = column // half_width * total + column % half_width
+    within = place % (2 * freq_local)
+    source = (group_index + group_size - place // (2 * freq_local) % group_size) % group_size
     freq = source * freq_local + within // 2
     angles = jnp.arange(total, dtype=jnp.int32)
     phase = (angles[:, None] * freq[None, :] % total).astype(jnp.float32) * (2.0 * math.pi / total)
     cos_part = jnp.cos(phase).astype(jnp.bfloat16)
     sin_part = (-jnp.sin(phase)).astype(jnp.bfloat16)
-    return jnp.where((within % 2 == 1)[None, :], sin_part, cos_part)
+    found = jnp.where((within % 2 == 1)[None, :], sin_part, cos_part)
+    return jnp.where((column % half_width < total)[None, :], found, jnp.zeros_like(found))
 
 
 def iota(shape, dim):
@@ -158,6 +162,7 @@
         out_shape=[pltpu.HBM((parts, rows, block), jnp.bfloat16), pltpu.HBM(raw.shape, jnp.bfloat16)],
         scratch_shapes=[pltpu.VMEM((block, channels), jnp.float32)],
         compiler_params=pltpu.CompilerParams(vmem_limit_bytes=VMEM_LIMIT),
+        cost_estimate=COST,
         name="cross_own",
     )(raw, summed)
 
@@ -203,34 +208,33 @@
         ),
         out_shape=[pltpu.HBM((rows, block), jnp.bfloat16)] * parts,
         compiler_params=pltpu.CompilerParams(vmem_limit_bytes=VMEM_LIMIT),
+        cost_estimate=COST,
         name="cross_next",
     )(group_index, unit, raw, summed)
 
 
-def affinities(load, pieces, piece_rows, trig_ref, held_ref, rows, width, factor):
-    depth = trig_ref.shape[1]
-    angles = trig_ref.shape[0]
+def turn(load, pieces, piece_rows, held_ref, base, width, rows, block):
     chunk = 16 * rows
     at = iota((chunk, chunk), 0)
-    turn = (iota((chunk, chunk), 1) == (at & 15) * rows + (at >> 4)).astype(jnp.bfloat16)
-    for c in range(depth // 16):
-        begin, end = c * chunk, (c + 1) * chunk
+    matrix = (iota((chunk, chunk), 1) == (at & 15) * rows + (at >> 4)).astype(jnp.bfloat16)
+    total = pieces * piece_rows
+    for c in range(-(-total // chunk)):
+        begin, end = c * chunk, min((c + 1) * chunk, total)
         found = []
         for p in range(begin // piece_rows, (end - 1) // piece_rows + 1):
             low, high = max(begin, p * piece_rows), min(end, (p + 1) * piece_rows)
             found.append(load(p, low - p * piece_rows, high - low))
         piece = found[0] if len(found) == 1 else jnp.concatenate(found, axis=0)
-        turned = jnp.dot(turn, piece, preferred_element_type=jnp.float32).astype(jnp.bfloat16)
+        turned = jnp.dot(matrix[:, : end - begin], piece, preferred_element_type=jnp.float32).astype(jnp.bfloat16)
         for i in range(rows):
-            held_ref[c * 16 : (c + 1) * 16, i * width : (i + 1) * width] = turned[i * 16 : (i + 1) * 16]
-    out = []
-    for pair in range(rows // 2):
-        corr = jnp.dot(
-            trig_ref[...], held_ref[:, pair * 2 * width : (pair + 1) * 2 * width], preferred_element_type=jnp.float32
-        )
-        mean = jnp.sum(jnp.exp(factor * corr), axis=0, keepdims=True) * (1.0 / angles)
-        out += [mean[:, :width], mean[:, width:]]
-    return out
+            held_ref[base + c * 16 : base + (c + 1) * 16, i * block : (i + 1) * block] = turned[i * 16 : (i + 1) * 16]
+    used = -(-total // chunk) * 16
+    if used < width:
+        held_ref[base + used : base + width, :] = jnp.zeros((width - used, rows * block), jnp.bfloat16)
+
+
+def mean_exp(corr, factor):
+    return jnp.sum(jnp.exp(factor * corr), axis=0, keepdims=True) * (1.0 / corr.shape[0])
 
 
 def own_kernel(factor, group_ref, terms_ref, trig_ref, out_ref, held_ref):
@@ -241,9 +245,15 @@
     def load(p, begin, count):
         return terms_ref[sources[p], begin : begin + count, :]
 
-    means = affinities(load, parts, size, trig_ref, held_ref, rows, block, factor)
-    for i in range(rows):
-        out_ref[i : i + 1, :] = means[i]
+    half = parts // 2
+    width = trig_ref.shape[1] // 2
+    for h in range(2):
+        turn(lambda p, *where: load(h * half + p, *where), half, size, held_ref, h * width, width, rows, block)
+    for i in range(0, rows, 2):
+        corr = jnp.dot(trig_ref[...], held_ref[:, i * block : (i + 2) * block], preferred_element_type=jnp.float32)
+        mean = mean_exp(corr, factor)
+        out_ref[i : i + 1, :] = mean[:, :block]
+        out_ref[i + 1 : i + 2, :] = mean[:, block:]
     at = iota((rows, block), 0) + rows * group_ref[0]
     gap = (iota((rows, block), 1) - at) & (block - 1)
     out_ref[...] = jnp.where(gap == 0, 0.0, out_ref[...])
@@ -263,19 +273,45 @@
     )(group_index, terms, trig)
 
 
-def next_kernel(factor, group_ref, trig_ref, own_ref, summed_ref, *refs):
+def first_kernel(trig_ref, *refs):
+    *piece_refs, out_ref, held_ref = refs
+    rows = 16
+    size, block = piece_refs[0].shape
+    width = held_ref.shape[0]
+    turn(lambda p, b, n: piece_refs[p][b : b + n, :], len(piece_refs), size, held_ref, 0, width, rows, block)
+    for i in range(0, rows, 2):
+        cut = slice(i * block, (i + 2) * block)
+        out_ref[:, cut] = jnp.dot(trig_ref[:, :width], held_ref[:, cut], preferred_element_type=jnp.float32)
+
+
+def first_part(pieces, trig):
+    rows = 16
+    block = pieces[0].shape[1]
+    return pl.pallas_call(
+        first_kernel,
+        in_specs=[pl.BlockSpec(memory_space=pltpu.VMEM)] * (1 + len(pieces)),
+        out_specs=pl.BlockSpec(memory_space=pltpu.VMEM),
+        out_shape=jax.ShapeDtypeStruct((trig.shape[0], rows * block), jnp.float32),
+        scratch_shapes=[pltpu.VMEM((trig.shape[1] // 2, rows * block), jnp.bfloat16)],
+        compiler_params=pltpu.CompilerParams(vmem_limit_bytes=VMEM_LIMIT),
+        name="first_part",
+    )(trig, *pieces)
+
+
+def next_kernel(factor, group_ref, trig_ref, own_ref, summed_ref, share_ref, *refs):
     *piece_refs, out_ref, held_ref, wide_ref = refs
     rows = 16
     size, block = piece_refs[0].shape
     half = block // 2
     group = group_ref[0]
-
-    def load(p, begin, count):
-        return piece_refs[p][begin : begin + count, :]
-
-    means = affinities(load, len(piece_refs), size, trig_ref, held_ref, rows, block, factor)
-    for i in range(rows):
-        out_ref[i : i + 1, :] = means[i]
+    width = held_ref.shape[0]
+    turn(lambda p, b, n: piece_refs[p][b : b + n, :], len(piece_refs), size, held_ref, 0, width, rows, block)
+    for i in range(0, rows, 2):
+        cut = slice(i * block, (i + 2) * block)
+        corr = jnp.dot(trig_ref[:, width:], held_ref[:, cut], preferred_element_type=jnp.float32)
+        mean = mean_exp(share_ref[:, cut] + corr, factor)
+        out_ref[i : i + 1, :] = mean[:, :block]
+        out_ref[i + 1 : i + 2, :] = mean[:, block:]
     own = own_ref[...]
     at = iota((8, block), 0) + 8 * group
     gap = (iota((8, block), 1) - at) & (block - 1)
@@ -295,22 +331,22 @@
     out_ref[rows + 8 :, :] = summed_ref[8:, :]
 
 
-def next_part(group_index, pieces, trig, own, summed, factor):
+def next_part(group_index, share, pieces, trig, own, summed, factor):
     rows = 16
     block = pieces[0].shape[1]
     return pl.pallas_call(
         functools.partial(next_kernel, factor),
         in_specs=[pl.BlockSpec(memory_space=pltpu.SMEM)]
-        + [pl.BlockSpec(memory_space=pltpu.VMEM)] * (3 + len(pieces)),
+        + [pl.BlockSpec(memory_space=pltpu.VMEM)] * (4 + len(pieces)),
         out_specs=pl.BlockSpec(memory_space=pltpu.VMEM),
         out_shape=jax.ShapeDtypeStruct((rows + summed.shape[0], block), jnp.float32),
         scratch_shapes=[
-            pltpu.VMEM((trig.shape[1], rows * block), jnp.bfloat16),
+            pltpu.VMEM((trig.shape[1] // 2, rows * block), jnp.bfloat16),
             pltpu.VMEM((2 * block, block), jnp.float32),
         ],
         compiler_params=pltpu.CompilerParams(vmem_limit_bytes=VMEM_LIMIT),
         name="next_part",
-    )(group_index, trig, own, summed, *pieces)
+    )(group_index, trig, own, summed, share, *pieces)
 
 
 def image_kernel(group_ref, parts_ref, before_ref, here_ref, after_ref, out_ref, own_ref, full_ref):
@@ -409,7 +445,8 @@
     next_terms = cross_next(group_index, own_unit, after_raw, summed_after, group_size, 5)
     next_terms = [next_terms[0]] + [passed_along(next_terms[r], "grp", r) for r in range(1, group_size)]
     own_aff = own_part(group_index, own_terms, trig, factor)
-    found = next_part(group_index, next_terms, trig, own_aff, summed, factor)
+    share = first_part(next_terms[: group_size // 2], trig)
+    found = next_part(group_index, share, next_terms[group_size // 2 :], trig, own_aff, summed, factor)
 
     found_before = passed_along(found, "blk", 1)
     edge_after = passed_along(found[16:24], "blk", -1)

time: 150 us -> 136 us (0.907)
  blocking collectives: 54.9 us -> 27.6 us
  starting transfers between devices: 27.8 us -> 39 us
    all_to_all x1 -> x0, blocking collectives: 20.6 us -> none  [per_device(): summed = jnp.sum(lax.all_to_all(begun, 'grp', 0, 0, tiled=True), axis=0)]
    all_to_all x1, blocking collectives: 25.4 us -> 19.4 us  [per_device(): stats = lax.all_to_all(stats, 'blk', 0, 0, tiled=True)]
    all_to_all x0 -> x1, starting transfers between devices: none -> 5.86 us  [per_device(): summed = jnp.sum(lax.all_to_all(begun, 'grp', 0, 0, tiled=True), axis=0)]
    ppermute x12, starting transfers between devices: 23 us -> 28.6 us  [passed_along(): return lax.ppermute(block, axis, route)]
    all_to_all x0 -> x1, waiting for transfers between devices: none -> 4.37 us  [per_device(): summed = jnp.sum(lax.all_to_all(begun, 'grp', 0, 0, tiled=True), axis=0)]
    ppermute x12, waiting for transfers between devices: 37.8 us -> 34.7 us  [passed_along(): return lax.ppermute(block, axis, route)]
    pallas_call x0 -> x1, Pallas kernels: none -> 1.72 us  [first_part(): pl.pallas_call(first_kernel, in_specs=[pl.BlockSpec(memory_space=pltpu.VM...]
  transfers between devices with their start and end apart: 13 -> 14, of which waited for: 7 -> 8; matrix products, arithmetic and copies ran while one was open for 3% -> 4% of each run, Pallas kernels for 6% -> 8%
where the time goes in v5:
time: 136 us; the launch traced here: 135 us
  waiting for transfers between devices  39.1 us (29%)
  starting transfers between devices  39 us (29%)
  blocking collectives  27.6 us (20%)
  Pallas kernels  18.8 us (14%)
  local copies, waits for them, and re-layouts  5.47 us (4%)
  other arithmetic  5 us (4%)
    ppermute x12, waiting for transfers between devices, passed_along(): return lax.ppermute(block, axis, route)  34.7 us
    ppermute x12, starting transfers between devices, passed_along(): return lax.ppermute(block, axis, route)  28.6 us
    all_to_all x1, blocking collectives, per_device(): stats = lax.all_to_all(stats, 'blk', 0, 0, tiled=True)  19.4 us
    all_to_all x1, blocking collectives, per_device(): parts = lax.all_to_all(sent, 'grp', 0, 0, tiled=True)  8.19 us
    all_to_all x1, starting transfers between devices, per_device(): summed = jnp.sum(lax.all_to_all(begun, 'grp', 0, 0, tiled=True), axis=0)  5.86 us
    unnamed x12, local copies, waits for them, and re-layouts  5.42 us
    select_n x1, other arithmetic, trig_columns(): jnp.where((column % half_width < total)[None, :], found, jnp.zeros_like(f...  4.91 us
    all_to_all x1, starting transfers between devices, per_device(): own_terms = lax.all_to_all(own_terms, 'grp', 0, 0, tiled=True)  4.53 us
  transfers between devices with their start and end apart: 14, of which 8 were waited for; matrix products, arithmetic and copies ran while one was open for 4% of the time, Pallas kernels for 8%

profile of v5, /device:TPU:1, one launch (start us, length us, event | category | flops | bytes accessed | tf_op | source)
XLA Modules:
  0.0 135.2 jit_solution(10146380995046963565)
XLA Ops:
  0.0 0.0 copy-start
  0.0 1.4 %copy-done = bf16[128,45,128]{2,0,1:T(8,128)(2,1)S(1)} copy-done((bf16[128,45,128]{2,0,1:T(8,128)(2,1)S(1)}, bf16[128,45,128]{2,0,1:T(8,128)(2,1)}, u32[]{:S(2)}) %copy-start) | copy-done | bytes 1474584
  1.4 0.7 copy-done.3
  2.1 2.6 %start.1 = (f32[8,24,128]{2,1,0:T(8,128)}, bf16[45,128,128]{2,1,0:T(8,128)(2,1)}) custom-call(s32[1]{0:T(128)} %bitcast.group_ref, bf16[45,128,128]{2,1,0:T(8,128)(2,1)S(1)} %bitcast.6, f32[16,16]{1,0:T(8,128)S(1)} %copy-done.3), custom_call_target="tpu_custom_call" | custom-call | tf_op jit(solution)/shard_map/start/pallas_call | solution.py:78
  4.7 5.9 %all-to-all-start = ((f32[8,24,128]{2,1,0:T(8,128)}), f32[8,24,128]{2,1,0:T(8,128)S(1)}, u32[]{:S(2)}, u32[]{:S(2)}) async-start(f32[8,24,128]{2,1,0:T(8,128)} %get-tuple-element.20), calls=%async_computation | async-start | bytes 196608 | tf_op jit(solution)/shard_map/all_to_all | solution.py:440
  10.5 1.0 collective-permute-start
  11.5 4.4 %all-to-all-done = f32[8,24,128]{2,1,0:T(8,128)S(1)} async-done(((f32[8,24,128]{2,1,0:T(8,128)}), f32[8,24,128]{2,1,0:T(8,128)S(1)}, u32[]{:S(2)}, u32[]{:S(2)}) %all-to-all-start) | async-done | bytes 98336 | tf_op jit(solution)/shard_map/all_to_all | solution.py:440
  15.9 3.1 %collective-permute-start.1 = (f32[24,128]{1,0:T(8,128)S(1)}, f32[24,128]{1,0:T(8,128)S(1)}, u32[]{:S(2)}, u32[]{:S(2)}) collective-permute-start(f32[24,128]{1,0:T(8,128)S(1)} %reduce_sum.9.summed_ref.here_ref), channel_id=1, source_target_pairs={{8,0},{16,8},{24,16},{32,24},{40,32},{48,40},{56,48},{64,56},{72,6... | collective-permute-start | bytes 36872 | tf_op jit(solution)/shard_map/ppermute | solution.py:21
  19.0 1.4 %copy-done.4 = bf16[45,128,128]{2,1,0:T(8,128)(2,1)S(1)} copy-done((bf16[45,128,128]{2,1,0:T(8,128)(2,1)S(1)}, bf16[45,128,128]{2,1,0:T(8,128)(2,1)}, u32[]{:S(2)}) %copy-start.4) | copy-done | bytes 1474584
  20.3 3.8 %cross_own.1 = (bf16[8,720,128]{2,1,0:T(8,128)(2,1)}, bf16[45,128,128]{2,1,0:T(8,128)(2,1)}) custom-call(bf16[45,128,128]{2,1,0:T(8,128)(2,1)S(1)} %copy-done.4, f32[24,128]{1,0:T(8,128)S(1)} %reduce_sum.9.summed_ref.here_ref), custom_call_target="tpu_custom_call" | custom-call | flops 20000000000 | bytes 6000000 | tf_op jit(solution)/shard_map/cross_own/pallas_call | solution.py:157
  24.1 4.5 %all-to-all-start.1 = ((bf16[8,720,128]{2,1,0:T(8,128)(2,1)}), bf16[8,720,128]{2,1,0:T(8,128)(2,1)S(1)}, u32[]{:S(2)}, u32[]{:S(2)}) async-start(bf16[8,720,128]{2,1,0:T(8,128)(2,1)} %get-tuple-element.21), calls=%async_computation.1 | async-start | bytes 2949120 | tf_op jit(solution)/shard_map/all_to_all | solution.py:444
  28.6 5.4 %collective-permute-done.1.summed_ref.after_ref = f32[24,128]{1,0:T(8,128)S(1)} collective-permute-done((f32[24,128]{1,0:T(8,128)S(1)}, f32[24,128]{1,0:T(8,128)S(1)}, u32[]{:S(2)}, u32[]{:S(2)}) %collective-permute-start.1) | collective-permute-done | bytes 12320 | tf_op jit(solution)/shard_map/ppermute | solution.py:21
  34.0 0.0 collective-permute-done.raw_ref
  34.0 1.4 %copy-done.5 = bf16[45,128,128]{2,1,0:T(8,128)(2,1)S(1)} copy-done((bf16[45,128,128]{2,1,0:T(8,128)(2,1)S(1)}, bf16[45,128,128]{2,1,0:T(8,128)(2,1)}, u32[]{:S(2)}) %copy-start.5) | copy-done | bytes 1474584
  35.4 3.8 %cross_next.1 = (bf16[1440,128]{1,0:T(8,128)(2,1)}, bf16[1440,128]{1,0:T(8,128)(2,1)}, bf16[1440,128]{1,0:T(8,128)(2,1)}, bf16[1440,128]{1,0:T(8,128)(2,1)}, bf1...) custom-call(s32[1]{0:T(128)} %bitcast.group_ref, ...), custom_call_target="tpu_custom_call" | custom-call | flops 20000000000 | bytes 6000000 | tf_op jit(solution)/shard_map/cross_next/pallas_call | solution.py:197
  39.2 1.4 %collective-permute-start.2 = (bf16[1440,128]{1,0:T(8,128)(2,1)}, bf16[1440,128]{1,0:T(8,128)(2,1)S(1)}, u32[]{:S(2)}, u32[]{:S(2)}) collective-permute-start(bf16[1440,128]{1,0:T(8,128)(2,1)} %get-tuple-element.24), channel_id=1, source_target_pairs={{7,0},{0,1},{1,2},{2,3},{3,4},{4,5},{5,6},{6,7},{15,8},{8,9},{9,10... | collective-permute-start | bytes 1105928 | tf_op jit(solution)/shard_map/ppermute | solution.py:21
  40.5 13.3 %collective-permute-start.3 = (bf16[1440,128]{1,0:T(8,128)(2,1)}, bf16[1440,128]{1,0:T(8,128)(2,1)S(1)}, u32[]{:S(2)}, u32[]{:S(2)}) collective-permute-start(bf16[1440,128]{1,0:T(8,128)(2,1)} %get-tuple-element.25), channel_id=1, source_target_pairs={{6,0},{7,1},{0,2},{1,3},{2,4},{3,5},{4,6},{5,7},{14,8},{15,9},{8,1... | collective-permute-start | bytes 1105928 | tf_op jit(solution)/shard_map/ppermute | solution.py:21
  53.8 2.4 %collective-permute-start.4 = (bf16[1440,128]{1,0:T(8,128)(2,1)}, bf16[1440,128]{1,0:T(8,128)(2,1)S(1)}, u32[]{:S(2)}, u32[]{:S(2)}) collective-permute-start(bf16[1440,128]{1,0:T(8,128)(2,1)} %get-tuple-element.26), channel_id=1, source_target_pairs={{5,0},{6,1},{7,2},{0,3},{1,4},{2,5},{3,6},{4,7},{13,8},{14,9},{15,... | collective-permute-start | bytes 1105928 | tf_op jit(solution)/shard_map/ppermute | solution.py:21
  56.2 0.8 collective-permute-start.5
  57.0 0.0 collective-permute-start.6
  57.0 10.1 %collective-permute-done.2.refs_1_ = bf16[1440,128]{1,0:T(8,128)(2,1)S(1)} collective-permute-done((bf16[1440,128]{1,0:T(8,128)(2,1)}, bf16[1440,128]{1,0:T(8,128)(2,1)S(1)}, u32[]{:S(2)}, u32[]{:S(2)}) %collective-permute-start.2) | collective-permute-done | bytes 368672 | tf_op jit(solution)/shard_map/ppermute | solution.py:21
  67.1 5.0 %collective-permute-start.7 = (bf16[1440,128]{1,0:T(8,128)(2,1)}, bf16[1440,128]{1,0:T(8,128)(2,1)}, u32[]{:S(2)}, u32[]{:S(2)}) collective-permute-start(bf16[1440,128]{1,0:T(8,128)(2,1)} %get-tuple-element.29), channel_id=1, source_target_pairs={{2,0},{3,1},{4,2},{5,3},{6,4},{7,5},{0,6},{1,7},{10,8},{11,9},{12,... | collective-permute-start | bytes 1105928 | tf_op jit(solution)/shard_map/ppermute | solution.py:21
  72.2 0.0 collective-permute-done.3.refs_2_
  72.2 0.1 collective-permute-start.8
  72.4 4.9 %fusion.6.trig_ref = bf16[360,768]{1,0:T(8,128)(2,1)S(1)} fusion(s32[768]{0:T(1024)S(1)} %fusion.15, pred[768]{0:T(1024)(128)(4,1)S(1)} %get-tuple-element.36, pred[768]{0:T(1024)(128)(4,1)S(1)} %get-tuple-element.37), kind=kLoop, calls=%fused_computation.10 | loop fusion | flops 3870720 | bytes 557568 | tf_op jit(solution)/shard_map/jit(_where)/select_n | solution.py:37
  77.3 0.0 copy-start.1
  77.3 0.0 all-to-all-done.1.terms_ref
  77.3 1.2 own_part.1.own_ref
  78.5 0.0 collective-permute-done.4.refs_3_
  78.5 0.0 copy-done.1
  78.6 1.7 %first_part.1.share_ref = f32[360,2048]{1,0:T(8,128)S(1)} custom-call(bf16[360,768]{1,0:T(8,128)(2,1)S(1)} %fusion.6.trig_ref, bf16[1440,128]{1,0:T(8,128)(2,1)S(1)} %copy-done.1, bf16[1440,128]{1,0:T(8,128)(2,1)S(1)} %collective-permute-done.2.refs_1_, bf16[1440,128]{1,0:T(8,128)(2,1)S(1)} %collective-permute-done.3.refs_2_, ...), custom_call_target="tpu_custom_call" | custom-call | tf_op jit(solution)/shard_map/first_part/pallas_call | solution.py:290
  80.3 1.3 collective-permute-done.5.refs_0_
  81.5 0.0 collective-permute-done.6.refs_1_
  81.5 0.0 collective-permute-done.7.refs_2_
  81.5 5.9 %collective-permute-done.8.refs_3_ = bf16[1440,128]{1,0:T(8,128)(2,1)} collective-permute-done((bf16[1440,128]{1,0:T(8,128)(2,1)}, bf16[1440,128]{1,0:T(8,128)(2,1)}, u32[]{:S(2)}, u32[]{:S(2)}) %collective-permute-start.8) | collective-permute-done | bytes 368672 | tf_op jit(solution)/shard_map/ppermute | solution.py:21
  87.4 3.6 %next_part.1 = f32[40,128]{1,0:T(8,128)S(1)} custom-call(s32[1]{0:T(128)} %bitcast.group_ref, bf16[360,768]{1,0:T(8,128)(2,1)S(1)} %fusion.6.trig_ref, f32[8,128]{1,0:T(8,128)S(1)} %own_part.1.own_ref, f32[24,128]{1,0:T(8,128)S(1)} %reduce_sum.9.summed_ref.here_ref, f32[360,2048]{1,0:T(8,128)S(1)} %first_part.1.share_ref, ...), custom_call_target="tpu_custom_call" | custom-call | tf_op jit(solution)/shard_map/next_part/pallas_call | solution.py:337
  91.0 0.0 collective-permute-start.9
  91.0 1.6 %collective-permute-start.11 = (f32[8,128]{1,0:T(8,128)S(1)}, f32[8,128]{1,0:T(8,128)S(1)}, u32[]{:S(2)}, u32[]{:S(2)}) collective-permute-start(f32[8,128]{1,0:T(8,128)S(1)} %slice.40), channel_id=1, source_target_pairs={{8,0},{16,8},{24,16},{32,24},{40,32},{48,40},{56,48},{64,56},{72,6... | collective-permute-start | bytes 12296 | tf_op jit(solution)/shard_map/ppermute | solution.py:21
  92.7 0.0 collective-permute-start.10
  92.7 0.6 collective-permute-done.9.before_ref
  93.3 2.4 %collective-permute-done.11 = f32[8,128]{1,0:T(8,128)S(1)} collective-permute-done((f32[8,128]{1,0:T(8,128)S(1)}, f32[8,128]{1,0:T(8,128)S(1)}, u32[]{:S(2)}, u32[]{:S(2)}) %collective-permute-start.11) | collective-permute-done | bytes 4128 | tf_op jit(solution)/shard_map/ppermute | solution.py:21
  95.6 9.1 %collective-permute-done.10 = f32[8,128]{1,0:T(8,128)S(1)} collective-permute-done((f32[8,128]{1,0:T(8,128)S(1)}, f32[8,128]{1,0:T(8,128)S(1)}, u32[]{:S(2)}, u32[]{:S(2)}) %collective-permute-start.10) | collective-permute-done | bytes 4128 | tf_op jit(solution)/shard_map/ppermute | solution.py:21
  104.8 8.2 %all_to_all.26.parts_ref = f32[8,48,128]{2,1,0:T(8,128)S(1)} all-to-all(f32[8,48,128]{2,1,0:T(8,128)S(1)} %broadcast_in_dim.37), channel_id=1, replica_groups=mesh['blk'=32,'grp'=8] {'grp'}, dimensions={0} | all-to-all | bytes 393216 | tf_op jit(solution)/shard_map/all_to_all | solution.py:466
  113.0 0.6 image_part.1
  113.6 0.0 copy-start.2
  113.6 0.6 copy-done.2
  114.2 19.4 %all_to_all.27 = f32[32,1,128]{2,1,0:T(1,128)} all-to-all(f32[32,1,128]{2,1,0:T(1,128)S(1)} %bitcast.7), channel_id=1, replica_groups=mesh['blk'=32,'grp'=8] {'blk'}, dimensions={0} | all-to-all | bytes 32768 | tf_op jit(solution)/shard_map/all_to_all | solution.py:468
  133.6 1.6 %final_part.1 = f32[16,16]{1,0:T(8,128)} custom-call(f32[32,128]{1,0:T(8,128)} %bitcast.8, f32[2,16,16]{2,1,0:T(8,128)} %copy-done.2), custom_call_target="tpu_custom_call" | custom-call | tf_op jit(solution)/shard_map/final_part/pallas_call | solution.py:421
  (13 shorter events, 0.1 us)
Async XLA Ops:
  0.0 1.4 %copy-start = (bf16[128,45,128]{2,0,1:T(8,128)(2,1)S(1)}, bf16[128,45,128]{2,0,1:T(8,128)(2,1)}, u32[]{:S(2)}) copy-start(bf16[128,45,128]{2,0,1:T(8,128)(2,1)} %param.2) | copy-start | bytes 4423684
  1.4 0.7 copy-start.3
  4.7 11.2 %all-to-all-start = ((f32[8,24,128]{2,1,0:T(8,128)}), f32[8,24,128]{2,1,0:T(8,128)S(1)}, u32[]{:S(2)}, u32[]{:S(2)}) async-start(f32[8,24,128]{2,1,0:T(8,128)} %get-tuple-element.20), calls=%async_computation | async-start | bytes 196608 | tf_op jit(solution)/shard_map/all_to_all | solution.py:440
  10.5 23.5 %collective-permute-start = (bf16[45,128,128]{2,1,0:T(8,128)(2,1)}, bf16[45,128,128]{2,1,0:T(8,128)(2,1)S(1)}, u32[]{:S(2)}, u32[]{:S(2)}) collective-permute-start(bf16[45,128,128]{2,1,0:T(8,128)(2,1)} %get-tuple-element.19.raw_ref), channel_id=1, source_target_pairs={{8,0},{16,8},{24,16},{32,24},{40,32},{48,40},{56,48},{64,56},{72,6... | collective-permute-start | bytes 4423688 | tf_op jit(solution)/shard_map/ppermute | solution.py:21
  15.9 18.1 %collective-permute-start.1 = (f32[24,128]{1,0:T(8,128)S(1)}, f32[24,128]{1,0:T(8,128)S(1)}, u32[]{:S(2)}, u32[]{:S(2)}) collective-permute-start(f32[24,128]{1,0:T(8,128)S(1)} %reduce_sum.9.summed_ref.here_ref), channel_id=1, source_target_pairs={{8,0},{16,8},{24,16},{32,24},{40,32},{48,40},{56,48},{64,56},{72,6... | collective-permute-start | bytes 36872 | tf_op jit(solution)/shard_map/ppermute | solution.py:21
  18.9 1.4 %copy-start.4 = (bf16[45,128,128]{2,1,0:T(8,128)(2,1)S(1)}, bf16[45,128,128]{2,1,0:T(8,128)(2,1)}, u32[]{:S(2)}) copy-start(bf16[45,128,128]{2,1,0:T(8,128)(2,1)} %get-tuple-element.19.raw_ref) | copy-start | bytes 4423684
  24.1 53.2 %all-to-all-start.1 = ((bf16[8,720,128]{2,1,0:T(8,128)(2,1)}), bf16[8,720,128]{2,1,0:T(8,128)(2,1)S(1)}, u32[]{:S(2)}, u32[]{:S(2)}) async-start(bf16[8,720,128]{2,1,0:T(8,128)(2,1)} %get-tuple-element.21), calls=%async_computation.1 | async-start | bytes 2949120 | tf_op jit(solution)/shard_map/all_to_all | solution.py:444
  34.0 1.4 %copy-start.5 = (bf16[45,128,128]{2,1,0:T(8,128)(2,1)S(1)}, bf16[45,128,128]{2,1,0:T(8,128)(2,1)}, u32[]{:S(2)}) copy-start(bf16[45,128,128]{2,1,0:T(8,128)(2,1)} %get-tuple-element.22.unit_ref) | copy-start | bytes 4423684
  39.2 28.0 %collective-permute-start.2 = (bf16[1440,128]{1,0:T(8,128)(2,1)}, bf16[1440,128]{1,0:T(8,128)(2,1)S(1)}, u32[]{:S(2)}, u32[]{:S(2)}) collective-permute-start(bf16[1440,128]{1,0:T(8,128)(2,1)} %get-tuple-element.24), channel_id=1, source_target_pairs={{7,0},{0,1},{1,2},{2,3},{3,4},{4,5},{5,6},{6,7},{15,8},{8,9},{9,10... | collective-permute-start | bytes 1105928 | tf_op jit(solution)/shard_map/ppermute | solution.py:21
  40.5 31.6 %collective-permute-start.3 = (bf16[1440,128]{1,0:T(8,128)(2,1)}, bf16[1440,128]{1,0:T(8,128)(2,1)S(1)}, u32[]{:S(2)}, u32[]{:S(2)}) collective-permute-start(bf16[1440,128]{1,0:T(8,128)(2,1)} %get-tuple-element.25), channel_id=1, source_target_pairs={{6,0},{7,1},{0,2},{1,3},{2,4},{3,5},{4,6},{5,7},{14,8},{15,9},{8,1... | collective-permute-start | bytes 1105928 | tf_op jit(solution)/shard_map/ppermute | solution.py:21
  53.8 24.7 %collective-permute-start.4 = (bf16[1440,128]{1,0:T(8,128)(2,1)}, bf16[1440,128]{1,0:T(8,128)(2,1)S(1)}, u32[]{:S(2)}, u32[]{:S(2)}) collective-permute-start(bf16[1440,128]{1,0:T(8,128)(2,1)} %get-tuple-element.26), channel_id=1, source_target_pairs={{5,0},{6,1},{7,2},{0,3},{1,4},{2,5},{3,6},{4,7},{13,8},{14,9},{15,... | collective-permute-start | bytes 1105928 | tf_op jit(solution)/shard_map/ppermute | solution.py:21
  56.2 25.3 %collective-permute-start.5 = (bf16[1440,128]{1,0:T(8,128)(2,1)}, bf16[1440,128]{1,0:T(8,128)(2,1)}, u32[]{:S(2)}, u32[]{:S(2)}) collective-permute-start(bf16[1440,128]{1,0:T(8,128)(2,1)} %get-tuple-element.27), channel_id=1, source_target_pairs={{4,0},{5,1},{6,2},{7,3},{0,4},{1,5},{2,6},{3,7},{12,8},{13,9},{14,... | collective-permute-start | bytes 1105928 | tf_op jit(solution)/shard_map/ppermute | solution.py:21
  57.0 24.5 %collective-permute-start.6 = (bf16[1440,128]{1,0:T(8,128)(2,1)}, bf16[1440,128]{1,0:T(8,128)(2,1)}, u32[]{:S(2)}, u32[]{:S(2)}) collective-permute-start(bf16[1440,128]{1,0:T(8,128)(2,1)} %get-tuple-element.28), channel_id=1, source_target_pairs={{3,0},{4,1},{5,2},{6,3},{7,4},{0,5},{1,6},{2,7},{11,8},{12,9},{13,... | collective-permute-start | bytes 1105928 | tf_op jit(solution)/shard_map/ppermute | solution.py:21
  67.1 14.4 %collective-permute-start.7 = (bf16[1440,128]{1,0:T(8,128)(2,1)}, bf16[1440,128]{1,0:T(8,128)(2,1)}, u32[]{:S(2)}, u32[]{:S(2)}) collective-permute-start(bf16[1440,128]{1,0:T(8,128)(2,1)} %get-tuple-element.29), channel_id=1, source_target_pairs={{2,0},{3,1},{4,2},{5,3},{6,4},{7,5},{0,6},{1,7},{10,8},{11,9},{12,... | collective-permute-start | bytes 1105928 | tf_op jit(solution)/shard_map/ppermute | solution.py:21
  72.2 15.3 %collective-permute-start.8 = (bf16[1440,128]{1,0:T(8,128)(2,1)}, bf16[1440,128]{1,0:T(8,128)(2,1)}, u32[]{:S(2)}, u32[]{:S(2)}) collective-permute-start(bf16[1440,128]{1,0:T(8,128)(2,1)} %get-tuple-element.30), channel_id=1, source_target_pairs={{1,0},{2,1},{3,2},{4,3},{5,4},{6,5},{7,6},{0,7},{9,8},{10,9},{11,1... | collective-permute-start | bytes 1105928 | tf_op jit(solution)/shard_map/ppermute | solution.py:21
  77.3 1.3 copy-start.1
  91.0 2.3 %collective-permute-start.9 = (f32[40,128]{1,0:T(8,128)S(1)}, f32[40,128]{1,0:T(8,128)S(1)}, u32[]{:S(2)}, u32[]{:S(2)}) collective-permute-start(f32[40,128]{1,0:T(8,128)S(1)} %next_part.1), channel_id=1, source_target_pairs={{248,0},{0,8},{8,16},{16,24},{24,32},{32,40},{40,48},{48,56},{56,6... | collective-permute-start | bytes 61448 | tf_op jit(solution)/shard_map/ppermute | solution.py:21
  91.0 4.6 %collective-permute-start.11 = (f32[8,128]{1,0:T(8,128)S(1)}, f32[8,128]{1,0:T(8,128)S(1)}, u32[]{:S(2)}, u32[]{:S(2)}) collective-permute-start(f32[8,128]{1,0:T(8,128)S(1)} %slice.40), channel_id=1, source_target_pairs={{8,0},{16,8},{24,16},{32,24},{40,32},{48,40},{56,48},{64,56},{72,6... | collective-permute-start | bytes 12296 | tf_op jit(solution)/shard_map/ppermute | solution.py:21
  92.7 12.0 %collective-permute-start.10 = (f32[8,128]{1,0:T(8,128)S(1)}, f32[8,128]{1,0:T(8,128)S(1)}, u32[]{:S(2)}, u32[]{:S(2)}) collective-permute-start(f32[8,128]{1,0:T(8,128)S(1)} %slice.40), channel_id=1, source_target_pairs={{240,0},{248,8},{0,16},{8,24},{16,32},{24,40},{32,48},{40,56},{48,... | collective-permute-start | bytes 12296 | tf_op jit(solution)/shard_map/ppermute | solution.py:21
  113.6 0.6 copy-start.2

commit v6 on v5

--- a/solution.py
+++ b/solution.py
@@ -74,7 +74,7 @@
 def start(group_index, coeffs, vectors, group_size):
     freq_local, block, channels = coeffs.shape
     rows = 8 + vectors.shape[1]
-    steps = 5
+    steps = 3
     return pl.pallas_call(
         start_kernel,
         grid_spec=pltpu.PrefetchScalarGridSpec(

time: 136 us -> 135 us (level)
  no operation moved by 1% of the time
where the time goes in v6:
time: 135 us
  waiting for transfers between devices  39.2 us (29%)
  starting transfers between devices  39 us (29%)
  blocking collectives  27.6 us (20%)
  Pallas kernels  18.3 us (14%)
  local copies, waits for them, and re-layouts  5.47 us (4%)
  other arithmetic  5 us (4%)
    ppermute x12, waiting for transfers between devices, passed_along(): return lax.ppermute(block, axis, route)  34.8 us
    ppermute x12, starting transfers between devices, passed_along(): return lax.ppermute(block, axis, route)  28.6 us
    all_to_all x1, blocking collectives, per_device(): stats = lax.all_to_all(stats, 'blk', 0, 0, tiled=True)  19.4 us
    all_to_all x1, blocking collectives, per_device(): parts = lax.all_to_all(sent, 'grp', 0, 0, tiled=True)  8.19 us
    all_to_all x1, starting transfers between devices, per_device(): summed = jnp.sum(lax.all_to_all(begun, 'grp', 0, 0, tiled=True), axis=0)  5.86 us
    unnamed x12, local copies, waits for them, and re-layouts  5.42 us
    select_n x1, other arithmetic, trig_columns(): jnp.where((column % half_width < total)[None, :], found, jnp.zeros_like(f...  4.91 us
    all_to_all x1, starting transfers between devices, per_device(): own_terms = lax.all_to_all(own_terms, 'grp', 0, 0, tiled=True)  4.53 us
  transfers between devices with their start and end apart: 14, of which 8 were waited for; matrix products, arithmetic and copies ran while one was open for 4% of the time, Pallas kernels for 8%

profile of v6, /device:TPU:1, one launch (start us, length us, event | category | flops | bytes accessed | tf_op | source)
XLA Modules:
  0.0 134.7 jit_solution(10620869666030339646)
XLA Ops:
  0.0 0.0 copy-start
  0.0 1.4 %copy-done = bf16[128,45,128]{2,0,1:T(8,128)(2,1)S(1)} copy-done((bf16[128,45,128]{2,0,1:T(8,128)(2,1)S(1)}, bf16[128,45,128]{2,0,1:T(8,128)(2,1)}, u32[]{:S(2)}) %copy-start) | copy-done | bytes 1474584
  1.4 0.7 copy-done.3
  2.1 2.1 %start.1 = (f32[8,24,128]{2,1,0:T(8,128)}, bf16[45,128,128]{2,1,0:T(8,128)(2,1)}) custom-call(s32[1]{0:T(128)} %bitcast.group_ref, bf16[45,128,128]{2,1,0:T(8,128)(2,1)S(1)} %bitcast.6, f32[16,16]{1,0:T(8,128)S(1)} %copy-done.3), custom_call_target="tpu_custom_call" | custom-call | tf_op jit(solution)/shard_map/start/pallas_call | solution.py:78
  4.2 5.9 %all-to-all-start = ((f32[8,24,128]{2,1,0:T(8,128)}), f32[8,24,128]{2,1,0:T(8,128)S(1)}, u32[]{:S(2)}, u32[]{:S(2)}) async-start(f32[8,24,128]{2,1,0:T(8,128)} %get-tuple-element.20), calls=%async_computation | async-start | bytes 196608 | tf_op jit(solution)/shard_map/all_to_all | solution.py:440
  10.0 1.0 collective-permute-start
  11.0 4.4 %all-to-all-done = f32[8,24,128]{2,1,0:T(8,128)S(1)} async-done(((f32[8,24,128]{2,1,0:T(8,128)}), f32[8,24,128]{2,1,0:T(8,128)S(1)}, u32[]{:S(2)}, u32[]{:S(2)}) %all-to-all-start) | async-done | bytes 98336 | tf_op jit(solution)/shard_map/all_to_all | solution.py:440
  15.4 3.1 %collective-permute-start.1 = (f32[24,128]{1,0:T(8,128)S(1)}, f32[24,128]{1,0:T(8,128)S(1)}, u32[]{:S(2)}, u32[]{:S(2)}) collective-permute-start(f32[24,128]{1,0:T(8,128)S(1)} %reduce_sum.9.summed_ref.here_ref), channel_id=1, source_target_pairs={{8,0},{16,8},{24,16},{32,24},{40,32},{48,40},{56,48},{64,56},{72,6... | collective-permute-start | bytes 36872 | tf_op jit(solution)/shard_map/ppermute | solution.py:21
  18.4 1.4 %copy-done.4 = bf16[45,128,128]{2,1,0:T(8,128)(2,1)S(1)} copy-done((bf16[45,128,128]{2,1,0:T(8,128)(2,1)S(1)}, bf16[45,128,128]{2,1,0:T(8,128)(2,1)}, u32[]{:S(2)}) %copy-start.4) | copy-done | bytes 1474584
  19.8 3.8 %cross_own.1 = (bf16[8,720,128]{2,1,0:T(8,128)(2,1)}, bf16[45,128,128]{2,1,0:T(8,128)(2,1)}) custom-call(bf16[45,128,128]{2,1,0:T(8,128)(2,1)S(1)} %copy-done.4, f32[24,128]{1,0:T(8,128)S(1)} %reduce_sum.9.summed_ref.here_ref), custom_call_target="tpu_custom_call" | custom-call | flops 20000000000 | bytes 6000000 | tf_op jit(solution)/shard_map/cross_own/pallas_call | solution.py:157
  23.6 4.5 %all-to-all-start.1 = ((bf16[8,720,128]{2,1,0:T(8,128)(2,1)}), bf16[8,720,128]{2,1,0:T(8,128)(2,1)S(1)}, u32[]{:S(2)}, u32[]{:S(2)}) async-start(bf16[8,720,128]{2,1,0:T(8,128)(2,1)} %get-tuple-element.21), calls=%async_computation.1 | async-start | bytes 2949120 | tf_op jit(solution)/shard_map/all_to_all | solution.py:444
  28.1 5.4 %collective-permute-done.1.summed_ref.after_ref = f32[24,128]{1,0:T(8,128)S(1)} collective-permute-done((f32[24,128]{1,0:T(8,128)S(1)}, f32[24,128]{1,0:T(8,128)S(1)}, u32[]{:S(2)}, u32[]{:S(2)}) %collective-permute-start.1) | collective-permute-done | bytes 12320 | tf_op jit(solution)/shard_map/ppermute | solution.py:21
  33.5 0.0 collective-permute-done.raw_ref
  33.5 1.4 %copy-done.5 = bf16[45,128,128]{2,1,0:T(8,128)(2,1)S(1)} copy-done((bf16[45,128,128]{2,1,0:T(8,128)(2,1)S(1)}, bf16[45,128,128]{2,1,0:T(8,128)(2,1)}, u32[]{:S(2)}) %copy-start.5) | copy-done | bytes 1474584
  34.9 3.8 %cross_next.1 = (bf16[1440,128]{1,0:T(8,128)(2,1)}, bf16[1440,128]{1,0:T(8,128)(2,1)}, bf16[1440,128]{1,0:T(8,128)(2,1)}, bf16[1440,128]{1,0:T(8,128)(2,1)}, bf1...) custom-call(s32[1]{0:T(128)} %bitcast.group_ref, ...), custom_call_target="tpu_custom_call" | custom-call | flops 20000000000 | bytes 6000000 | tf_op jit(solution)/shard_map/cross_next/pallas_call | solution.py:197
  38.7 1.4 %collective-permute-start.2 = (bf16[1440,128]{1,0:T(8,128)(2,1)}, bf16[1440,128]{1,0:T(8,128)(2,1)S(1)}, u32[]{:S(2)}, u32[]{:S(2)}) collective-permute-start(bf16[1440,128]{1,0:T(8,128)(2,1)} %get-tuple-element.24), channel_id=1, source_target_pairs={{7,0},{0,1},{1,2},{2,3},{3,4},{4,5},{5,6},{6,7},{15,8},{8,9},{9,10... | collective-permute-start | bytes 1105928 | tf_op jit(solution)/shard_map/ppermute | solution.py:21
  40.0 13.3 %collective-permute-start.3 = (bf16[1440,128]{1,0:T(8,128)(2,1)}, bf16[1440,128]{1,0:T(8,128)(2,1)S(1)}, u32[]{:S(2)}, u32[]{:S(2)}) collective-permute-start(bf16[1440,128]{1,0:T(8,128)(2,1)} %get-tuple-element.25), channel_id=1, source_target_pairs={{6,0},{7,1},{0,2},{1,3},{2,4},{3,5},{4,6},{5,7},{14,8},{15,9},{8,1... | collective-permute-start | bytes 1105928 | tf_op jit(solution)/shard_map/ppermute | solution.py:21
  53.3 2.4 %collective-permute-start.4 = (bf16[1440,128]{1,0:T(8,128)(2,1)}, bf16[1440,128]{1,0:T(8,128)(2,1)S(1)}, u32[]{:S(2)}, u32[]{:S(2)}) collective-permute-start(bf16[1440,128]{1,0:T(8,128)(2,1)} %get-tuple-element.26), channel_id=1, source_target_pairs={{5,0},{6,1},{7,2},{0,3},{1,4},{2,5},{3,6},{4,7},{13,8},{14,9},{15,... | collective-permute-start | bytes 1105928 | tf_op jit(solution)/shard_map/ppermute | solution.py:21
  55.7 0.8 collective-permute-start.5
  56.5 0.0 collective-permute-start.6
  56.5 10.1 %collective-permute-done.2.refs_1_ = bf16[1440,128]{1,0:T(8,128)(2,1)S(1)} collective-permute-done((bf16[1440,128]{1,0:T(8,128)(2,1)}, bf16[1440,128]{1,0:T(8,128)(2,1)S(1)}, u32[]{:S(2)}, u32[]{:S(2)}) %collective-permute-start.2) | collective-permute-done | bytes 368672 | tf_op jit(solution)/shard_map/ppermute | solution.py:21
  66.6 5.0 %collective-permute-start.7 = (bf16[1440,128]{1,0:T(8,128)(2,1)}, bf16[1440,128]{1,0:T(8,128)(2,1)}, u32[]{:S(2)}, u32[]{:S(2)}) collective-permute-start(bf16[1440,128]{1,0:T(8,128)(2,1)} %get-tuple-element.29), channel_id=1, source_target_pairs={{2,0},{3,1},{4,2},{5,3},{6,4},{7,5},{0,6},{1,7},{10,8},{11,9},{12,... | collective-permute-start | bytes 1105928 | tf_op jit(solution)/shard_map/ppermute | solution.py:21
  71.6 0.0 collective-permute-done.3.refs_2_
  71.7 0.1 collective-permute-start.8
  71.8 4.9 %fusion.6.trig_ref = bf16[360,768]{1,0:T(8,128)(2,1)S(1)} fusion(s32[768]{0:T(1024)S(1)} %fusion.15, pred[768]{0:T(1024)(128)(4,1)S(1)} %get-tuple-element.36, pred[768]{0:T(1024)(128)(4,1)S(1)} %get-tuple-element.37), kind=kLoop, calls=%fused_computation.10 | loop fusion | flops 3870720 | bytes 557568 | tf_op jit(solution)/shard_map/jit(_where)/select_n | solution.py:37
  76.7 0.0 copy-start.1
  76.8 0.0 all-to-all-done.1.terms_ref
  76.8 1.2 own_part.1.own_ref
  78.0 0.0 collective-permute-done.4.refs_3_
  78.0 0.0 copy-done.1
  78.0 1.7 %first_part.1.share_ref = f32[360,2048]{1,0:T(8,128)S(1)} custom-call(bf16[360,768]{1,0:T(8,128)(2,1)S(1)} %fusion.6.trig_ref, bf16[1440,128]{1,0:T(8,128)(2,1)S(1)} %copy-done.1, bf16[1440,128]{1,0:T(8,128)(2,1)S(1)} %collective-permute-done.2.refs_1_, bf16[1440,128]{1,0:T(8,128)(2,1)S(1)} %collective-permute-done.3.refs_2_, ...), custom_call_target="tpu_custom_call" | custom-call | tf_op jit(solution)/shard_map/first_part/pallas_call | solution.py:290
  79.8 1.3 collective-permute-done.5.refs_0_
  81.0 0.0 collective-permute-done.6.refs_1_
  81.0 0.0 collective-permute-done.7.refs_2_
  81.0 5.9 %collective-permute-done.8.refs_3_ = bf16[1440,128]{1,0:T(8,128)(2,1)} collective-permute-done((bf16[1440,128]{1,0:T(8,128)(2,1)}, bf16[1440,128]{1,0:T(8,128)(2,1)}, u32[]{:S(2)}, u32[]{:S(2)}) %collective-permute-start.8) | collective-permute-done | bytes 368672 | tf_op jit(solution)/shard_map/ppermute | solution.py:21
  86.9 3.6 %next_part.1 = f32[40,128]{1,0:T(8,128)S(1)} custom-call(s32[1]{0:T(128)} %bitcast.group_ref, bf16[360,768]{1,0:T(8,128)(2,1)S(1)} %fusion.6.trig_ref, f32[8,128]{1,0:T(8,128)S(1)} %own_part.1.own_ref, f32[24,128]{1,0:T(8,128)S(1)} %reduce_sum.9.summed_ref.here_ref, f32[360,2048]{1,0:T(8,128)S(1)} %first_part.1.share_ref, ...), custom_call_target="tpu_custom_call" | custom-call | tf_op jit(solution)/shard_map/next_part/pallas_call | solution.py:337
  90.5 0.0 collective-permute-start.9
  90.5 1.6 %collective-permute-start.11 = (f32[8,128]{1,0:T(8,128)S(1)}, f32[8,128]{1,0:T(8,128)S(1)}, u32[]{:S(2)}, u32[]{:S(2)}) collective-permute-start(f32[8,128]{1,0:T(8,128)S(1)} %slice.40), channel_id=1, source_target_pairs={{8,0},{16,8},{24,16},{32,24},{40,32},{48,40},{56,48},{64,56},{72,6... | collective-permute-start | bytes 12296 | tf_op jit(solution)/shard_map/ppermute | solution.py:21
  92.1 0.0 collective-permute-start.10
  92.1 0.6 collective-permute-done.9.before_ref
  92.7 2.4 %collective-permute-done.11 = f32[8,128]{1,0:T(8,128)S(1)} collective-permute-done((f32[8,128]{1,0:T(8,128)S(1)}, f32[8,128]{1,0:T(8,128)S(1)}, u32[]{:S(2)}, u32[]{:S(2)}) %collective-permute-start.11) | collective-permute-done | bytes 4128 | tf_op jit(solution)/shard_map/ppermute | solution.py:21
  95.1 9.2 %collective-permute-done.10 = f32[8,128]{1,0:T(8,128)S(1)} collective-permute-done((f32[8,128]{1,0:T(8,128)S(1)}, f32[8,128]{1,0:T(8,128)S(1)}, u32[]{:S(2)}, u32[]{:S(2)}) %collective-permute-start.10) | collective-permute-done | bytes 4128 | tf_op jit(solution)/shard_map/ppermute | solution.py:21
  104.3 8.2 %all_to_all.26.parts_ref = f32[8,48,128]{2,1,0:T(8,128)S(1)} all-to-all(f32[8,48,128]{2,1,0:T(8,128)S(1)} %broadcast_in_dim.37), channel_id=1, replica_groups=mesh['blk'=32,'grp'=8] {'grp'}, dimensions={0} | all-to-all | bytes 393216 | tf_op jit(solution)/shard_map/all_to_all | solution.py:466
  112.5 0.6 image_part.1
  113.1 0.0 copy-start.2
  113.1 0.6 copy-done.2
  113.7 19.4 %all_to_all.27 = f32[32,1,128]{2,1,0:T(1,128)} all-to-all(f32[32,1,128]{2,1,0:T(1,128)S(1)} %bitcast.7), channel_id=1, replica_groups=mesh['blk'=32,'grp'=8] {'blk'}, dimensions={0} | all-to-all | bytes 32768 | tf_op jit(solution)/shard_map/all_to_all | solution.py:468
  133.1 1.6 %final_part.1 = f32[16,16]{1,0:T(8,128)} custom-call(f32[32,128]{1,0:T(8,128)} %bitcast.8, f32[2,16,16]{2,1,0:T(8,128)} %copy-done.2), custom_call_target="tpu_custom_call" | custom-call | tf_op jit(solution)/shard_map/final_part/pallas_call | solution.py:421
  (13 shorter events, 0.1 us)
Async XLA Ops:
  0.0 1.4 %copy-start = (bf16[128,45,128]{2,0,1:T(8,128)(2,1)S(1)}, bf16[128,45,128]{2,0,1:T(8,128)(2,1)}, u32[]{:S(2)}) copy-start(bf16[128,45,128]{2,0,1:T(8,128)(2,1)} %param.2) | copy-start | bytes 4423684
  1.4 0.7 copy-start.3
  4.2 11.2 %all-to-all-start = ((f32[8,24,128]{2,1,0:T(8,128)}), f32[8,24,128]{2,1,0:T(8,128)S(1)}, u32[]{:S(2)}, u32[]{:S(2)}) async-start(f32[8,24,128]{2,1,0:T(8,128)} %get-tuple-element.20), calls=%async_computation | async-start | bytes 196608 | tf_op jit(solution)/shard_map/all_to_all | solution.py:440
  10.0 23.5 %collective-permute-start = (bf16[45,128,128]{2,1,0:T(8,128)(2,1)}, bf16[45,128,128]{2,1,0:T(8,128)(2,1)S(1)}, u32[]{:S(2)}, u32[]{:S(2)}) collective-permute-start(bf16[45,128,128]{2,1,0:T(8,128)(2,1)} %get-tuple-element.19.raw_ref), channel_id=1, source_target_pairs={{8,0},{16,8},{24,16},{32,24},{40,32},{48,40},{56,48},{64,56},{72,6... | collective-permute-start | bytes 4423688 | tf_op jit(solution)/shard_map/ppermute | solution.py:21
  15.4 18.1 %collective-permute-start.1 = (f32[24,128]{1,0:T(8,128)S(1)}, f32[24,128]{1,0:T(8,128)S(1)}, u32[]{:S(2)}, u32[]{:S(2)}) collective-permute-start(f32[24,128]{1,0:T(8,128)S(1)} %reduce_sum.9.summed_ref.here_ref), channel_id=1, source_target_pairs={{8,0},{16,8},{24,16},{32,24},{40,32},{48,40},{56,48},{64,56},{72,6... | collective-permute-start | bytes 36872 | tf_op jit(solution)/shard_map/ppermute | solution.py:21
  18.4 1.4 %copy-start.4 = (bf16[45,128,128]{2,1,0:T(8,128)(2,1)S(1)}, bf16[45,128,128]{2,1,0:T(8,128)(2,1)}, u32[]{:S(2)}) copy-start(bf16[45,128,128]{2,1,0:T(8,128)(2,1)} %get-tuple-element.19.raw_ref) | copy-start | bytes 4423684
  23.6 53.2 %all-to-all-start.1 = ((bf16[8,720,128]{2,1,0:T(8,128)(2,1)}), bf16[8,720,128]{2,1,0:T(8,128)(2,1)S(1)}, u32[]{:S(2)}, u32[]{:S(2)}) async-start(bf16[8,720,128]{2,1,0:T(8,128)(2,1)} %get-tuple-element.21), calls=%async_computation.1 | async-start | bytes 2949120 | tf_op jit(solution)/shard_map/all_to_all | solution.py:444
  33.5 1.4 %copy-start.5 = (bf16[45,128,128]{2,1,0:T(8,128)(2,1)S(1)}, bf16[45,128,128]{2,1,0:T(8,128)(2,1)}, u32[]{:S(2)}) copy-start(bf16[45,128,128]{2,1,0:T(8,128)(2,1)} %get-tuple-element.22.unit_ref) | copy-start | bytes 4423684
  38.7 28.0 %collective-permute-start.2 = (bf16[1440,128]{1,0:T(8,128)(2,1)}, bf16[1440,128]{1,0:T(8,128)(2,1)S(1)}, u32[]{:S(2)}, u32[]{:S(2)}) collective-permute-start(bf16[1440,128]{1,0:T(8,128)(2,1)} %get-tuple-element.24), channel_id=1, source_target_pairs={{7,0},{0,1},{1,2},{2,3},{3,4},{4,5},{5,6},{6,7},{15,8},{8,9},{9,10... | collective-permute-start | bytes 1105928 | tf_op jit(solution)/shard_map/ppermute | solution.py:21
  40.0 31.6 %collective-permute-start.3 = (bf16[1440,128]{1,0:T(8,128)(2,1)}, bf16[1440,128]{1,0:T(8,128)(2,1)S(1)}, u32[]{:S(2)}, u32[]{:S(2)}) collective-permute-start(bf16[1440,128]{1,0:T(8,128)(2,1)} %get-tuple-element.25), channel_id=1, source_target_pairs={{6,0},{7,1},{0,2},{1,3},{2,4},{3,5},{4,6},{5,7},{14,8},{15,9},{8,1... | collective-permute-start | bytes 1105928 | tf_op jit(solution)/shard_map/ppermute | solution.py:21
  53.3 24.7 %collective-permute-start.4 = (bf16[1440,128]{1,0:T(8,128)(2,1)}, bf16[1440,128]{1,0:T(8,128)(2,1)S(1)}, u32[]{:S(2)}, u32[]{:S(2)}) collective-permute-start(bf16[1440,128]{1,0:T(8,128)(2,1)} %get-tuple-element.26), channel_id=1, source_target_pairs={{5,0},{6,1},{7,2},{0,3},{1,4},{2,5},{3,6},{4,7},{13,8},{14,9},{15,... | collective-permute-start | bytes 1105928 | tf_op jit(solution)/shard_map/ppermute | solution.py:21
  55.7 25.3 %collective-permute-start.5 = (bf16[1440,128]{1,0:T(8,128)(2,1)}, bf16[1440,128]{1,0:T(8,128)(2,1)}, u32[]{:S(2)}, u32[]{:S(2)}) collective-permute-start(bf16[1440,128]{1,0:T(8,128)(2,1)} %get-tuple-element.27), channel_id=1, source_target_pairs={{4,0},{5,1},{6,2},{7,3},{0,4},{1,5},{2,6},{3,7},{12,8},{13,9},{14,... | collective-permute-start | bytes 1105928 | tf_op jit(solution)/shard_map/ppermute | solution.py:21
  56.5 24.5 %collective-permute-start.6 = (bf16[1440,128]{1,0:T(8,128)(2,1)}, bf16[1440,128]{1,0:T(8,128)(2,1)}, u32[]{:S(2)}, u32[]{:S(2)}) collective-permute-start(bf16[1440,128]{1,0:T(8,128)(2,1)} %get-tuple-element.28), channel_id=1, source_target_pairs={{3,0},{4,1},{5,2},{6,3},{7,4},{0,5},{1,6},{2,7},{11,8},{12,9},{13,... | collective-permute-start | bytes 1105928 | tf_op jit(solution)/shard_map/ppermute | solution.py:21
  66.6 14.4 %collective-permute-start.7 = (bf16[1440,128]{1,0:T(8,128)(2,1)}, bf16[1440,128]{1,0:T(8,128)(2,1)}, u32[]{:S(2)}, u32[]{:S(2)}) collective-permute-start(bf16[1440,128]{1,0:T(8,128)(2,1)} %get-tuple-element.29), channel_id=1, source_target_pairs={{2,0},{3,1},{4,2},{5,3},{6,4},{7,5},{0,6},{1,7},{10,8},{11,9},{12,... | collective-permute-start | bytes 1105928 | tf_op jit(solution)/shard_map/ppermute | solution.py:21
  71.7 15.2 %collective-permute-start.8 = (bf16[1440,128]{1,0:T(8,128)(2,1)}, bf16[1440,128]{1,0:T(8,128)(2,1)}, u32[]{:S(2)}, u32[]{:S(2)}) collective-permute-start(bf16[1440,128]{1,0:T(8,128)(2,1)} %get-tuple-element.30), channel_id=1, source_target_pairs={{1,0},{2,1},{3,2},{4,3},{5,4},{6,5},{7,6},{0,7},{9,8},{10,9},{11,1... | collective-permute-start | bytes 1105928 | tf_op jit(solution)/shard_map/ppermute | solution.py:21
  76.7 1.3 copy-start.1
  90.5 2.3 %collective-permute-start.9 = (f32[40,128]{1,0:T(8,128)S(1)}, f32[40,128]{1,0:T(8,128)S(1)}, u32[]{:S(2)}, u32[]{:S(2)}) collective-permute-start(f32[40,128]{1,0:T(8,128)S(1)} %next_part.1), channel_id=1, source_target_pairs={{248,0},{0,8},{8,16},{16,24},{24,32},{32,40},{40,48},{48,56},{56,6... | collective-permute-start | bytes 61448 | tf_op jit(solution)/shard_map/ppermute | solution.py:21
  90.5 4.6 %collective-permute-start.11 = (f32[8,128]{1,0:T(8,128)S(1)}, f32[8,128]{1,0:T(8,128)S(1)}, u32[]{:S(2)}, u32[]{:S(2)}) collective-permute-start(f32[8,128]{1,0:T(8,128)S(1)} %slice.40), channel_id=1, source_target_pairs={{8,0},{16,8},{24,16},{32,24},{40,32},{48,40},{56,48},{64,56},{72,6... | collective-permute-start | bytes 12296 | tf_op jit(solution)/shard_map/ppermute | solution.py:21
  92.1 12.1 %collective-permute-start.10 = (f32[8,128]{1,0:T(8,128)S(1)}, f32[8,128]{1,0:T(8,128)S(1)}, u32[]{:S(2)}, u32[]{:S(2)}) collective-permute-start(f32[8,128]{1,0:T(8,128)S(1)} %slice.40), channel_id=1, source_target_pairs={{240,0},{248,8},{0,16},{8,24},{16,32},{24,40},{32,48},{40,56},{48,... | collective-permute-start | bytes 12296 | tf_op jit(solution)/shard_map/ppermute | solution.py:21
  113.1 0.6 copy-start.2

commit v7 on v6

--- a/solution.py
+++ b/solution.py
@@ -237,7 +237,7 @@
     return jnp.sum(jnp.exp(factor * corr), axis=0, keepdims=True) * (1.0 / corr.shape[0])
 
 
-def own_kernel(factor, group_ref, terms_ref, trig_ref, out_ref, held_ref):
+def own_kernel(factor, group_ref, terms_ref, trig_ref, out_ref, degree_ref, held_ref, wide_ref):
     parts, size, block = terms_ref.shape
     rows = out_ref.shape[0]
     sources = [lax.rem(group_ref[0] + (parts - p), parts) for p in range(parts)]
@@ -256,7 +256,15 @@
         out_ref[i + 1 : i + 2, :] = mean[:, block:]
     at = iota((rows, block), 0) + rows * group_ref[0]
     gap = (iota((rows, block), 1) - at) & (block - 1)
-    out_ref[...] = jnp.where(gap == 0, 0.0, out_ref[...])
+    own = jnp.where(gap == 0, 0.0, out_ref[...])
+    out_ref[...] = own
+    top = (gap >= 1) & (gap <= block // 2)
+    own_at = pl.multiple_of(rows * group_ref[0], rows)
+    wide_ref[...] = jnp.zeros_like(wide_ref)
+    wide_ref[pl.ds(own_at, rows), :] = jnp.where(top, own, 0.0)
+    wide_ref[pl.ds(block // 2 + own_at, rows), :] = jnp.where(top, 0.0, own)
+    by_row = dot(jnp.ones((8, block), jnp.float32), wide_ref[...], ((1,), (1,)))
+    degree_ref[...] = by_row[0:1] + jnp.sum(own, axis=0, keepdims=True)
 
 
 def own_part(group_index, terms, trig, factor):
@@ -265,9 +273,12 @@
     return pl.pallas_call(
         functools.partial(own_kernel, factor),
         in_specs=[pl.BlockSpec(memory_space=pltpu.SMEM)] + [pl.BlockSpec(memory_space=pltpu.VMEM)] * 2,
-        out_specs=pl.BlockSpec(memory_space=pltpu.VMEM),
-        out_shape=jax.ShapeDtypeStruct((rows, block), jnp.float32),
-        scratch_shapes=[pltpu.VMEM((trig.shape[1], rows * block), jnp.bfloat16)],
+        out_specs=[pl.BlockSpec(memory_space=pltpu.VMEM)] * 2,
+        out_shape=[jax.ShapeDtypeStruct((n, block), jnp.float32) for n in (rows, 1)],
+        scratch_shapes=[
+            pltpu.VMEM((trig.shape[1], rows * block), jnp.bfloat16),
+            pltpu.VMEM((block, block), jnp.float32),
+        ],
         compiler_params=pltpu.CompilerParams(vmem_limit_bytes=VMEM_LIMIT),
         name="own_part",
     )(group_index, terms, trig)
@@ -298,11 +309,10 @@
     )(trig, *pieces)
 
 
-def next_kernel(factor, group_ref, trig_ref, own_ref, summed_ref, share_ref, *refs):
+def next_kernel(factor, group_ref, trig_ref, degree_ref, summed_ref, share_ref, *refs):
     *piece_refs, out_ref, held_ref, wide_ref = refs
     rows = 16
     size, block = piece_refs[0].shape
-    half = block // 2
     group = group_ref[0]
     width = held_ref.shape[0]
     turn(lambda p, b, n: piece_refs[p][b : b + n, :], len(piece_refs), size, held_ref, 0, width, rows, block)
@@ -312,26 +322,18 @@
         mean = mean_exp(share_ref[:, cut] + corr, factor)
         out_ref[i : i + 1, :] = mean[:, :block]
         out_ref[i + 1 : i + 2, :] = mean[:, block:]
-    own = own_ref[...]
-    at = iota((8, block), 0) + 8 * group
-    gap = (iota((8, block), 1) - at) & (block - 1)
-    top = (gap >= 1) & (gap <= half)
-    upper, lower = jnp.where(top, own, 0.0), jnp.where(top, 0.0, own)
     wide_ref[...] = jnp.zeros_like(wide_ref)
     wide_ref[pl.ds(pl.multiple_of(rows * group, rows), rows), :] = out_ref[0:rows, :]
-    own_at = pl.multiple_of(8 * group, 8)
-    wide_ref[pl.ds(block + own_at, 8), :] = upper
-    wide_ref[pl.ds(block + half + own_at, 8), :] = lower
     ones = jnp.ones((8, block), jnp.float32)
     by_row = dot(ones, wide_ref[...], ((1,), (1,)))
-    degree = by_row[0:1, :block] + by_row[0:1, block:] + jnp.sum(own, axis=0, keepdims=True)
+    degree = by_row[0:1] + degree_ref[...]
     out_ref[rows : rows + 8, :] = jnp.zeros((8, block), jnp.float32)
     out_ref[rows : rows + 1, :] = degree
     out_ref[rows + 1 : rows + 2, :] = jnp.sum(out_ref[0:rows, :], axis=0, keepdims=True)
     out_ref[rows + 8 :, :] = summed_ref[8:, :]
 
 
-def next_part(group_index, share, pieces, trig, own, summed, factor):
+def next_part(group_index, share, pieces, trig, own_degree, summed, factor):
     rows = 16
     block = pieces[0].shape[1]
     return pl.pallas_call(
@@ -342,11 +344,11 @@
         out_shape=jax.ShapeDtypeStruct((rows + summed.shape[0], block), jnp.float32),
         scratch_shapes=[
             pltpu.VMEM((trig.shape[1] // 2, rows * block), jnp.bfloat16),
-            pltpu.VMEM((2 * block, block), jnp.float32),
+            pltpu.VMEM((block, block), jnp.float32),
         ],
         compiler_params=pltpu.CompilerParams(vmem_limit_bytes=VMEM_LIMIT),
         name="next_part",
-    )(group_index, trig, own, summed, share, *pieces)
+    )(group_index, trig, own_degree, summed, share, *pieces)
 
 
 def image_kernel(group_ref, parts_ref, before_ref, here_ref, after_ref, out_ref, own_ref, full_ref):
@@ -444,9 +446,9 @@
     own_terms = lax.all_to_all(own_terms, "grp", 0, 0, tiled=True)
     next_terms = cross_next(group_index, own_unit, after_raw, summed_after, group_size, 5)
     next_terms = [next_terms[0]] + [passed_along(next_terms[r], "grp", r) for r in range(1, group_size)]
-    own_aff = own_part(group_index, own_terms, trig, factor)
+    own_aff, own_degree = own_part(group_index, own_terms, trig, factor)
     share = first_part(next_terms[: group_size // 2], trig)
-    found = next_part(group_index, share, next_terms[group_size // 2 :], trig, own_aff, summed, factor)
+    found = next_part(group_index, share, next_terms[group_size // 2 :], trig, own_degree, summed, factor)
 
     found_before = passed_along(found, "blk", 1)
     edge_after = passed_along(found[16:24], "blk", -1)

time: 135 us -> 135 us (level)
  waiting for transfers between devices: 39.2 us -> 37.2 us
    ppermute x12, waiting for transfers between devices: 34.8 us -> 32.8 us  [passed_along(): return lax.ppermute(block, axis, route)]
    unnamed x12 -> x16, local copies, waits for them, and re-layouts: 5.42 us -> 6.2 us
  transfers between devices with their start and end apart: 14 -> 14, of which waited for: 8 -> 7; matrix products, arithmetic and copies ran while one was open for 4% -> 4% of each run, Pallas kernels for 8% -> 9%
where the time goes in v7:
time: 135 us; the launch traced here: 134 us
  starting transfers between devices  39.1 us (29%)
  waiting for transfers between devices  37.2 us (28%)
  blocking collectives  27.6 us (20%)
  Pallas kernels  19.1 us (14%)
  local copies, waits for them, and re-layouts  6.25 us (5%)
  other arithmetic  5 us (4%)
    ppermute x12, waiting for transfers between devices, passed_along(): return lax.ppermute(block, axis, route)  32.8 us
    ppermute x12, starting transfers between devices, passed_along(): return lax.ppermute(block, axis, route)  28.7 us
    all_to_all x1, blocking collectives, per_device(): stats = lax.all_to_all(stats, 'blk', 0, 0, tiled=True)  19.4 us
    all_to_all x1, blocking collectives, per_device(): parts = lax.all_to_all(sent, 'grp', 0, 0, tiled=True)  8.19 us
    unnamed x16, local copies, waits for them, and re-layouts  6.2 us
    all_to_all x1, starting transfers between devices, per_device(): summed = jnp.sum(lax.all_to_all(begun, 'grp', 0, 0, tiled=True), axis=0)  5.86 us
    select_n x1, other arithmetic, trig_columns(): jnp.where((column % half_width < total)[None, :], found, jnp.zeros_like(f...  4.91 us
    all_to_all x1, starting transfers between devices, per_device(): own_terms = lax.all_to_all(own_terms, 'grp', 0, 0, tiled=True)  4.54 us
  transfers between devices with their start and end apart: 14, of which 7 were waited for; matrix products, arithmetic and copies ran while one was open for 4% of the time, Pallas kernels for 9%

profile of v7, /device:TPU:1, one launch (start us, length us, event | category | flops | bytes accessed | tf_op | source)
XLA Modules:
  0.0 134.4 jit_solution(6737908508007790816)
XLA Ops:
  0.0 1.4 %copy-done = bf16[128,45,128]{2,0,1:T(8,128)(2,1)S(1)} copy-done((bf16[128,45,128]{2,0,1:T(8,128)(2,1)S(1)}, bf16[128,45,128]{2,0,1:T(8,128)(2,1)}, u32[]{:S(2)}) %copy-start) | copy-done | bytes 1474584
  1.4 0.7 copy-done.5
  2.1 2.1 %start.1 = (f32[8,24,128]{2,1,0:T(8,128)}, bf16[45,128,128]{2,1,0:T(8,128)(2,1)}) custom-call(s32[1]{0:T(128)} %bitcast.group_ref, bf16[45,128,128]{2,1,0:T(8,128)(2,1)S(1)} %bitcast.6, f32[16,16]{1,0:T(8,128)S(1)} %copy-done.5), custom_call_target="tpu_custom_call" | custom-call | tf_op jit(solution)/shard_map/start/pallas_call | solution.py:78
  4.2 5.9 %all-to-all-start = ((f32[8,24,128]{2,1,0:T(8,128)}), f32[8,24,128]{2,1,0:T(8,128)S(1)}, u32[]{:S(2)}, u32[]{:S(2)}) async-start(f32[8,24,128]{2,1,0:T(8,128)} %get-tuple-element.22), calls=%async_computation | async-start | bytes 196608 | tf_op jit(solution)/shard_map/all_to_all | solution.py:442
  10.0 1.0 collective-permute-start
  11.0 4.4 %all-to-all-done = f32[8,24,128]{2,1,0:T(8,128)S(1)} async-done(((f32[8,24,128]{2,1,0:T(8,128)}), f32[8,24,128]{2,1,0:T(8,128)S(1)}, u32[]{:S(2)}, u32[]{:S(2)}) %all-to-all-start) | async-done | bytes 98336 | tf_op jit(solution)/shard_map/all_to_all | solution.py:442
  15.4 3.1 %collective-permute-start.1 = (f32[24,128]{1,0:T(8,128)S(1)}, f32[24,128]{1,0:T(8,128)S(1)}, u32[]{:S(2)}, u32[]{:S(2)}) collective-permute-start(f32[24,128]{1,0:T(8,128)S(1)} %reduce_sum.9.summed_ref.here_ref), channel_id=1, source_target_pairs={{8,0},{16,8},{24,16},{32,24},{40,32},{48,40},{56,48},{64,56},{72,6... | collective-permute-start | bytes 36872 | tf_op jit(solution)/shard_map/ppermute | solution.py:21
  18.4 1.4 %copy-done.6 = bf16[45,128,128]{2,1,0:T(8,128)(2,1)S(1)} copy-done((bf16[45,128,128]{2,1,0:T(8,128)(2,1)S(1)}, bf16[45,128,128]{2,1,0:T(8,128)(2,1)}, u32[]{:S(2)}) %copy-start.6) | copy-done | bytes 1474584
  19.8 3.8 %cross_own.1 = (bf16[8,720,128]{2,1,0:T(8,128)(2,1)}, bf16[45,128,128]{2,1,0:T(8,128)(2,1)}) custom-call(bf16[45,128,128]{2,1,0:T(8,128)(2,1)S(1)} %copy-done.6, f32[24,128]{1,0:T(8,128)S(1)} %reduce_sum.9.summed_ref.here_ref), custom_call_target="tpu_custom_call" | custom-call | flops 20000000000 | bytes 6000000 | tf_op jit(solution)/shard_map/cross_own/pallas_call | solution.py:157
  23.6 4.5 %all-to-all-start.1 = ((bf16[8,720,128]{2,1,0:T(8,128)(2,1)}), bf16[8,720,128]{2,1,0:T(8,128)(2,1)S(1)}, u32[]{:S(2)}, u32[]{:S(2)}) async-start(bf16[8,720,128]{2,1,0:T(8,128)(2,1)} %get-tuple-element.23), calls=%async_computation.1 | async-start | bytes 2949120 | tf_op jit(solution)/shard_map/all_to_all | solution.py:446
  28.1 5.4 %collective-permute-done.1.summed_ref.after_ref = f32[24,128]{1,0:T(8,128)S(1)} collective-permute-done((f32[24,128]{1,0:T(8,128)S(1)}, f32[24,128]{1,0:T(8,128)S(1)}, u32[]{:S(2)}, u32[]{:S(2)}) %collective-permute-start.1) | collective-permute-done | bytes 12320 | tf_op jit(solution)/shard_map/ppermute | solution.py:21
  33.5 0.0 collective-permute-done.raw_ref
  33.5 1.4 %copy-done.7 = bf16[45,128,128]{2,1,0:T(8,128)(2,1)S(1)} copy-done((bf16[45,128,128]{2,1,0:T(8,128)(2,1)S(1)}, bf16[45,128,128]{2,1,0:T(8,128)(2,1)}, u32[]{:S(2)}) %copy-start.7) | copy-done | bytes 1474584
  34.9 3.8 %cross_next.1 = (bf16[1440,128]{1,0:T(8,128)(2,1)}, bf16[1440,128]{1,0:T(8,128)(2,1)}, bf16[1440,128]{1,0:T(8,128)(2,1)}, bf16[1440,128]{1,0:T(8,128)(2,1)}, bf1...) custom-call(s32[1]{0:T(128)} %bitcast.group_ref, ...), custom_call_target="tpu_custom_call" | custom-call | flops 20000000000 | bytes 6000000 | tf_op jit(solution)/shard_map/cross_next/pallas_call | solution.py:197
  38.7 1.4 %collective-permute-start.2 = (bf16[1440,128]{1,0:T(8,128)(2,1)}, bf16[1440,128]{1,0:T(8,128)(2,1)S(1)}, u32[]{:S(2)}, u32[]{:S(2)}) collective-permute-start(bf16[1440,128]{1,0:T(8,128)(2,1)} %get-tuple-element.27), channel_id=1, source_target_pairs={{7,0},{0,1},{1,2},{2,3},{3,4},{4,5},{5,6},{6,7},{15,8},{8,9},{9,10... | collective-permute-start | bytes 1105928 | tf_op jit(solution)/shard_map/ppermute | solution.py:21
  40.0 13.3 %collective-permute-start.3 = (bf16[1440,128]{1,0:T(8,128)(2,1)}, bf16[1440,128]{1,0:T(8,128)(2,1)S(1)}, u32[]{:S(2)}, u32[]{:S(2)}) collective-permute-start(bf16[1440,128]{1,0:T(8,128)(2,1)} %get-tuple-element.28), channel_id=1, source_target_pairs={{6,0},{7,1},{0,2},{1,3},{2,4},{3,5},{4,6},{5,7},{14,8},{15,9},{8,1... | collective-permute-start | bytes 1105928 | tf_op jit(solution)/shard_map/ppermute | solution.py:21
  53.3 2.4 %collective-permute-start.4 = (bf16[1440,128]{1,0:T(8,128)(2,1)}, bf16[1440,128]{1,0:T(8,128)(2,1)}, u32[]{:S(2)}, u32[]{:S(2)}) collective-permute-start(bf16[1440,128]{1,0:T(8,128)(2,1)} %get-tuple-element.29), channel_id=1, source_target_pairs={{5,0},{6,1},{7,2},{0,3},{1,4},{2,5},{3,6},{4,7},{13,8},{14,9},{15,... | collective-permute-start | bytes 1105928 | tf_op jit(solution)/shard_map/ppermute | solution.py:21
  55.7 0.8 collective-permute-start.5
  56.5 0.0 collective-permute-start.6
  56.5 10.1 %collective-permute-done.2.refs_1_ = bf16[1440,128]{1,0:T(8,128)(2,1)S(1)} collective-permute-done((bf16[1440,128]{1,0:T(8,128)(2,1)}, bf16[1440,128]{1,0:T(8,128)(2,1)S(1)}, u32[]{:S(2)}, u32[]{:S(2)}) %collective-permute-start.2) | collective-permute-done | bytes 368672 | tf_op jit(solution)/shard_map/ppermute | solution.py:21
  66.6 5.0 %collective-permute-start.7 = (bf16[1440,128]{1,0:T(8,128)(2,1)}, bf16[1440,128]{1,0:T(8,128)(2,1)}, u32[]{:S(2)}, u32[]{:S(2)}) collective-permute-start(bf16[1440,128]{1,0:T(8,128)(2,1)} %get-tuple-element.32), channel_id=1, source_target_pairs={{2,0},{3,1},{4,2},{5,3},{6,4},{7,5},{0,6},{1,7},{10,8},{11,9},{12,... | collective-permute-start | bytes 1105928 | tf_op jit(solution)/shard_map/ppermute | solution.py:21
  71.6 0.0 collective-permute-done.3.refs_2_
  71.6 0.8 copy-done.2
  72.4 0.2 collective-permute-start.8
  72.6 4.9 %fusion.6.trig_ref = bf16[360,768]{1,0:T(8,128)(2,1)S(1)} fusion(s32[768]{0:T(1024)S(1)} %fusion.15, pred[768]{0:T(1024)(128)(4,1)S(1)} %get-tuple-element.40, pred[768]{0:T(1024)(128)(4,1)S(1)} %get-tuple-element.41), kind=kLoop, calls=%fused_computation.10 | loop fusion | flops 3870720 | bytes 557568 | tf_op jit(solution)/shard_map/jit(_where)/select_n | solution.py:37
  77.6 0.0 copy-start.1
  77.6 0.0 all-to-all-done.1.terms_ref
  77.6 0.0 copy-start.3
  77.6 1.4 %own_part.1 = (f32[8,128]{1,0:T(8,128)S(1)}, f32[1,128]{1,0:T(1,128)S(1)}) custom-call(s32[1]{0:T(128)} %bitcast.group_ref, bf16[8,720,128]{2,1,0:T(8,128)(2,1)S(1)} %all-to-all-done.1.terms_ref, bf16[360,768]{1,0:T(8,128)(2,1)S(1)} %fusion.6.trig_ref), custom_call_target="tpu_custom_call" | custom-call | tf_op jit(solution)/shard_map/own_part/pallas_call | solution.py:273
  79.0 0.0 collective-permute-done.4.refs_3_
  79.0 0.0 copy-done.3
  79.1 2.7 %first_part.1.share_ref = f32[360,2048]{1,0:T(8,128)S(1)} custom-call(bf16[360,768]{1,0:T(8,128)(2,1)S(1)} %fusion.6.trig_ref, bf16[1440,128]{1,0:T(8,128)(2,1)S(1)} %copy-done.1, bf16[1440,128]{1,0:T(8,128)(2,1)S(1)} %collective-permute-done.2.refs_1_, bf16[1440,128]{1,0:T(8,128)(2,1)S(1)} %copy-done.3, bf16[1440,128]{1,0:T(8,128)(2,1)} %collective-permute-done.4.refs_3_), custom_call_target="tpu_custom_call" | custom-call | tf_op jit(solution)/shard_map/first_part/pallas_call | solution.py:301
  81.7 0.0 collective-permute-done.5.refs_0_
  81.8 0.0 collective-permute-done.6.refs_1_
  81.8 0.0 collective-permute-done.7.refs_2_
  81.8 5.2 %collective-permute-done.8.refs_3_ = bf16[1440,128]{1,0:T(8,128)(2,1)} collective-permute-done((bf16[1440,128]{1,0:T(8,128)(2,1)}, bf16[1440,128]{1,0:T(8,128)(2,1)}, u32[]{:S(2)}, u32[]{:S(2)}) %collective-permute-start.8) | collective-permute-done | bytes 368672 | tf_op jit(solution)/shard_map/ppermute | solution.py:21
  86.9 3.2 %next_part.1 = f32[40,128]{1,0:T(8,128)S(1)} custom-call(s32[1]{0:T(128)} %bitcast.group_ref, bf16[360,768]{1,0:T(8,128)(2,1)S(1)} %fusion.6.trig_ref, f32[1,128]{1,0:T(1,128)S(1)} %get-tuple-element.24.degree_ref, f32[24,128]{1,0:T(8,128)S(1)} %reduce_sum.9.summed_ref.here_ref, f32[360,2048]{1,0:T(8,128)S(1)} %first_part.1.share_ref, ...), custom_call_target="tpu_custom_call" | custom-call | tf_op jit(solution)/shard_map/next_part/pallas_call | solution.py:339
  90.1 0.0 collective-permute-start.9
  90.2 1.6 %collective-permute-start.11 = (f32[8,128]{1,0:T(8,128)S(1)}, f32[8,128]{1,0:T(8,128)S(1)}, u32[]{:S(2)}, u32[]{:S(2)}) collective-permute-start(f32[8,128]{1,0:T(8,128)S(1)} %slice.40), channel_id=1, source_target_pairs={{8,0},{16,8},{24,16},{32,24},{40,32},{48,40},{56,48},{64,56},{72,6... | collective-permute-start | bytes 12296 | tf_op jit(solution)/shard_map/ppermute | solution.py:21
  91.8 0.0 collective-permute-start.10
  91.8 0.6 collective-permute-done.9.before_ref
  92.4 2.4 %collective-permute-done.11 = f32[8,128]{1,0:T(8,128)S(1)} collective-permute-done((f32[8,128]{1,0:T(8,128)S(1)}, f32[8,128]{1,0:T(8,128)S(1)}, u32[]{:S(2)}, u32[]{:S(2)}) %collective-permute-start.11) | collective-permute-done | bytes 4128 | tf_op jit(solution)/shard_map/ppermute | solution.py:21
  94.8 9.2 %collective-permute-done.10 = f32[8,128]{1,0:T(8,128)S(1)} collective-permute-done((f32[8,128]{1,0:T(8,128)S(1)}, f32[8,128]{1,0:T(8,128)S(1)}, u32[]{:S(2)}, u32[]{:S(2)}) %collective-permute-start.10) | collective-permute-done | bytes 4128 | tf_op jit(solution)/shard_map/ppermute | solution.py:21
  104.0 8.2 %all_to_all.26.parts_ref = f32[8,48,128]{2,1,0:T(8,128)S(1)} all-to-all(f32[8,48,128]{2,1,0:T(8,128)S(1)} %broadcast_in_dim.37), channel_id=1, replica_groups=mesh['blk'=32,'grp'=8] {'grp'}, dimensions={0} | all-to-all | bytes 393216 | tf_op jit(solution)/shard_map/all_to_all | solution.py:468
  112.2 0.6 image_part.1
  112.8 0.6 copy-done.4
  113.4 19.4 %all_to_all.27 = f32[32,1,128]{2,1,0:T(1,128)} all-to-all(f32[32,1,128]{2,1,0:T(1,128)S(1)} %bitcast.7), channel_id=1, replica_groups=mesh['blk'=32,'grp'=8] {'blk'}, dimensions={0} | all-to-all | bytes 32768 | tf_op jit(solution)/shard_map/all_to_all | solution.py:470
  132.8 1.6 %final_part.1 = f32[16,16]{1,0:T(8,128)} custom-call(f32[32,128]{1,0:T(8,128)} %bitcast.8, f32[2,16,16]{2,1,0:T(8,128)} %copy-done.4), custom_call_target="tpu_custom_call" | custom-call | tf_op jit(solution)/shard_map/final_part/pallas_call | solution.py:423
  (17 shorter events, 0.2 us)
Async XLA Ops:
  0.0 1.4 %copy-start = (bf16[128,45,128]{2,0,1:T(8,128)(2,1)S(1)}, bf16[128,45,128]{2,0,1:T(8,128)(2,1)}, u32[]{:S(2)}) copy-start(bf16[128,45,128]{2,0,1:T(8,128)(2,1)} %param.2) | copy-start | bytes 4423684
  1.4 0.7 copy-start.5
  4.2 11.2 %all-to-all-start = ((f32[8,24,128]{2,1,0:T(8,128)}), f32[8,24,128]{2,1,0:T(8,128)S(1)}, u32[]{:S(2)}, u32[]{:S(2)}) async-start(f32[8,24,128]{2,1,0:T(8,128)} %get-tuple-element.22), calls=%async_computation | async-start | bytes 196608 | tf_op jit(solution)/shard_map/all_to_all | solution.py:442
  10.0 23.5 %collective-permute-start = (bf16[45,128,128]{2,1,0:T(8,128)(2,1)}, bf16[45,128,128]{2,1,0:T(8,128)(2,1)S(1)}, u32[]{:S(2)}, u32[]{:S(2)}) collective-permute-start(bf16[45,128,128]{2,1,0:T(8,128)(2,1)} %get-tuple-element.21.raw_ref), channel_id=1, source_target_pairs={{8,0},{16,8},{24,16},{32,24},{40,32},{48,40},{56,48},{64,56},{72,6... | collective-permute-start | bytes 4423688 | tf_op jit(solution)/shard_map/ppermute | solution.py:21
  15.4 18.1 %collective-permute-start.1 = (f32[24,128]{1,0:T(8,128)S(1)}, f32[24,128]{1,0:T(8,128)S(1)}, u32[]{:S(2)}, u32[]{:S(2)}) collective-permute-start(f32[24,128]{1,0:T(8,128)S(1)} %reduce_sum.9.summed_ref.here_ref), channel_id=1, source_target_pairs={{8,0},{16,8},{24,16},{32,24},{40,32},{48,40},{56,48},{64,56},{72,6... | collective-permute-start | bytes 36872 | tf_op jit(solution)/shard_map/ppermute | solution.py:21
  18.4 1.4 %copy-start.6 = (bf16[45,128,128]{2,1,0:T(8,128)(2,1)S(1)}, bf16[45,128,128]{2,1,0:T(8,128)(2,1)}, u32[]{:S(2)}) copy-start(bf16[45,128,128]{2,1,0:T(8,128)(2,1)} %get-tuple-element.21.raw_ref) | copy-start | bytes 4423684
  23.6 54.0 %all-to-all-start.1 = ((bf16[8,720,128]{2,1,0:T(8,128)(2,1)}), bf16[8,720,128]{2,1,0:T(8,128)(2,1)S(1)}, u32[]{:S(2)}, u32[]{:S(2)}) async-start(bf16[8,720,128]{2,1,0:T(8,128)(2,1)} %get-tuple-element.23), calls=%async_computation.1 | async-start | bytes 2949120 | tf_op jit(solution)/shard_map/all_to_all | solution.py:446
  33.5 1.4 %copy-start.7 = (bf16[45,128,128]{2,1,0:T(8,128)(2,1)S(1)}, bf16[45,128,128]{2,1,0:T(8,128)(2,1)}, u32[]{:S(2)}) copy-start(bf16[45,128,128]{2,1,0:T(8,128)(2,1)} %get-tuple-element.25.unit_ref) | copy-start | bytes 4423684
  38.7 27.9 %collective-permute-start.2 = (bf16[1440,128]{1,0:T(8,128)(2,1)}, bf16[1440,128]{1,0:T(8,128)(2,1)S(1)}, u32[]{:S(2)}, u32[]{:S(2)}) collective-permute-start(bf16[1440,128]{1,0:T(8,128)(2,1)} %get-tuple-element.27), channel_id=1, source_target_pairs={{7,0},{0,1},{1,2},{2,3},{3,4},{4,5},{5,6},{6,7},{15,8},{8,9},{9,10... | collective-permute-start | bytes 1105928 | tf_op jit(solution)/shard_map/ppermute | solution.py:21
  40.0 31.6 %collective-permute-start.3 = (bf16[1440,128]{1,0:T(8,128)(2,1)}, bf16[1440,128]{1,0:T(8,128)(2,1)S(1)}, u32[]{:S(2)}, u32[]{:S(2)}) collective-permute-start(bf16[1440,128]{1,0:T(8,128)(2,1)} %get-tuple-element.28), channel_id=1, source_target_pairs={{6,0},{7,1},{0,2},{1,3},{2,4},{3,5},{4,6},{5,7},{14,8},{15,9},{8,1... | collective-permute-start | bytes 1105928 | tf_op jit(solution)/shard_map/ppermute | solution.py:21
  53.3 25.7 %collective-permute-start.4 = (bf16[1440,128]{1,0:T(8,128)(2,1)}, bf16[1440,128]{1,0:T(8,128)(2,1)}, u32[]{:S(2)}, u32[]{:S(2)}) collective-permute-start(bf16[1440,128]{1,0:T(8,128)(2,1)} %get-tuple-element.29), channel_id=1, source_target_pairs={{5,0},{6,1},{7,2},{0,3},{1,4},{2,5},{3,6},{4,7},{13,8},{14,9},{15,... | collective-permute-start | bytes 1105928 | tf_op jit(solution)/shard_map/ppermute | solution.py:21
  55.7 26.0 %collective-permute-start.5 = (bf16[1440,128]{1,0:T(8,128)(2,1)}, bf16[1440,128]{1,0:T(8,128)(2,1)S(1)}, u32[]{:S(2)}, u32[]{:S(2)}) collective-permute-start(bf16[1440,128]{1,0:T(8,128)(2,1)} %get-tuple-element.30), channel_id=1, source_target_pairs={{4,0},{5,1},{6,2},{7,3},{0,4},{1,5},{2,6},{3,7},{12,8},{13,9},{14,... | collective-permute-start | bytes 1105928 | tf_op jit(solution)/shard_map/ppermute | solution.py:21
  56.5 25.3 %collective-permute-start.6 = (bf16[1440,128]{1,0:T(8,128)(2,1)}, bf16[1440,128]{1,0:T(8,128)(2,1)S(1)}, u32[]{:S(2)}, u32[]{:S(2)}) collective-permute-start(bf16[1440,128]{1,0:T(8,128)(2,1)} %get-tuple-element.31), channel_id=1, source_target_pairs={{3,0},{4,1},{5,2},{6,3},{7,4},{0,5},{1,6},{2,7},{11,8},{12,9},{13,... | collective-permute-start | bytes 1105928 | tf_op jit(solution)/shard_map/ppermute | solution.py:21
  66.6 15.2 %collective-permute-start.7 = (bf16[1440,128]{1,0:T(8,128)(2,1)}, bf16[1440,128]{1,0:T(8,128)(2,1)}, u32[]{:S(2)}, u32[]{:S(2)}) collective-permute-start(bf16[1440,128]{1,0:T(8,128)(2,1)} %get-tuple-element.32), channel_id=1, source_target_pairs={{2,0},{3,1},{4,2},{5,3},{6,4},{7,5},{0,6},{1,7},{10,8},{11,9},{12,... | collective-permute-start | bytes 1105928 | tf_op jit(solution)/shard_map/ppermute | solution.py:21
  71.6 0.8 copy-start.2
  72.4 14.6 %collective-permute-start.8 = (bf16[1440,128]{1,0:T(8,128)(2,1)}, bf16[1440,128]{1,0:T(8,128)(2,1)}, u32[]{:S(2)}, u32[]{:S(2)}) collective-permute-start(bf16[1440,128]{1,0:T(8,128)(2,1)} %get-tuple-element.33), channel_id=1, source_target_pairs={{1,0},{2,1},{3,2},{4,3},{5,4},{6,5},{7,6},{0,7},{9,8},{10,9},{11,1... | collective-permute-start | bytes 1105928 | tf_op jit(solution)/shard_map/ppermute | solution.py:21
  77.6 1.5 %copy-start.1 = (bf16[1440,128]{1,0:T(8,128)(2,1)S(1)}, bf16[1440,128]{1,0:T(8,128)(2,1)}, u32[]{:S(2)}) copy-start(bf16[1440,128]{1,0:T(8,128)(2,1)} %get-tuple-element.26.refs_0_) | copy-start | bytes 1105924
  77.6 1.5 %copy-start.3 = (bf16[1440,128]{1,0:T(8,128)(2,1)S(1)}, bf16[1440,128]{1,0:T(8,128)(2,1)}, u32[]{:S(2)}) copy-start(bf16[1440,128]{1,0:T(8,128)(2,1)} %copy-done.2) | copy-start | bytes 1105924
  90.1 2.3 %collective-permute-start.9 = (f32[40,128]{1,0:T(8,128)S(1)}, f32[40,128]{1,0:T(8,128)S(1)}, u32[]{:S(2)}, u32[]{:S(2)}) collective-permute-start(f32[40,128]{1,0:T(8,128)S(1)} %next_part.1), channel_id=1, source_target_pairs={{248,0},{0,8},{8,16},{16,24},{24,32},{32,40},{40,48},{48,56},{56,6... | collective-permute-start | bytes 61448 | tf_op jit(solution)/shard_map/ppermute | solution.py:21
  90.2 4.6 %collective-permute-start.11 = (f32[8,128]{1,0:T(8,128)S(1)}, f32[8,128]{1,0:T(8,128)S(1)}, u32[]{:S(2)}, u32[]{:S(2)}) collective-permute-start(f32[8,128]{1,0:T(8,128)S(1)} %slice.40), channel_id=1, source_target_pairs={{8,0},{16,8},{24,16},{32,24},{40,32},{48,40},{56,48},{64,56},{72,6... | collective-permute-start | bytes 12296 | tf_op jit(solution)/shard_map/ppermute | solution.py:21
  91.8 12.1 %collective-permute-start.10 = (f32[8,128]{1,0:T(8,128)S(1)}, f32[8,128]{1,0:T(8,128)S(1)}, u32[]{:S(2)}, u32[]{:S(2)}) collective-permute-start(f32[8,128]{1,0:T(8,128)S(1)} %slice.40), channel_id=1, source_target_pairs={{240,0},{248,8},{0,16},{8,24},{16,32},{24,40},{32,48},{40,56},{48,... | collective-permute-start | bytes 12296 | tf_op jit(solution)/shard_map/ppermute | solution.py:21
  112.8 0.6 copy-start.4

commit v8 on v6

--- a/solution.py
+++ b/solution.py
@@ -440,9 +440,9 @@
     summed = jnp.sum(lax.all_to_all(begun, "grp", 0, 0, tiled=True), axis=0)
     after_raw = passed_along(by_freq, "blk", -1)
     summed_after = passed_along(summed, "blk", -1)
-    own_terms, own_unit = cross_own(by_freq, summed, group_size, 5)
+    own_terms, own_unit = cross_own(by_freq, summed, group_size, 9)
     own_terms = lax.all_to_all(own_terms, "grp", 0, 0, tiled=True)
-    next_terms = cross_next(group_index, own_unit, after_raw, summed_after, group_size, 5)
+    next_terms = cross_next(group_index, own_unit, after_raw, summed_after, group_size, 9)
     next_terms = [next_terms[0]] + [passed_along(next_terms[r], "grp", r) for r in range(1, group_size)]
     own_aff = own_part(group_index, own_terms, trig, factor)
     share = first_part(next_terms[: group_size // 2], trig)

time: 135 us -> 138 us (1.022)
  starting transfers between devices: 39 us -> 31.8 us
  blocking collectives: 27.6 us -> 31.9 us
  Pallas kernels: 18.3 us -> 21.5 us
  waiting for transfers between devices: 39.2 us -> 42.1 us
    ppermute x12, starting transfers between devices: 28.6 us -> 21.4 us  [passed_along(): return lax.ppermute(block, axis, route)]
    ppermute x12, waiting for transfers between devices: 34.8 us -> 37.7 us  [passed_along(): return lax.ppermute(block, axis, route)]
    all_to_all x1, blocking collectives: 19.4 us -> 21.8 us  [per_device(): stats = lax.all_to_all(stats, 'blk', 0, 0, tiled=True)]
    all_to_all x1, blocking collectives: 8.19 us -> 10.2 us  [per_device(): parts = lax.all_to_all(sent, 'grp', 0, 0, tiled=True)]
    pallas_call x1, Pallas kernels: 3.77 us -> 5.37 us  [cross_own(): pl.pallas_call(functools.partial(cross_own_kernel, freq * parts * channel...]
    pallas_call x1, Pallas kernels: 3.76 us -> 5.33 us  [cross_next(): pl.pallas_call(functools.partial(cross_next_kernel, freq * parts * channe...]
  transfers between devices with their start and end apart: 14 -> 14, of which waited for: 8 -> 8; matrix products, arithmetic and copies ran while one was open for 4% -> 4% of each run, Pallas kernels for 8% -> 10%
where the time goes in v8:
time: 138 us
  waiting for transfers between devices  42.1 us (31%)
  blocking collectives  31.9 us (23%)
  starting transfers between devices  31.8 us (23%)
  Pallas kernels  21.5 us (16%)
  local copies, waits for them, and re-layouts  5.47 us (4%)
  other arithmetic  5 us (4%)
    ppermute x12, waiting for transfers between devices, passed_along(): return lax.ppermute(block, axis, route)  37.7 us
    all_to_all x1, blocking collectives, per_device(): stats = lax.all_to_all(stats, 'blk', 0, 0, tiled=True)  21.8 us
    ppermute x12, starting transfers between devices, passed_along(): return lax.ppermute(block, axis, route)  21.4 us
    all_to_all x1, blocking collectives, per_device(): parts = lax.all_to_all(sent, 'grp', 0, 0, tiled=True)  10.2 us
    all_to_all x1, starting transfers between devices, per_device(): summed = jnp.sum(lax.all_to_all(begun, 'grp', 0, 0, tiled=True), axis=0)  5.86 us
    unnamed x12, local copies, waits for them, and re-layouts  5.42 us
    pallas_call x1, Pallas kernels, cross_own(): pl.pallas_call(functools.partial(cross_own_kernel, freq * parts * channel...  5.37 us
    pallas_call x1, Pallas kernels, cross_next(): pl.pallas_call(functools.partial(cross_next_kernel, freq * parts * channe...  5.33 us
  transfers between devices with their start and end apart: 14, of which 8 were waited for; matrix products, arithmetic and copies ran while one was open for 4% of the time, Pallas kernels for 10%

profile of v8, /device:TPU:1, one launch (start us, length us, event | category | flops | bytes accessed | tf_op | source)
XLA Modules:
  0.0 138.0 jit_solution(7401707246378272329)
XLA Ops:
  0.0 0.0 copy-start
  0.0 1.4 copy-done
  1.4 0.7 copy-done.3
  2.1 2.1 %start.1 = (f32[8,24,128]{2,1,0:T(8,128)}, bf16[45,128,128]{2,1,0:T(8,128)(2,1)}) custom-call(s32[1]{0:T(128)} %bitcast.group_ref, bf16[45,128,128]{2,1,0:T(8,128)(2,1)S(1)} %bitcast.6, f32[16,16]{1,0:T(8,128)S(1)} %copy-done.3), custom_call_target="tpu_custom_call" | custom-call | tf_op jit(solution)/shard_map/start/pallas_call | solution.py:78
  4.2 5.9 %all-to-all-start = ((f32[8,24,128]{2,1,0:T(8,128)}), f32[8,24,128]{2,1,0:T(8,128)S(1)}, u32[]{:S(2)}, u32[]{:S(2)}) async-start(f32[8,24,128]{2,1,0:T(8,128)} %get-tuple-element.20), calls=%async_computation | async-start | bytes 196608 | tf_op jit(solution)/shard_map/all_to_all | solution.py:440
  10.0 1.0 collective-permute-start
  11.0 4.4 %all-to-all-done = f32[8,24,128]{2,1,0:T(8,128)S(1)} async-done(((f32[8,24,128]{2,1,0:T(8,128)}), f32[8,24,128]{2,1,0:T(8,128)S(1)}, u32[]{:S(2)}, u32[]{:S(2)}) %all-to-all-start) | async-done | bytes 98336 | tf_op jit(solution)/shard_map/all_to_all | solution.py:440
  15.4 3.1 %collective-permute-start.1 = (f32[24,128]{1,0:T(8,128)S(1)}, f32[24,128]{1,0:T(8,128)S(1)}, u32[]{:S(2)}, u32[]{:S(2)}) collective-permute-start(f32[24,128]{1,0:T(8,128)S(1)} %reduce_sum.9.summed_ref.here_ref), channel_id=1, source_target_pairs={{8,0},{16,8},{24,16},{32,24},{40,32},{48,40},{56,48},{64,56},{72,6... | collective-permute-start | bytes 36872 | tf_op jit(solution)/shard_map/ppermute | solution.py:21
  18.4 1.4 copy-done.4
  19.8 5.4 %cross_own.1 = (bf16[8,720,128]{2,1,0:T(8,128)(2,1)}, bf16[45,128,128]{2,1,0:T(8,128)(2,1)}) custom-call(bf16[45,128,128]{2,1,0:T(8,128)(2,1)S(1)} %copy-done.4, f32[24,128]{1,0:T(8,128)S(1)} %reduce_sum.9.summed_ref.here_ref), custom_call_target="tpu_custom_call" | custom-call | flops 20000000000 | bytes 6000000 | tf_op jit(solution)/shard_map/cross_own/pallas_call | solution.py:157
  25.2 4.5 %all-to-all-start.1 = ((bf16[8,720,128]{2,1,0:T(8,128)(2,1)}), bf16[8,720,128]{2,1,0:T(8,128)(2,1)S(1)}, u32[]{:S(2)}, u32[]{:S(2)}) async-start(bf16[8,720,128]{2,1,0:T(8,128)(2,1)} %get-tuple-element.21), calls=%async_computation.1 | async-start | bytes 2949120 | tf_op jit(solution)/shard_map/all_to_all | solution.py:444
  29.7 2.2 %collective-permute-done.1.summed_ref.after_ref = f32[24,128]{1,0:T(8,128)S(1)} collective-permute-done((f32[24,128]{1,0:T(8,128)S(1)}, f32[24,128]{1,0:T(8,128)S(1)}, u32[]{:S(2)}, u32[]{:S(2)}) %collective-permute-start.1) | collective-permute-done | bytes 12320 | tf_op jit(solution)/shard_map/ppermute | solution.py:21
  31.9 0.0 collective-permute-done.raw_ref
  31.9 1.4 copy-done.5
  33.3 5.3 %cross_next.1 = (bf16[1440,128]{1,0:T(8,128)(2,1)}, bf16[1440,128]{1,0:T(8,128)(2,1)}, bf16[1440,128]{1,0:T(8,128)(2,1)}, bf16[1440,128]{1,0:T(8,128)(2,1)}, bf1...) custom-call(s32[1]{0:T(128)} %bitcast.group_ref, ...), custom_call_target="tpu_custom_call" | custom-call | flops 20000000000 | bytes 6000000 | tf_op jit(solution)/shard_map/cross_next/pallas_call | solution.py:197
  38.6 1.4 collective-permute-start.2
  40.0 6.2 %collective-permute-start.3 = (bf16[1440,128]{1,0:T(8,128)(2,1)}, bf16[1440,128]{1,0:T(8,128)(2,1)S(1)}, u32[]{:S(2)}, u32[]{:S(2)}) collective-permute-start(bf16[1440,128]{1,0:T(8,128)(2,1)} %get-tuple-element.25), channel_id=1, source_target_pairs={{6,0},{7,1},{0,2},{1,3},{2,4},{3,5},{4,6},{5,7},{14,8},{15,9},{8,1... | collective-permute-start | bytes 1105928 | tf_op jit(solution)/shard_map/ppermute | solution.py:21
  46.2 2.3 %collective-permute-start.4 = (bf16[1440,128]{1,0:T(8,128)(2,1)}, bf16[1440,128]{1,0:T(8,128)(2,1)S(1)}, u32[]{:S(2)}, u32[]{:S(2)}) collective-permute-start(bf16[1440,128]{1,0:T(8,128)(2,1)} %get-tuple-element.26), channel_id=1, source_target_pairs={{5,0},{6,1},{7,2},{0,3},{1,4},{2,5},{3,6},{4,7},{13,8},{14,9},{15,... | collective-permute-start | bytes 1105928 | tf_op jit(solution)/shard_map/ppermute | solution.py:21
  48.5 0.4 collective-permute-start.5
  48.8 0.3 collective-permute-start.6
  49.2 22.8 %collective-permute-done.2.refs_1_ = bf16[1440,128]{1,0:T(8,128)(2,1)S(1)} collective-permute-done((bf16[1440,128]{1,0:T(8,128)(2,1)}, bf16[1440,128]{1,0:T(8,128)(2,1)S(1)}, u32[]{:S(2)}, u32[]{:S(2)}) %collective-permute-start.2) | collective-permute-done | bytes 368672 | tf_op jit(solution)/shard_map/ppermute | solution.py:21
  71.9 0.0 collective-permute-start.7
  72.0 0.0 collective-permute-done.3.refs_2_
  72.0 0.0 collective-permute-start.8
  72.0 4.9 %fusion.6.trig_ref = bf16[360,768]{1,0:T(8,128)(2,1)S(1)} fusion(s32[768]{0:T(1024)S(1)} %fusion.15, pred[768]{0:T(1024)(128)(4,1)S(1)} %get-tuple-element.36, pred[768]{0:T(1024)(128)(4,1)S(1)} %get-tuple-element.37), kind=kLoop, calls=%fused_computation.10 | loop fusion | flops 3870720 | bytes 557568 | tf_op jit(solution)/shard_map/jit(_where)/select_n | solution.py:37
  77.0 0.0 copy-start.1
  77.0 0.0 all-to-all-done.1.terms_ref
  77.0 1.2 own_part.1.own_ref
  78.2 0.0 collective-permute-done.4.refs_3_
  78.2 0.0 copy-done.1
  78.2 1.7 %first_part.1.share_ref = f32[360,2048]{1,0:T(8,128)S(1)} custom-call(bf16[360,768]{1,0:T(8,128)(2,1)S(1)} %fusion.6.trig_ref, bf16[1440,128]{1,0:T(8,128)(2,1)S(1)} %copy-done.1, bf16[1440,128]{1,0:T(8,128)(2,1)S(1)} %collective-permute-done.2.refs_1_, bf16[1440,128]{1,0:T(8,128)(2,1)S(1)} %collective-permute-done.3.refs_2_, ...), custom_call_target="tpu_custom_call" | custom-call | tf_op jit(solution)/shard_map/first_part/pallas_call | solution.py:290
  80.0 2.5 %collective-permute-done.5.refs_0_ = bf16[1440,128]{1,0:T(8,128)(2,1)} collective-permute-done((bf16[1440,128]{1,0:T(8,128)(2,1)}, bf16[1440,128]{1,0:T(8,128)(2,1)}, u32[]{:S(2)}, u32[]{:S(2)}) %collective-permute-start.5) | collective-permute-done | bytes 368672 | tf_op jit(solution)/shard_map/ppermute | solution.py:21
  82.5 2.9 %collective-permute-done.6.refs_1_ = bf16[1440,128]{1,0:T(8,128)(2,1)} collective-permute-done((bf16[1440,128]{1,0:T(8,128)(2,1)}, bf16[1440,128]{1,0:T(8,128)(2,1)}, u32[]{:S(2)}, u32[]{:S(2)}) %collective-permute-start.6) | collective-permute-done | bytes 368672 | tf_op jit(solution)/shard_map/ppermute | solution.py:21
  85.4 0.0 collective-permute-done.7.refs_2_
  85.4 2.4 %collective-permute-done.8.refs_3_ = bf16[1440,128]{1,0:T(8,128)(2,1)} collective-permute-done((bf16[1440,128]{1,0:T(8,128)(2,1)}, bf16[1440,128]{1,0:T(8,128)(2,1)}, u32[]{:S(2)}, u32[]{:S(2)}) %collective-permute-start.8) | collective-permute-done | bytes 368672 | tf_op jit(solution)/shard_map/ppermute | solution.py:21
  87.8 3.6 %next_part.1 = f32[40,128]{1,0:T(8,128)S(1)} custom-call(s32[1]{0:T(128)} %bitcast.group_ref, bf16[360,768]{1,0:T(8,128)(2,1)S(1)} %fusion.6.trig_ref, f32[8,128]{1,0:T(8,128)S(1)} %own_part.1.own_ref, f32[24,128]{1,0:T(8,128)S(1)} %reduce_sum.9.summed_ref.here_ref, f32[360,2048]{1,0:T(8,128)S(1)} %first_part.1.share_ref, ...), custom_call_target="tpu_custom_call" | custom-call | tf_op jit(solution)/shard_map/next_part/pallas_call | solution.py:337
  91.4 5.5 %collective-permute-start.9 = (f32[40,128]{1,0:T(8,128)S(1)}, f32[40,128]{1,0:T(8,128)S(1)}, u32[]{:S(2)}, u32[]{:S(2)}) collective-permute-start(f32[40,128]{1,0:T(8,128)S(1)} %next_part.1), channel_id=1, source_target_pairs={{248,0},{0,8},{8,16},{16,24},{24,32},{32,40},{40,48},{48,56},{56,6... | collective-permute-start | bytes 61448 | tf_op jit(solution)/shard_map/ppermute | solution.py:21
  96.9 0.0 collective-permute-start.11
  96.9 1.4 collective-permute-start.10
  98.3 0.0 collective-permute-done.9.before_ref
  98.3 3.2 %collective-permute-done.11 = f32[8,128]{1,0:T(8,128)S(1)} collective-permute-done((f32[8,128]{1,0:T(8,128)S(1)}, f32[8,128]{1,0:T(8,128)S(1)}, u32[]{:S(2)}, u32[]{:S(2)}) %collective-permute-start.11) | collective-permute-done | bytes 4128 | tf_op jit(solution)/shard_map/ppermute | solution.py:21
  101.5 1.7 %collective-permute-done.10 = f32[8,128]{1,0:T(8,128)S(1)} collective-permute-done((f32[8,128]{1,0:T(8,128)S(1)}, f32[8,128]{1,0:T(8,128)S(1)}, u32[]{:S(2)}, u32[]{:S(2)}) %collective-permute-start.10) | collective-permute-done | bytes 4128 | tf_op jit(solution)/shard_map/ppermute | solution.py:21
  103.2 10.2 %all_to_all.26.parts_ref = f32[8,48,128]{2,1,0:T(8,128)S(1)} all-to-all(f32[8,48,128]{2,1,0:T(8,128)S(1)} %broadcast_in_dim.37), channel_id=1, replica_groups=mesh['blk'=32,'grp'=8] {'grp'}, dimensions={0} | all-to-all | bytes 393216 | tf_op jit(solution)/shard_map/all_to_all | solution.py:466
  113.4 0.6 image_part.1
  114.0 0.0 copy-start.2
  114.0 0.6 copy-done.2
  114.6 21.8 %all_to_all.27 = f32[32,1,128]{2,1,0:T(1,128)} all-to-all(f32[32,1,128]{2,1,0:T(1,128)S(1)} %bitcast.7), channel_id=1, replica_groups=mesh['blk'=32,'grp'=8] {'blk'}, dimensions={0} | all-to-all | bytes 32768 | tf_op jit(solution)/shard_map/all_to_all | solution.py:468
  136.4 1.6 %final_part.1 = f32[16,16]{1,0:T(8,128)} custom-call(f32[32,128]{1,0:T(8,128)} %bitcast.8, f32[2,16,16]{2,1,0:T(8,128)} %copy-done.2), custom_call_target="tpu_custom_call" | custom-call | tf_op jit(solution)/shard_map/final_part/pallas_call | solution.py:421
  (13 shorter events, 0.1 us)
Async XLA Ops:
  0.0 1.4 copy-start
  1.4 0.7 copy-start.3
  4.2 11.2 %all-to-all-start = ((f32[8,24,128]{2,1,0:T(8,128)}), f32[8,24,128]{2,1,0:T(8,128)S(1)}, u32[]{:S(2)}, u32[]{:S(2)}) async-start(f32[8,24,128]{2,1,0:T(8,128)} %get-tuple-element.20), calls=%async_computation | async-start | bytes 196608 | tf_op jit(solution)/shard_map/all_to_all | solution.py:440
  10.0 21.9 %collective-permute-start = (bf16[45,128,128]{2,1,0:T(8,128)(2,1)}, bf16[45,128,128]{2,1,0:T(8,128)(2,1)S(1)}, u32[]{:S(2)}, u32[]{:S(2)}) collective-permute-start(bf16[45,128,128]{2,1,0:T(8,128)(2,1)} %get-tuple-element.19.raw_ref), channel_id=1, source_target_pairs={{8,0},{16,8},{24,16},{32,24},{40,32},{48,40},{56,48},{64,56},{72,6... | collective-permute-start | bytes 4423688 | tf_op jit(solution)/shard_map/ppermute | solution.py:21
  15.4 16.5 %collective-permute-start.1 = (f32[24,128]{1,0:T(8,128)S(1)}, f32[24,128]{1,0:T(8,128)S(1)}, u32[]{:S(2)}, u32[]{:S(2)}) collective-permute-start(f32[24,128]{1,0:T(8,128)S(1)} %reduce_sum.9.summed_ref.here_ref), channel_id=1, source_target_pairs={{8,0},{16,8},{24,16},{32,24},{40,32},{48,40},{56,48},{64,56},{72,6... | collective-permute-start | bytes 36872 | tf_op jit(solution)/shard_map/ppermute | solution.py:21
  18.4 1.4 copy-start.4
  25.2 51.8 %all-to-all-start.1 = ((bf16[8,720,128]{2,1,0:T(8,128)(2,1)}), bf16[8,720,128]{2,1,0:T(8,128)(2,1)S(1)}, u32[]{:S(2)}, u32[]{:S(2)}) async-start(bf16[8,720,128]{2,1,0:T(8,128)(2,1)} %get-tuple-element.21), calls=%async_computation.1 | async-start | bytes 2949120 | tf_op jit(solution)/shard_map/all_to_all | solution.py:444
  31.9 1.4 copy-start.5
  38.6 33.3 %collective-permute-start.2 = (bf16[1440,128]{1,0:T(8,128)(2,1)}, bf16[1440,128]{1,0:T(8,128)(2,1)S(1)}, u32[]{:S(2)}, u32[]{:S(2)}) collective-permute-start(bf16[1440,128]{1,0:T(8,128)(2,1)} %get-tuple-element.24), channel_id=1, source_target_pairs={{7,0},{0,1},{1,2},{2,3},{3,4},{4,5},{5,6},{6,7},{15,8},{8,9},{9,10... | collective-permute-start | bytes 1105928 | tf_op jit(solution)/shard_map/ppermute | solution.py:21
  40.0 32.0 %collective-permute-start.3 = (bf16[1440,128]{1,0:T(8,128)(2,1)}, bf16[1440,128]{1,0:T(8,128)(2,1)S(1)}, u32[]{:S(2)}, u32[]{:S(2)}) collective-permute-start(bf16[1440,128]{1,0:T(8,128)(2,1)} %get-tuple-element.25), channel_id=1, source_target_pairs={{6,0},{7,1},{0,2},{1,3},{2,4},{3,5},{4,6},{5,7},{14,8},{15,9},{8,1... | collective-permute-start | bytes 1105928 | tf_op jit(solution)/shard_map/ppermute | solution.py:21
  46.2 32.0 %collective-permute-start.4 = (bf16[1440,128]{1,0:T(8,128)(2,1)}, bf16[1440,128]{1,0:T(8,128)(2,1)S(1)}, u32[]{:S(2)}, u32[]{:S(2)}) collective-permute-start(bf16[1440,128]{1,0:T(8,128)(2,1)} %get-tuple-element.26), channel_id=1, source_target_pairs={{5,0},{6,1},{7,2},{0,3},{1,4},{2,5},{3,6},{4,7},{13,8},{14,9},{15,... | collective-permute-start | bytes 1105928 | tf_op jit(solution)/shard_map/ppermute | solution.py:21
  48.5 34.0 %collective-permute-start.5 = (bf16[1440,128]{1,0:T(8,128)(2,1)}, bf16[1440,128]{1,0:T(8,128)(2,1)}, u32[]{:S(2)}, u32[]{:S(2)}) collective-permute-start(bf16[1440,128]{1,0:T(8,128)(2,1)} %get-tuple-element.27), channel_id=1, source_target_pairs={{4,0},{5,1},{6,2},{7,3},{0,4},{1,5},{2,6},{3,7},{12,8},{13,9},{14,... | collective-permute-start | bytes 1105928 | tf_op jit(solution)/shard_map/ppermute | solution.py:21
  48.8 36.6 %collective-permute-start.6 = (bf16[1440,128]{1,0:T(8,128)(2,1)}, bf16[1440,128]{1,0:T(8,128)(2,1)}, u32[]{:S(2)}, u32[]{:S(2)}) collective-permute-start(bf16[1440,128]{1,0:T(8,128)(2,1)} %get-tuple-element.28), channel_id=1, source_target_pairs={{3,0},{4,1},{5,2},{6,3},{7,4},{0,5},{1,6},{2,7},{11,8},{12,9},{13,... | collective-permute-start | bytes 1105928 | tf_op jit(solution)/shard_map/ppermute | solution.py:21
  71.9 13.5 %collective-permute-start.7 = (bf16[1440,128]{1,0:T(8,128)(2,1)}, bf16[1440,128]{1,0:T(8,128)(2,1)}, u32[]{:S(2)}, u32[]{:S(2)}) collective-permute-start(bf16[1440,128]{1,0:T(8,128)(2,1)} %get-tuple-element.29), channel_id=1, source_target_pairs={{2,0},{3,1},{4,2},{5,3},{6,4},{7,5},{0,6},{1,7},{10,8},{11,9},{12,... | collective-permute-start | bytes 1105928 | tf_op jit(solution)/shard_map/ppermute | solution.py:21
  72.0 15.9 %collective-permute-start.8 = (bf16[1440,128]{1,0:T(8,128)(2,1)}, bf16[1440,128]{1,0:T(8,128)(2,1)}, u32[]{:S(2)}, u32[]{:S(2)}) collective-permute-start(bf16[1440,128]{1,0:T(8,128)(2,1)} %get-tuple-element.30), channel_id=1, source_target_pairs={{1,0},{2,1},{3,2},{4,3},{5,4},{6,5},{7,6},{0,7},{9,8},{10,9},{11,1... | collective-permute-start | bytes 1105928 | tf_op jit(solution)/shard_map/ppermute | solution.py:21
  77.0 1.3 copy-start.1
  91.4 6.9 %collective-permute-start.9 = (f32[40,128]{1,0:T(8,128)S(1)}, f32[40,128]{1,0:T(8,128)S(1)}, u32[]{:S(2)}, u32[]{:S(2)}) collective-permute-start(f32[40,128]{1,0:T(8,128)S(1)} %next_part.1), channel_id=1, source_target_pairs={{248,0},{0,8},{8,16},{16,24},{24,32},{32,40},{40,48},{48,56},{56,6... | collective-permute-start | bytes 61448 | tf_op jit(solution)/shard_map/ppermute | solution.py:21
  96.9 4.5 %collective-permute-start.11 = (f32[8,128]{1,0:T(8,128)S(1)}, f32[8,128]{1,0:T(8,128)S(1)}, u32[]{:S(2)}, u32[]{:S(2)}) collective-permute-start(f32[8,128]{1,0:T(8,128)S(1)} %slice.40), channel_id=1, source_target_pairs={{8,0},{16,8},{24,16},{32,24},{40,32},{48,40},{56,48},{64,56},{72,6... | collective-permute-start | bytes 12296 | tf_op jit(solution)/shard_map/ppermute | solution.py:21
  96.9 6.2 %collective-permute-start.10 = (f32[8,128]{1,0:T(8,128)S(1)}, f32[8,128]{1,0:T(8,128)S(1)}, u32[]{:S(2)}, u32[]{:S(2)}) collective-permute-start(f32[8,128]{1,0:T(8,128)S(1)} %slice.40), channel_id=1, source_target_pairs={{240,0},{248,8},{0,16},{8,24},{16,32},{24,40},{32,48},{40,56},{48,... | collective-permute-start | bytes 12296 | tf_op jit(solution)/shard_map/ppermute | solution.py:21
  114.0 0.6 copy-start.2
